TPU v7x, 32 devices: a whole 2x2x4 slice. The times are simulated.
32 devices in a mesh: dp: 8 (over z, x), fsdp: 4 (over y, core).
Axes of the slice: x: 2, y: 2, z: 4, core: 2. Of those that a mesh axis runs over, the one named last changes fastest.
Arguments:
- tokens: bfloat16 [5120, 768], P(('dp', 'fsdp')), may hold values from -6 to 6
- image_tokens: bfloat16 [128, 256, 768], P(('dp', 'fsdp')), may hold values from -6 to 6
- caption_lengths: int32 [32, 4], P(('dp', 'fsdp')), may hold values from 1 to 64, 160 in all within a row
- arrival_order: int32 [32, 160], P(('dp', 'fsdp')), may hold values from 0 to 159, each once within a row
- w_qkv: bfloat16 [1769472], P(('dp', 'fsdp')), may hold values from -0.21875 to 0.21875
- w_out: bfloat16 [589824], P(('dp', 'fsdp')), may hold values from -0.4375 to 0.4375
- w_cross_q: bfloat16 [589824], P(('dp', 'fsdp')), may hold values from -0.21875 to 0.21875
- w_cross_kv: bfloat16 [1179648], P(('dp', 'fsdp')), may hold values from -0.21875 to 0.21875
- w_cross_out: bfloat16 [589824], P(('dp', 'fsdp')), may hold values from -0.875 to 0.875
- w_up: bfloat16 [2359296], P(('dp', 'fsdp')), may hold values from -0.21875 to 0.21875
- w_down: bfloat16 [2359296], P(('dp', 'fsdp')), may hold values from -0.109375 to 0.109375
- small_params: bfloat16 [8448], P(('dp', 'fsdp')), may hold values from -0.5 to 1.5
- cotangent: bfloat16 [5120, 768], P(('dp', 'fsdp')), may hold values from -6 to 6
Outputs:
- layer_out: bfloat16 [5120, 768], P(('dp', 'fsdp'))
- grad_tokens: bfloat16 [5120, 768], P(('dp', 'fsdp'))
- grad_image: bfloat16 [128, 256, 768], P(('dp', 'fsdp'))
- grad_qkv: float32 [1769472], P(('dp', 'fsdp'))
- grad_out: float32 [589824], P(('dp', 'fsdp'))
- grad_cross_q: float32 [589824], P(('dp', 'fsdp'))
- grad_cross_kv: float32 [1179648], P(('dp', 'fsdp'))
- grad_cross_out: float32 [589824], P(('dp', 'fsdp'))
- grad_up: float32 [2359296], P(('dp', 'fsdp'))
- grad_down: float32 [2359296], P(('dp', 'fsdp'))
- grad_small: float32 [8448], P(('dp', 'fsdp'))
All inputs are finite; a program needn't handle non-finite values.
Results may differ from a plain program's by a relative error of at most 0.018.
Values may be sent and summed in bfloat16 or wider, within the bound.
No kernel may reach another device: no remote copies, remote signals or barrier semaphores. Data moves between devices by JAX's collectives and lax.ppermute only.
A program may use at most 128 MiB of HBM per device.

v0:
```python
import functools

import jax
import jax.numpy as jnp
from jax import lax
from jax.experimental import pallas as pl
from jax.experimental.pallas import tpu as pltpu
from jax.sharding import Mesh
from jax.sharding import PartitionSpec as P

D = 768
HEAD_DIM = 64
FF = 3072
V = 768
IMG = 256
CAP_LEN = 64
LANES = 128
PAIRS = D // LANES
HALF = D // 2
HEADS = 4
WIDE = HEADS * HEAD_DIM
BATCHES = D // WIDE
FOLD = FF // D
GROUP = FOLD * LANES
GROUPS = FF // GROUP
TOKENS_AT = 32
SCALE = HEAD_DIM ** (-0.5)
epsilon = 1e-05
masked_fill = 1e30

BF = jnp.bfloat16
F32 = jnp.float32
AXES = ("z", "x", "y", "c")


def mm(a, b):
    return lax.dot_general(a, b, (((1,), (0,)), ((), ())), preferred_element_type=F32)


def mm_t(a, b):
    return lax.dot_general(a, b, (((1,), (1,)), ((), ())), preferred_element_type=F32)


def t_mm(a, b):
    return lax.dot_general(a, b, (((0,), (0,)), ((), ())), preferred_element_type=F32)


def wide(value):
    return value.astype(F32)


def norm_rows(inputs, gain_vec, shift_vec):
    centred = inputs - jnp.mean(inputs, axis=-1, keepdims=True)
    variance = jnp.mean(centred * centred, axis=-1, keepdims=True)
    return centred * lax.rsqrt(variance + epsilon) * gain_vec + shift_vec


def norm_back(inputs, gain_vec, grad_normed):
    centred = inputs - jnp.mean(inputs, axis=-1, keepdims=True)
    variance = jnp.mean(centred * centred, axis=-1, keepdims=True)
    scale = lax.rsqrt(variance + epsilon)
    unit = centred * scale
    weighted = grad_normed * gain_vec
    grad_in = scale * (
        weighted
        - jnp.mean(weighted, axis=-1, keepdims=True)
        - unit * jnp.mean(weighted * unit, axis=-1, keepdims=True)
    )
    grad_gain = jnp.sum(grad_normed * unit, axis=0, keepdims=True)
    grad_shift = jnp.sum(grad_normed, axis=0, keepdims=True)
    return grad_in, grad_gain, grad_shift


def arrival_pick(arr_ref):
    rows = arr_ref.shape[1]
    place = lax.broadcasted_iota(jnp.int32, (rows, rows), 0)
    return jnp.where(place == arr_ref[...], 1.0, 0.0).astype(BF)


def caption_of(index, lens_ref):
    end = jnp.int32(0)
    found = jnp.zeros_like(index)
    for c in range(lens_ref.shape[1] - 1):
        end = end + lens_ref[0, c]
        found = found + jnp.where(index >= end, 1, 0)
    return found


def slot_pick(lens_ref, rows):
    captions = lens_ref.shape[1]
    shape = (captions * CAP_LEN, rows)
    slot = lax.broadcasted_iota(jnp.int32, shape, 0)
    row = lax.broadcasted_iota(jnp.int32, shape, 1)
    start = jnp.int32(0)
    hit = jnp.zeros(shape, F32)
    for c in range(captions):
        length = lens_ref[0, c]
        inside = slot - c * CAP_LEN
        ok = (inside >= 0) & (inside < length) & (row - start == inside)
        hit = hit + jnp.where(ok, 1.0, 0.0)
        start = start + length
    return hit.astype(BF)


def fold_pick(back):
    source = lax.broadcasted_iota(jnp.int32, (GROUP, GROUP), 1 if back else 0)
    target = lax.broadcasted_iota(jnp.int32, (GROUP, GROUP), 0 if back else 1)
    return jnp.where(target == (source % FOLD) * LANES + source // FOLD, 1.0, 0.0).astype(BF)


def head_mask(rows):
    shape = (HEADS * rows, WIDE)
    head = lax.broadcasted_iota(jnp.int32, shape, 1) // HEAD_DIM
    row = lax.broadcasted_iota(jnp.int32, shape, 0)
    inside = (row >= head * rows) & (row < (head + 1) * rows)
    return jnp.where(inside, 1.0, 0.0).astype(BF)


def stack_heads(block, mask):
    return jnp.concatenate([block] * HEADS, axis=0) * mask


def merge_heads(stacked):
    rows = stacked.shape[0] // HEADS
    head = lax.broadcasted_iota(jnp.int32, (rows, WIDE), 1) // HEAD_DIM
    out = stacked[:rows]
    for n in range(1, HEADS):
        out = jnp.where(head == n, stacked[n * rows : (n + 1) * rows], out)
    return out


def softmax_rows(scores):
    shifted = jnp.exp(scores - jnp.max(scores, axis=-1, keepdims=True))
    return shifted * (1.0 / jnp.sum(shifted, axis=-1, keepdims=True))


def lanes_at(start, width):
    return pl.ds(pl.multiple_of(start, LANES), width)


def pack_halves(shards, out, rows, at=0):
    depth, _, height, _ = out.shape
    pieces = HALF // LANES
    for shard, mats in shards:
        rows[: shard.shape[0], :] = wide(shard[...])
        for mat in range(mats):
            for half in range(2):
                for i in range(pieces):
                    index = mat * PAIRS + half * pieces + i
                    value = rows[pl.ds(index, height, stride=mats * PAIRS), :].astype(BF)
                    lanes = slice(at + i * LANES, at + (i + 1) * LANES)
                    for z in range(depth):
                        out[z, half, :, lanes] = value
            at += HALF
    return at


def pack_self_kernel(w_qkv, w_out, attend, rows):
    pack_halves(((w_qkv, 3), (w_out, 1)), attend, rows)


def pack_cross_kernel(w_cross_q, w_cross_kv, w_cross_out, small, attend, rows):
    at = pack_halves(((w_cross_q, 1), (w_cross_kv, 2), (w_cross_out, 1)), attend, rows)
    depth, _, height, _ = attend.shape
    flat = wide(small[...])
    tail = jnp.zeros((1, LANES - small.shape[1] % LANES), F32)
    flat = jnp.concatenate([flat, tail], axis=1)
    parts = [flat[:, n : n + LANES] for n in range(0, flat.shape[1], LANES)]
    block = jnp.concatenate(parts + [jnp.zeros((height - len(parts), LANES), F32)], axis=0)
    for z in range(depth):
        for half in range(2):
            attend[z, half, :, at:] = block.astype(BF)


def pack_group_kernel(me, w_up, w_down, tokens, cotangent, near, core, chip, rows, parts):
    chunks = FF // LANES
    height = w_up.shape[0] // chunks

    def chunk(index):
        return rows[pl.ds(index, height, stride=chunks), :].astype(BF)

    rows[...] = wide(w_up[...])
    pick = fold_pick(False)
    for t in range(GROUPS):
        group = jnp.concatenate([chunk(t * FOLD + k) for k in range(FOLD)], axis=1)
        folded = mm(group, pick).astype(BF)
        for j in range(FOLD):
            parts[j, :height, t * LANES : (t + 1) * LANES] = folded[
                :, j * LANES : (j + 1) * LANES
            ]
    rows[...] = wide(w_down[...])
    for j in range(FOLD):
        for i in range(PAIRS):
            at = D + i * LANES
            parts[j, :height, at : at + LANES] = chunk(j * PAIRS + i)
        parts[j, TOKENS_AT : TOKENS_AT + tokens.shape[1], :D] = tokens[j]
        parts[j, TOKENS_AT : TOKENS_AT + tokens.shape[1], D:] = cotangent[j]
    near[...] = parts[part_of(me, 0, 0)]
    core[...] = parts[part_of(me, 0, 1)]
    for c in range(2):
        chip[c] = parts[part_of(me, 1, c)]


def transpose_kernel(img, out):
    for n in range(0, img.shape[0], IMG):
        out[:, n : n + IMG] = img[n : n + IMG, :].T


def part_of(me, far_y, far_c):
    return lax.bitwise_xor(me[0, 2], far_y) * 2 + lax.bitwise_xor(me[0, 3], far_c)


def spread_kernel(me, arr, near, chip, core, both, hidden, slotted, grad_slot, arrived):
    height, count = hidden.shape[2], arrived.shape[0] // FOLD
    for value, far_y, far_c in (
        (near[...], 0, 0), (chip[0], 1, 0), (core[...], 0, 1), (both[...], 1, 1),
    ):
        index = part_of(me, far_y, far_c)
        for z in range(hidden.shape[0]):
            hidden[z, index] = value[:height]
        at = pl.multiple_of(index * count, 8)
        arrived[pl.ds(at, count), :] = wide(value[TOKENS_AT : TOKENS_AT + count])
    pick = arrival_pick(arr)
    slotted[...] = mm(pick, arrived[:, :D].astype(BF)).astype(BF)
    grad_slot[...] = mm(pick, arrived[:, D:].astype(BF)).astype(BF)


def fill_table(share, me, pieces, flat, table):
    depth, height = pieces.shape[1], pieces.shape[2] // 2
    lane = lax.broadcasted_iota(jnp.int32, (3, LANES), 1)
    flat[...] = jnp.zeros_like(flat)
    for owner in range(8 * depth):
        z, x, y, c = owner // 8, owner // 4 % 2, owner // 2 % 2, owner % 2
        index = lax.bitwise_xor(me[0, 1], x) * 2 + lax.bitwise_xor(me[0, 2], y)
        value = wide(pieces[index, z])[c * height : c * height + 3, :]
        row, shift = divmod(owner * share, LANES)
        if shift == 0:
            flat[row : row + 3, :] += value
        else:
            moved = pltpu.roll(value, shift, axis=1)
            flat[row : row + 3, :] += jnp.where(lane >= shift, moved, 0.0)
            flat[row + 1 : row + 4, :] += jnp.where(lane < shift, moved, 0.0)
    for n in range(table.shape[0] * PAIRS):
        row, lanes = n // PAIRS, slice(n % PAIRS * LANES, (n % PAIRS + 1) * LANES)
        table[row : row + 1, lanes] = flat[n : n + 1, :]


def depth_sum_kernel(me, got, near, core, chip, total):
    height = near.shape[0]
    value = wide(got[0])
    for z in range(1, got.shape[0]):
        value = value + wide(got[z])
    total[...] = value

    def part(far_y, far_c):
        at = pl.multiple_of(part_of(me, far_y, far_c) * height, 8)
        return total[pl.ds(at, height), :].astype(BF)

    near[...] = part(0, 0)
    core[...] = part(0, 1)
    for c in range(2):
        chip[c] = part(1, c)


def unpack_hidden_kernel(me, near, chip, core, both, up, down, got):
    for value, far_y, far_c in (
        (near[...], 0, 0), (chip[0], 1, 0), (core[...], 0, 1), (both[...], 1, 1),
    ):
        got[part_of(me, far_y, far_c)] = value
    height = got.shape[1]
    chunks = FF // LANES
    pick = fold_pick(True)
    for t in range(GROUPS):
        group = jnp.concatenate(
            [got[j, :, t * LANES : (t + 1) * LANES] for j in range(FOLD)], axis=1
        )
        natural = mm(group, pick)
        for k in range(FOLD):
            up[pl.ds(t * FOLD + k, height, stride=chunks), :] = natural[
                :, k * LANES : (k + 1) * LANES
            ]
    for j in range(FOLD):
        for i in range(PAIRS):
            at = D + i * LANES
            down[pl.ds(j * PAIRS + i, height, stride=chunks), :] = wide(
                got[j, :, at : at + LANES]
            )


def unpack_halves(got, outs):
    depth, height = got.shape[0], got.shape[2]
    parts = HALF // LANES
    place = 0
    for out in outs:
        chunks = out.shape[0] // height
        for mat in range(chunks // PAIRS):
            for half in range(2):
                for i in range(parts):
                    at = place + i * LANES
                    total = wide(got[0, half, :, at : at + LANES])
                    for z in range(1, depth):
                        total = total + wide(got[z, half, :, at : at + LANES])
                    index = mat * PAIRS + half * parts + i
                    out[pl.ds(index, height, stride=chunks), :] = total
            place += HALF
    return place


class Fetch:
    def __init__(self, sems):
        self.sems = sems
        self.used = 0

    def start(self, source, target):
        copy = pltpu.make_async_copy(source, target, self.sems.at[self.used])
        self.used += 1
        copy.start()
        return copy

    def columns(self, pieces, me, piece_at, target, target_at):
        copies = []
        for index, piece in enumerate(pieces):
            half = lax.bitwise_xor(me[0, 3], index // 4)
            x = lax.bitwise_xor(me[0, 1], index // 2 % 2)
            y = lax.bitwise_xor(me[0, 2], index % 2)
            copies.append(
                self.start(
                    piece.at[:, :, pl.ds(piece_at, HALF)],
                    target.at[:, x, y, :, lanes_at(target_at + half * HALF, HALF)],
                )
            )
        return copies


def wait(copies):
    for copy in copies:
        copy.wait()


def matrix(ref):
    shape = ref.shape
    return ref[...].reshape(shape[0] * shape[1] * shape[2] * shape[3], shape[4])


def forward_kernel(share, lens, me, slotted, img, *refs):
    pieces_a, pieces_b = refs[:8], refs[8:16]
    (
        table,
        projected, probs_self, saved, after_self, after_cross, normed_mlp, query_slots,
        kv_out, probs_out, kv, probs_cross, w_qkv, w_out, w_cq, w_kv, w_co, mixed_slots, small, flat, sems,
    ) = refs[16:]
    fetch = Fetch(sems)
    got_small = [
        fetch.start(pieces_b[n].at[:, :, pl.ds(4 * HALF, LANES)], small.at[n]) for n in range(4)
    ]
    got_qkv = []
    for mat in range(3):
        got_qkv += fetch.columns(pieces_a, me, mat * HALF, w_qkv, mat * D)
    got_out = fetch.columns(pieces_a, me, 3 * HALF, w_out, 0)
    got_cq = fetch.columns(pieces_b, me, 0, w_cq, 0)
    got_kv = fetch.columns(pieces_b, me, HALF, w_kv, 0)
    got_kv += fetch.columns(pieces_b, me, 2 * HALF, w_kv, D)
    got_co = fetch.columns(pieces_b, me, 3 * HALF, w_co, 0)
    rows = slotted.shape[0]
    wait(got_small)
    fill_table(share, me, small, flat, table)
    saved[:, :D] = norm_rows(wide(slotted[...]), table[0:1, :], table[3:4, :]).astype(BF)
    wait(got_qkv)
    projected[...] = mm(saved[:, :D], matrix(w_qkv)).astype(BF)
    query_at = lax.broadcasted_iota(jnp.int32, (rows, rows), 0)
    key_at = lax.broadcasted_iota(jnp.int32, (rows, rows), 1)
    same = caption_of(query_at, lens) == caption_of(key_at, lens)
    block = jnp.where(same & (key_at <= query_at), 0.0, -masked_fill)
    barred = jnp.concatenate([block] * HEADS, axis=0)
    mask = head_mask(rows)
    for n in range(BATCHES):
        query, key, value = (
            projected[:, m * D + n * WIDE : m * D + (n + 1) * WIDE] for m in range(3)
        )
        scores = mm_t(stack_heads(query, mask), key) * SCALE + barred
        weights_low = softmax_rows(scores).astype(BF)
        probs_self[n] = weights_low
        saved[:, D + n * WIDE : D + (n + 1) * WIDE] = merge_heads(
            mm(weights_low, value)
        ).astype(BF)
    wait(got_out)
    state = wide(slotted[...]) + mm(saved[:, D : 2 * D], matrix(w_out))
    after_self[...] = state
    low = norm_rows(state, table[1:2, :], table[4:5, :]).astype(BF)
    saved[:, 2 * D : 3 * D] = low
    wait(got_cq)
    pick = slot_pick(lens, rows)
    query_slots[...] = mm(pick, mm(low, matrix(w_cq)).astype(BF)).astype(BF)
    wait(got_kv)
    kv_mat = matrix(w_kv)
    mask = head_mask(CAP_LEN)
    sent = []
    for c in range(lens.shape[1]):
        slots = slice(c * CAP_LEN, (c + 1) * CAP_LEN)
        images = slice(c * IMG, (c + 1) * IMG)
        kv[images, :] = mm(img[images, :], kv_mat).astype(BF)
        for n in range(BATCHES):
            cols = slice(n * WIDE, (n + 1) * WIDE)
            query = stack_heads(query_slots[slots, cols], mask)
            weights_low = softmax_rows(mm_t(query, kv[images, cols]) * SCALE).astype(BF)
            probs_cross[c * BATCHES + n] = weights_low
            value = kv[images, D + n * WIDE : D + (n + 1) * WIDE]
            mixed_slots[slots, cols] = merge_heads(mm(weights_low, value)).astype(BF)
        batch = slice(c * BATCHES, (c + 1) * BATCHES)
        sent.append(fetch.start(kv.at[images], kv_out.at[images]))
        sent.append(fetch.start(probs_cross.at[batch], probs_out.at[batch]))
    low = t_mm(pick, mixed_slots[...]).astype(BF)
    saved[:, 3 * D :] = low
    wait(got_co)
    state = after_self[...] + mm(low, matrix(w_co))
    after_cross[...] = state
    normed_mlp[...] = norm_rows(state, table[2:3, :], table[5:6, :]).astype(BF)
    wait(sent)


def put_small(small, row, value):
    for k in range(PAIRS):
        at = row * PAIRS + k
        small[at : at + 1, :] = value[:, k * LANES : (k + 1) * LANES]


def own_part(value, me):
    part = me[0, 2] * 2 + me[0, 3]
    out = value[:, :LANES]
    for j in range(1, FOLD):
        out = jnp.where(part == j, value[:, j * LANES : (j + 1) * LANES], out)
    return out


def mlp_kernel(me, table, *refs):
    inputs, grads, pieces = refs[:4], refs[4:8], refs[8:10]
    (
        grad_near, grad_keep, grad_send, grad_send_y, out_near, out_keep, out_send, out_send_y,
        active, grad_hidden, small, all_in, all_grad, w_up, w_down, grad_part, out_part, sems,
    ) = refs[10:]
    fetch = Fetch(sems)
    got_up, got_down = [], []
    for index in range(2):
        x = lax.bitwise_xor(me[0, 1], index)
        got_up.append(fetch.start(pieces[index].at[:, :, pl.ds(0, D)], w_up.at[:, x]))
        got_down.append(fetch.start(pieces[index].at[:, :, pl.ds(D, D)], w_down.at[:, x]))
    rows = inputs[0].shape[0]
    for n in range(4):
        all_in[n * rows : (n + 1) * rows, :] = inputs[n][...]
        all_grad[n * rows : (n + 1) * rows, :] = grads[n][...]
    bias = [
        table[6 + n // PAIRS : 7 + n // PAIRS, n % PAIRS * LANES : (n % PAIRS + 1) * LANES]
        for n in range(FF // LANES)
    ]
    bias = jnp.concatenate(
        [jnp.concatenate(bias[t * FOLD : (t + 1) * FOLD], axis=1) for t in range(GROUPS)], axis=0
    )
    bias = own_part(mm(bias.astype(BF), fold_pick(False)), me)
    bias = jnp.concatenate([bias[t : t + 1, :] for t in range(GROUPS)], axis=1)
    wait(got_up)
    up_mat = w_up[...].reshape(D, D)
    wait(got_down)
    down_mat = w_down[...].reshape(D, D)

    def rows_of(n, total):
        at = pl.ds(pl.multiple_of(n * 2 * rows, 64), 2 * rows)
        hidden = mm(all_in[at, :], up_mat) + bias
        half = 0.5 + 0.5 * lax.erf(hidden * (0.5**0.5))
        act = (hidden * half).astype(BF)
        active[at, :] = act
        slope = half + hidden * (jnp.exp(hidden * hidden * -0.5) * 0.3989422804014327)
        grad_hid = (mm_t(all_grad[at, :], down_mat) * slope).astype(BF)
        grad_hidden[at, :] = grad_hid
        grad_part[n] = mm_t(grad_hid, up_mat)
        out_part[n] = mm(act, down_mat)
        return total + jnp.sum(wide(grad_hid), axis=0, keepdims=True)

    sums = lax.fori_loop(0, 2, rows_of, jnp.zeros((1, D), F32)).astype(BF)
    for part, outs in (
        (grad_part, (grad_near, grad_send, grad_keep, grad_send_y)),
        (out_part, (out_near, out_send, out_keep, out_send_y)),
    ):
        for n, out in enumerate(outs):
            out[...] = part[n // 2, n % 2 * rows : (n % 2 + 1) * rows].astype(out.dtype)
    sums = jnp.concatenate(
        [sums[:, t * LANES : (t + 1) * LANES] for t in range(GROUPS)] + [sums[:, :LANES]] * 2,
        axis=0,
    )
    part = me[0, 2] * 2 + me[0, 3]
    spread = jnp.concatenate(
        [jnp.where(part == j, sums, jnp.zeros_like(sums)) for j in range(FOLD)], axis=1
    )
    natural = mm(spread, fold_pick(True))
    small[...] = jnp.zeros_like(small)
    for n in range(FF // LANES):
        at = 6 * PAIRS + n
        small[at : at + 1, :] = natural[
            n // FOLD : n // FOLD + 1, n % FOLD * LANES : (n % FOLD + 1) * LANES
        ]
    put_small(small, 10, jnp.sum(wide(grads[0][...]), axis=0, keepdims=True))


def hidden_grad_kernel(*refs):
    normed, grad_slot = refs[:4], refs[4:8]
    active, grad_hidden, out = refs[8:]
    rows = lambda parts: jnp.concatenate([r[...] for r in parts], axis=0)
    out[:, :D] = t_mm(rows(normed), grad_hidden[...]).astype(BF)
    out[:, D:] = t_mm(active[...], rows(grad_slot)).astype(BF)


def combine_kernel(keep, far, out):
    out[...] = (wide(keep[...]) + wide(far[...])).astype(BF)


def cross_back_kernel(
    lens, me, grad_near, grad_core, grad_far, after_cross, grad_slot, probs_in, query_slots, kv_in,
    after_self, table, small_in, *refs,
):
    pieces = refs[:8]
    (
        grad_state, small, half_keep, half_send, keep_out, send_out,
        w_co, w_cq, mixed_slots, query_grads, grad_kv, kv_keep, kv_send, kv, probs, sems,
    ) = refs[8:]
    fetch = Fetch(sems)
    got_co = fetch.columns(pieces, me, 3 * HALF, w_co, 0)
    got_kv = [fetch.start(kv_in, kv), fetch.start(probs_in, probs)]
    got_cq = fetch.columns(pieces, me, 0, w_cq, 0)
    rows = after_self.shape[0]
    sent = []
    halves = ((0, half_keep, kv_keep), (1, half_send, kv_send))
    small[...] = small_in[...]
    grad_in, grad_gain, grad_shift = norm_back(
        after_cross[...],
        table[2:3, :],
        grad_near[...] + wide(grad_core[...]) + wide(grad_far[...]),
    )
    put_small(small, 2, grad_gain)
    put_small(small, 5, grad_shift)
    grad_after = wide(grad_slot[...]) + grad_in
    grad_state[...] = grad_after
    pick = slot_pick(lens, rows)
    wait(got_co)
    query_grads[:rows, :] = grad_after.astype(BF)
    mixed_slots[...] = mm(pick, mm_t(query_grads[:rows, :], matrix(w_co)).astype(BF)).astype(BF)
    for rel, half_out, _ in halves:
        at = lax.bitwise_xor(me[0, 3], rel) * HALF
        half_out[:, HALF : 2 * HALF] = query_grads[:rows, lanes_at(at, HALF)]
    mask = head_mask(CAP_LEN)
    wait(got_kv)
    for c in range(lens.shape[1]):
        slots = slice(c * CAP_LEN, (c + 1) * CAP_LEN)
        images = slice(c * IMG, (c + 1) * IMG)
        for n in range(BATCHES):
            cols = slice(n * WIDE, (n + 1) * WIDE)
            value_cols = slice(D + n * WIDE, D + (n + 1) * WIDE)
            grad_mixed = stack_heads(mixed_slots[slots, cols], mask)
            query = stack_heads(query_slots[slots, cols], mask)
            weights_low = probs[c * BATCHES + n]
            attn = wide(weights_low)
            grad_weights = mm_t(grad_mixed, kv[images, value_cols])
            centre = jnp.sum(attn * grad_weights, axis=-1, keepdims=True)
            grad_scores = (attn * (grad_weights - centre)).astype(BF)
            query_grads[slots, cols] = (
                merge_heads(mm(grad_scores, kv[images, cols])) * SCALE
            ).astype(BF)
            grad_kv[images, cols] = (t_mm(grad_scores, query) * SCALE).astype(BF)
            grad_kv[images, value_cols] = t_mm(weights_low, grad_mixed).astype(BF)
        for rel, _, kv_half in halves:
            at = lax.bitwise_xor(me[0, 3], rel) * HALF
            kv_half[images, :HALF] = grad_kv[images, lanes_at(at, HALF)]
            kv_half[images, HALF:] = grad_kv[images, lanes_at(at + D, HALF)]
        sent.append(fetch.start(kv_send.at[images], send_out.at[images]))
        sent.append(fetch.start(kv_keep.at[images], keep_out.at[images]))
    mixed_slots[:rows, :] = t_mm(pick, query_grads[...]).astype(BF)
    wait(got_cq)
    grad_in, grad_gain, grad_shift = norm_back(
        after_self[...], table[1:2, :], mm_t(mixed_slots[:rows, :], matrix(w_cq))
    )
    put_small(small, 1, grad_gain)
    put_small(small, 4, grad_shift)
    grad_after = grad_state[...] + grad_in
    grad_state[...] = grad_after
    query_grads[:rows, :] = grad_after.astype(BF)
    for rel, half_out, _ in halves:
        at = lax.bitwise_xor(me[0, 3], rel) * HALF
        half_out[:, :HALF] = mixed_slots[:rows, lanes_at(at, HALF)]
        half_out[:, 2 * HALF :] = query_grads[:rows, lanes_at(at, HALF)]
    wait(sent)


def self_back_kernel(me, grad_state, probs, projected, slotted, table, small_in, *refs):
    pieces = refs[:8]
    (
        grad_rows, small, keep, send,
        w_out, w_qkv, mixed, grad_projected, sems,
    ) = refs[8:]
    fetch = Fetch(sems)
    got_out = fetch.columns(pieces, me, 3 * HALF, w_out, 0)
    got_qkv = []
    for mat in range(3):
        got_qkv += fetch.columns(pieces, me, mat * HALF, w_qkv, mat * D)
    rows = slotted.shape[0]
    wait(got_out)
    mixed[...] = mm_t(grad_state[...].astype(BF), matrix(w_out)).astype(BF)
    mask = head_mask(rows)
    for n in range(BATCHES):
        cols, key_cols, value_cols = (
            slice(m * D + n * WIDE, m * D + (n + 1) * WIDE) for m in range(3)
        )
        grad_mixed = stack_heads(mixed[:, cols], mask)
        query = stack_heads(projected[:, cols], mask)
        weights_low = probs[n]
        attn = wide(weights_low)
        grad_weights = mm_t(grad_mixed, projected[:, value_cols])
        centre = jnp.sum(attn * grad_weights, axis=-1, keepdims=True)
        grad_scores = (attn * (grad_weights - centre)).astype(BF)
        grad_projected[:, cols] = (
            merge_heads(mm(grad_scores, projected[:, key_cols])) * SCALE
        ).astype(BF)
        grad_projected[:, key_cols] = (t_mm(grad_scores, query) * SCALE).astype(BF)
        grad_projected[:, value_cols] = t_mm(weights_low, grad_mixed).astype(BF)
    for mat in range(3):
        for rel, out in ((0, keep), (1, send)):
            at = lax.bitwise_xor(me[0, 3], rel) * HALF + mat * D
            out[:, mat * HALF : (mat + 1) * HALF] = grad_projected[:, lanes_at(at, HALF)]
    wait(got_qkv)
    grad_in, grad_gain, grad_shift = norm_back(
        wide(slotted[...]), table[0:1, :], mm_t(grad_projected[...], matrix(w_qkv))
    )
    grad_slotted = (grad_state[...] + grad_in).astype(BF)
    grad_rows[...] = grad_slotted
    small[...] = small_in[...]
    put_small(small, 0, grad_gain)
    put_small(small, 3, grad_shift)


def put_quadrants(grads, me, outs, at, first):
    depth, height = outs[0].shape[1:3]
    width = grads.shape[1]
    for i, out in enumerate(outs):
        for j in range(2):
            far_x, far_y = (i, j) if first == "x" else (j, i)
            x, y = lax.bitwise_xor(me[0, 1], far_x), lax.bitwise_xor(me[0, 2], far_y)
            for z in range(depth):
                low = pl.multiple_of(((z * 2 + x) * 2 + y) * height, 16)
                out[j, z, :, at : at + width] = grads[pl.ds(low, height), :].astype(BF)


def half_grads(pieces, me, outs, grads, first, at=0):
    for left, far_left, right, far_right in pieces:
        width = right.shape[1]
        grads[:, :width] = t_mm(left, right) + t_mm(far_left, far_right)
        put_quadrants(grads.at[:, :width], me, outs, at, first)
        at += width


def cross_grad_kernel(me, *refs):
    sources, targets, landed, made, grads, sems = (
        refs[:8], refs[8:12], refs[12:20], refs[20:24], refs[24], refs[25],
    )
    fetch = Fetch(sems)
    copies = [fetch.start(source, target) for source, target in zip(sources, landed)]
    saved, saved_far, half, half_far, img_t, img_t_far, kv, kv_far = landed
    part = lambda ref, n, width: ref[:, n * width : (n + 1) * width]
    piece = lambda left, right: (
        part(saved, left, D), part(saved_far, left, D),
        part(half, right, HALF), part(half_far, right, HALF),
    )
    wait(copies[:4])
    half_grads([piece(3, 1), piece(1, 2)], me, made[2:], grads, "y")
    sent = [fetch.start(made[n], targets[n]) for n in (3, 2)]
    half_grads([piece(2, 0)], me, made[:2], grads, "x")
    wait(copies[4:])
    grads[...] = mm(img_t[...], kv[...]) + mm(img_t_far[...], kv_far[...])
    put_quadrants(grads, me, made[:2], HALF, "x")
    sent += [fetch.start(made[n], targets[n]) for n in (1, 0)]
    wait(sent)


def owner_rows(small, blocks, share):
    height = blocks.shape[0] // (small.shape[0] * LANES // share)
    lane = lax.broadcasted_iota(jnp.int32, (3, LANES), 1)
    blocks[...] = jnp.zeros_like(blocks)
    table = jnp.concatenate([small[...], jnp.zeros((6, LANES), F32)], axis=0)
    for owner in range(small.shape[0] * LANES // share):
        row, shift = divmod(owner * share, LANES)
        if shift == 0:
            value = table[row : row + 3]
        else:
            moved = pltpu.roll(table[row : row + 4], LANES - shift, axis=1)
            value = jnp.where(lane < LANES - shift, moved[:3], moved[1:4])
        blocks[owner * height : owner * height + 3, :] = value


def self_grad_kernel(share, me, small, *refs):
    sources, targets, landed, made, grads, sems = (
        refs[:4], refs[4:8], refs[8:12], refs[12:16], refs[16], refs[17],
    )
    fetch = Fetch(sems)
    sources = [sources[0].at[:, pl.ds(0, D)], sources[1].at[:, pl.ds(0, D)], *sources[2:]]
    copies = [fetch.start(source, target) for source, target in zip(sources, landed)]
    own, far, half, half_far = landed
    wait(copies)
    half_grads([(own[...], far[...], half[:, :D], half_far[:, :D])], me, made[:2], grads, "y")
    sent = [fetch.start(made[n], targets[n]) for n in (1, 0)]
    half_grads([(own[...], far[...], half[:, D:], half_far[:, D:])], me, made[2:], grads, "x")
    blocks = grads.at[:, :LANES]
    owner_rows(small, blocks, share)
    put_quadrants(blocks, me, made[2:], HALF, "x")
    sent += [fetch.start(made[n], targets[n]) for n in (3, 2)]
    wait(sent)


def unpack_kernel(got, *outs):
    at = unpack_halves(got, outs[:-1])
    total = jnp.zeros((8, LANES), F32)
    for z in range(got.shape[0]):
        for c in range(2):
            total = total + wide(got[z, c, :8, at:])
    outs[-1][...] = total


def return_kernel(
    me, arr, after_cross, table, out_near, out_core, out_far, grad_rows, near, core, chip, rows
):
    pick = arrival_pick(arr)
    count = near.shape[0]
    result = after_cross[...] + out_near[...] + wide(out_core[...]) + wide(out_far[...])
    result = result + table[10:11, :]
    rows[:, :D] = t_mm(pick, result.astype(BF))
    rows[:, D:] = t_mm(pick, grad_rows[...])

    def part(far_y, far_c):
        at = pl.multiple_of(part_of(me, far_y, far_c) * count, 8)
        return rows[pl.ds(at, count), :].astype(BF)

    near[...] = part(0, 0)
    core[...] = part(0, 1)
    for c in range(2):
        chip[c] = part(1, c)


def collect_kernel(me, near, chip, core, both, layer_out, grad_tokens):
    for value, far_y, far_c in ((near[...], 0, 0), (chip[0], 1, 0), (core[...], 0, 1), (both[...], 1, 1)):
        index = part_of(me, far_y, far_c)
        layer_out[index] = value[:, :D]
        grad_tokens[index] = value[:, D:]


def image_grad_kernel(kv_keep, kv_send, *refs):
    me, pieces = refs[0], refs[1:9]
    grad_image, w_kv, sems = refs[9:]
    fetch = Fetch(sems)
    copies = []
    for index, piece in enumerate(pieces):
        x = lax.bitwise_xor(me[0, 1], index // 2 % 2)
        y = lax.bitwise_xor(me[0, 2], index % 2)
        copies.append(
            fetch.start(piece.at[:, :, pl.ds(HALF, D)], w_kv.at[index // 4, :, x, y])
        )
    wait(copies)
    near, far = w_kv[0].reshape(D, D), w_kv[1].reshape(D, D)
    for c in range(kv_keep.shape[0] // IMG):
        rows = pl.ds(c * IMG, IMG)
        grad_image[rows, :] = (mm_t(kv_keep[rows, :], near) + mm_t(kv_send[rows, :], far)).astype(
            BF
        )


def add_kernel(counts, joined, *refs):
    outs = refs[sum(counts) :]
    first = at = 0
    for n, count in enumerate(counts):
        for z in range(refs[first].shape[0]):
            total = wide(refs[first][z])
            for ref in refs[first + 1 : first + count]:
                total = total + wide(ref[z])
            if joined:
                outs[0][z, :, at : at + total.shape[-1]] = total.astype(BF)
            else:
                outs[n][z] = total.astype(BF)
        at += total.shape[-1]
        first += count


VM = pl.BlockSpec(memory_space=pltpu.VMEM)
SM = pl.BlockSpec(memory_space=pltpu.SMEM)
HB = pl.BlockSpec(memory_space=pl.ANY)


def run(kernel, outs, specs, scratch, *args, mib=58, copied=0):
    return pl.pallas_call(
        kernel,
        out_shape=[jax.ShapeDtypeStruct(s, t) for s, t in outs],
        in_specs=specs,
        out_specs=[VM] * (len(outs) - copied) + [HB] * copied,
        scratch_shapes=scratch,
        compiler_params=pltpu.CompilerParams(vmem_limit_bytes=mib * 2**20),
        name=(kernel.func if isinstance(kernel, functools.partial) else kernel).__name__,
    )(*args)


def add_up(*sums, joined=False):
    args, specs, shapes = [], [], []
    for terms in sums:
        for term in terms:
            array, index = term if isinstance(term, tuple) else (term, None)
            block = array.shape[-3:]
            if index is None:
                specs.append(pl.BlockSpec(block, lambda i: (0, 0, 0)))
            else:
                specs.append(pl.BlockSpec((None,) + block, lambda i, n=index: (n, 0, 0, 0)))
            args.append(array)
        shapes.append(block)
    if joined:
        shapes = [shapes[0][:2] + (sum(s[2] for s in shapes),)]
    return pl.pallas_call(
        functools.partial(add_kernel, [len(terms) for terms in sums], joined),
        grid=(1,),
        out_shape=[jax.ShapeDtypeStruct(s, BF) for s in shapes],
        in_specs=specs,
        out_specs=[pl.BlockSpec(s, lambda i: (0, 0, 0)) for s in shapes],
        compiler_params=pltpu.CompilerParams(vmem_limit_bytes=58 * 2**20),
        name="add_kernel",
    )(*args)


def flip(value, axis):
    return lax.ppermute(value, axis, [(0, 1), (1, 0)])


def swap_all(value, axes):
    return lax.all_to_all(value, axes, split_axis=0, concat_axis=0, tiled=True)


def tie(*values):
    return lax.optimization_barrier(values)


def on_device(
    tokens,
    image_tokens,
    caption_lengths,
    arrival_order,
    w_qkv,
    w_out,
    w_cross_q,
    w_cross_kv,
    w_cross_out,
    w_up,
    w_down,
    small_params,
    cotangent,
):
    depth = lax.axis_size("z")
    height = D // (8 * depth)
    rows = tokens.shape[0]
    captions = caption_lengths.shape[1]
    slots = captions * CAP_LEN
    images = captions * IMG
    lens, arr = caption_lengths, arrival_order
    me = jnp.stack([lax.axis_index(a) for a in AXES]).astype(jnp.int32).reshape(1, 4)
    vmem = pltpu.VMEM
    sems = lambda n: pltpu.SemaphoreType.DMA((n,))
    shards = (w_qkv, w_out, w_cross_q, w_cross_kv, w_cross_out, w_up, w_down)

    share = small_params.shape[0]
    flat_shards = [w.reshape(-1, LANES) for w in shards]
    packed = lambda n: [((depth, 2, height, n), BF)]
    chunked = [vmem((w_up.shape[0] // LANES, LANES), F32)]
    (a,) = run(pack_self_kernel, packed(4 * HALF), [VM] * 2, chunked, *flat_shards[:2])
    (b,) = run(
        pack_cross_kernel, packed(4 * HALF + LANES), [VM] * 4, chunked,
        *flat_shards[2:5], small_params.reshape(1, share),
    )
    part = ((TOKENS_AT + 48, 2 * D), BF)
    near, core, chip = run(
        pack_group_kernel,
        [part, part, ((2,) + part[0], BF)],
        [SM] + [VM] * 4,
        chunked + [vmem((FOLD,) + part[0], BF)],
        me, *flat_shards[5:], tokens.reshape(FOLD, -1, D), cotangent.reshape(FOLD, -1, D),
    )

    def along_z(packed):
        got = swap_all(packed.reshape(2 * depth, height, -1), ("z", "c"))
        return got.reshape(depth, 2 * height, -1)

    a, chip = along_z(a), flip(chip, "y")
    img = image_tokens.reshape(images, V)
    (img_t,) = run(transpose_kernel, [((V, images), BF)], [VM], [], img)
    a, b, chip, core, img_t = tie(a, b, chip, core, img_t)
    b = along_z(b)
    ax, ay = flip(a, "x"), flip(a, "y")
    img_t_far = flip(img_t, "c")
    hidden, slotted, grad_slot = run(
        spread_kernel,
        [((depth, FOLD, height, 2 * D), BF), ((rows, D), BF), ((rows, D), BF)],
        [SM] + [VM] * 5,
        [vmem((rows, 2 * D), F32)],
        me, arr, near, chip, flip(core, "c"), flip(chip[1], "c"),
    )
    a_far = flip(a, "c")
    b, ax, ay, hidden, grad_slot, img_t_far, a_far = tie(
        b, ax, ay, hidden, grad_slot, img_t_far, a_far
    )
    def group_rows(value):
        far = flip(value, "y")
        return (value, flip(value, "c"), far, flip(far, "c"))

    bx, by = flip(b, "x"), flip(b, "y")
    hidden = swap_all(hidden.reshape(depth, FOLD * height, 2 * D), "z")
    b_far, ax_far, ay_far = flip(b, "c"), flip(ax, "c"), flip(ay, "c")
    bx, by, ax, ax_far, ay_far, b_far = tie(bx, by, ax, ax_far, ay_far, b_far)
    axy, byx = flip(ax, "y"), flip(by, "x")
    by_far, bx_far = flip(by, "c"), flip(bx, "c")
    axy, byx, by_far, bx_far, hidden = tie(axy, byx, by_far, bx_far, hidden)
    pieces_a = (a, ay, ax, axy, a_far, ay_far, ax_far, flip(axy, "c"))
    pieces_b = (b, by, bx, byx, b_far, by_far, bx_far, flip(byx, "c"))
    hidden, pieces_a, pieces_b = tie(hidden, pieces_a, pieces_b)
    hidden_far = flip(hidden, "x")
    grad_slots = group_rows(grad_slot)

    weight_shape = lambda n: vmem((depth, 2, 2, 2 * height, n * D), BF)
    (
        table, projected, probs_self, saved, after_self, after_cross, normed_mlp, query_slots, kv,
        probs_cross,
    ) = run(
        functools.partial(forward_kernel, share),
        [
            ((8 * depth * share // D, D), F32),
            ((rows, 3 * D), BF),
            ((BATCHES, HEADS * rows, rows), BF),
            ((rows, 4 * D), BF),
            ((rows, D), F32),
            ((rows, D), F32),
            ((rows, D), BF),
            ((slots, D), BF),
            ((images, 2 * D), BF),
            ((captions * BATCHES, HEADS * CAP_LEN, IMG), BF),
        ],
        [SM, SM] + [VM] * 2 + [HB] * 16,
        [
            vmem((images, 2 * D), BF),
            vmem((captions * BATCHES, HEADS * CAP_LEN, IMG), BF),
            weight_shape(3),
            weight_shape(1),
            weight_shape(1),
            weight_shape(2),
            weight_shape(1),
            vmem((slots, D), BF),
            vmem((4, depth, 2 * height, LANES), BF),
            vmem((72, LANES), F32),
            sems(68 + 2 * captions),
        ],
        lens, me, slotted, img, *pieces_a, *pieces_b,
        copied=2,
    )
    inputs = group_rows(normed_mlp)
    small_shape = ((11 * PAIRS, LANES), F32)
    saved_far = flip(saved, "c")
    (
        grad_near, grad_keep, grad_send, grad_send_y, out_near, out_keep, out_send, out_send_y,
        active, grad_hidden, small,
    ) = run(
        mlp_kernel,
        [
            ((rows, D), F32),
            ((rows, D), BF),
            ((rows, D), BF),
            ((rows, D), BF),
            ((rows, D), F32),
            ((rows, D), BF),
            ((rows, D), BF),
            ((rows, D), BF),
            ((4 * rows, D), BF),
            ((4 * rows, D), BF),
            small_shape,
        ],
        [SM] + [VM] * 9 + [HB] * 2,
        [
            vmem((4 * rows, D), BF),
            vmem((4 * rows, D), BF),
            vmem((depth, 2, FOLD * height, D), BF),
            vmem((depth, 2, FOLD * height, D), BF),
            vmem((2, 2 * rows, D), F32),
            vmem((2, 2 * rows, D), F32),
            sems(4),
        ],
        me, table, *inputs, *grad_slots,
        hidden, hidden_far,
    )

    def owned(value, parts, axes):
        got = swap_all(value.reshape(parts * depth, height, -1), axes)
        return got.reshape(depth, parts, height, -1)

    flat = lambda n: ((height * n * PAIRS, LANES), F32)

    def combined(keep, far):
        return run(combine_kernel, [((rows, D), BF)], [VM] * 2, [], keep, far, mib=16)[0]

    grad_far = flip(combined(grad_keep, flip(grad_send_y, "c")), "y")
    grad_core = flip(grad_send, "c")
    (hidden_grad,) = run(
        hidden_grad_kernel,
        [((D, 2 * D), BF)],
        [VM] * 10,
        [],
        *inputs, *grad_slots, active, grad_hidden,
    )
    grad_far, grad_core, hidden_grad, saved_far, out_send, out_send_y = tie(
        grad_far, grad_core, hidden_grad, saved_far, out_send, out_send_y
    )
    hidden_got = swap_all(hidden_grad.reshape(2 * depth, FOLD * height, 2 * D), ("z", "x"))
    out_core, out_core_y = flip(out_send, "c"), flip(out_send_y, "c")
    grad_state, small, half_keep, half_send, kv_keep, kv_send = run(
        cross_back_kernel,
        [
            ((rows, D), F32),
            small_shape,
            ((rows, 3 * HALF), BF),
            ((rows, 3 * HALF), BF),
            ((images, D), BF),
            ((images, D), BF),
        ],
        [SM, SM] + [VM] * 5 + [HB, VM, HB] + [VM] * 3 + [HB] * 8,
        [
            weight_shape(1),
            weight_shape(1),
            vmem((slots, D), BF),
            vmem((slots, D), BF),
            vmem((images, 2 * D), BF),
            vmem((images, D), BF),
            vmem((images, D), BF),
            vmem((images, 2 * D), BF),
            vmem((captions * BATCHES, HEADS * CAP_LEN, IMG), BF),
            sems(18 + 2 * captions),
        ],
        lens, me, grad_near, grad_core, grad_far, after_cross, grad_slot, probs_cross, query_slots,
        kv, after_self, table, small, *pieces_b,
        copied=2,
    )
    grad_state, half_send, kv_send, out_core_y = tie(grad_state, half_send, kv_send, out_core_y)
    half_far, kv_far = flip(half_send, "c"), flip(kv_send, "c")
    out_far = flip(combined(out_keep, out_core_y), "y")
    grad_rows, small, self_keep, self_send = run(
        self_back_kernel,
        [
            ((rows, D), BF),
            small_shape,
            ((rows, 3 * HALF), BF),
            ((rows, 3 * HALF), BF),
        ],
        [SM] + [VM] * 6 + [HB] * 8,
        [
            weight_shape(1),
            weight_shape(3),
            vmem((rows, D), BF),
            vmem((rows, 3 * D), BF),
            sems(32),
        ],
        me, grad_state, probs_self, projected, slotted, table, small, *pieces_a,
    )
    self_send, grad_rows, half_far, kv_far, out_far = tie(
        self_send, grad_rows, half_far, kv_far, out_far
    )
    self_far = flip(self_send, "c")
    block = lambda n: ((2, depth, 2 * height, n), BF)
    kv_0, kv_1, mix_0, mix_1 = run(
        cross_grad_kernel,
        [block(3 * HALF)] * 2 + [block(2 * HALF)] * 2,
        [SM] + [HB] * 8,
        [vmem((rows, 4 * D), BF)] * 2
        + [vmem((rows, 3 * HALF), BF)] * 2
        + [vmem((V, images), BF)] * 2
        + [vmem((images, D), BF)] * 2
        + [vmem(block(n * HALF)[0], BF) for n in (3, 3, 2, 2)]
        + [vmem((D, D), F32), sems(12)],
        me, saved, saved_far, half_keep, half_far, img_t, img_t_far, kv_keep, kv_far,
        copied=4,
    )
    kv_0, kv_1, mix_0, mix_1, self_far, grad_rows = tie(
        kv_0, kv_1, mix_0, mix_1, self_far, grad_rows
    )
    kv_1, mix_1 = flip(kv_1, "x"), flip(mix_1, "y")
    q_0, q_1, v_0, v_1 = run(
        functools.partial(self_grad_kernel, share),
        [block(D)] * 2 + [block(HALF + LANES)] * 2,
        [SM, VM] + [HB] * 4,
        [vmem((rows, D), BF)] * 2
        + [vmem((rows, 3 * HALF), BF)] * 2
        + [vmem(block(n)[0], BF) for n in (D, D, HALF + LANES, HALF + LANES)]
        + [vmem((D, D), F32), sems(8)],
        me, small, saved, saved_far, self_keep, self_far,
        copied=4,
    )
    q_0, q_1, v_0, v_1, grad_rows = tie(q_0, q_1, v_0, v_1, grad_rows)
    q_1, v_1 = flip(q_1, "y"), flip(v_1, "x")
    part = ((rows // FOLD, 2 * D), BF)
    near, core, chip = run(
        return_kernel,
        [part, part, ((2,) + part[0], BF)],
        [SM] + [VM] * 7,
        [vmem((rows, 2 * D), F32)],
        me, arr, after_cross, table, out_near, out_core, out_far, grad_rows,
    )
    kv_1, mix_1, q_1, v_1, chip = tie(kv_1, mix_1, q_1, v_1, chip)
    kv_2, mix_2, q_2, v_2 = add_up(
        *([(near, 1), (got, 1)] for near, got in ((kv_0, kv_1), (mix_0, mix_1), (q_0, q_1), (v_0, v_1)))
    )
    kv_2, mix_2, q_2, v_2 = flip(kv_2, "y"), flip(mix_2, "x"), flip(q_2, "x"), flip(v_2, "y")
    kv_2, mix_2, q_2, v_2, hidden_got, kv_send, chip = tie(
        kv_2, mix_2, q_2, v_2, hidden_got, kv_send, chip
    )
    (got,) = add_up(
        [(kv_0, 0), (kv_1, 0), kv_2],
        [(mix_0, 0), (mix_1, 0), mix_2],
        [(q_0, 0), (q_1, 0), q_2],
        [(v_0, 0), (v_1, 0), v_2],
        joined=True,
    )
    got = owned(got, 2, ("z", "c"))
    chip = flip(chip, "y")
    hidden_part = ((height, 2 * D), BF)
    hidden_near, hidden_core, hidden_chip = run(
        depth_sum_kernel,
        [hidden_part, hidden_part, ((2,) + hidden_part[0], BF)],
        [SM, VM],
        [vmem((FOLD * height, 2 * D), F32)],
        me, hidden_got,
    )
    hidden_chip = flip(hidden_chip, "y")
    (grad_image,) = run(
        image_grad_kernel,
        [((images, D), BF)],
        [VM, VM, SM] + [HB] * 8,
        [vmem((2, depth, 2, 2, 2 * height, D), BF), sems(8)],
        kv_keep, kv_send, me, *pieces_b,
    )
    grad_up, grad_down = run(
        unpack_hidden_kernel, [flat(FOLD)] * 2, [SM] + [VM] * 4,
        [vmem((FOLD, height, 2 * D), BF)],
        me, hidden_near, hidden_chip, flip(hidden_core, "c"), flip(hidden_chip[1], "c"),
    )
    layer_out, grad_tokens = run(
        collect_kernel, [((FOLD, rows // FOLD, D), BF)] * 2, [SM] + [VM] * 4, [],
        me, near, chip, flip(core, "c"), flip(chip[1], "c"),
    )
    grad_cq, grad_ckv, grad_co, grad_out, grad_qkv, grad_small = run(
        unpack_kernel,
        [flat(n) for n in (1, 2, 1, 1, 3)] + [((8, LANES), F32)],
        [VM],
        [],
        got,
        mib=16,
    )
    return (
        layer_out.reshape(tokens.shape),
        grad_tokens.reshape(tokens.shape),
        grad_image.reshape(image_tokens.shape),
        *(
            g.reshape(-1)
            for g in (grad_qkv, grad_out, grad_cq, grad_ckv, grad_co, grad_up, grad_down)
        ),
        grad_small.reshape(-1)[: small_params.shape[0]],
    )


def general_norm_rows(inputs, gain_vec, shift_vec):
    centred = inputs - jnp.mean(inputs, axis=-1, keepdims=True)
    variance = jnp.mean(centred * centred, axis=-1, keepdims=True)
    return centred * lax.rsqrt(variance + epsilon) * gain_vec + shift_vec


def general_norm_back(inputs, gain_vec, shift_vec, grad_normed):
    _, pullback = jax.vjp(general_norm_rows, inputs, gain_vec, shift_vec)
    return pullback(grad_normed)


def general_gelu_exact(inputs):
    return jax.nn.gelu(inputs, approximate=False)


def general_gelu_back(inputs, grad_active):
    _, pullback = jax.vjp(general_gelu_exact, inputs)
    return pullback(grad_active)[0]


def general_slot_index(lengths, arrivals):
    run_ends = jnp.cumsum(lengths)
    starts = run_ends - lengths
    caption = jnp.sum((run_ends[None, :] <= arrivals[:, None]).astype(jnp.int32), axis=1)
    picked = caption[:, None] == jnp.arange(lengths.shape[0], dtype=jnp.int32)[None, :]
    first_row = jnp.sum(jnp.where(picked, starts[None, :], 0), axis=1)
    return caption * CAP_LEN + arrivals - first_row


def general_score_block(queries, keys_in, allowed):
    scores = jnp.einsum(
        "cqhd,ckhd->chqk", queries, keys_in, preferred_element_type=jnp.float32
    ) * HEAD_DIM ** (-0.5)
    return jnp.where(allowed, scores, -masked_fill)


def general_attention(queries, keys_in, values, allowed):
    scores = general_score_block(queries, keys_in, allowed)
    row_max = jnp.max(scores, axis=-1, keepdims=True)
    log_total = row_max + jnp.log(jnp.sum(jnp.exp(scores - row_max), axis=-1, keepdims=True))
    attn_weights = jnp.exp(scores - log_total).astype(jnp.bfloat16)
    mixed_out = jnp.einsum(
        "chqk,ckhd->cqhd", attn_weights, values, preferred_element_type=jnp.float32
    ).astype(jnp.bfloat16)
    return (mixed_out, log_total)


def general_attention_back(queries, keys_in, values, log_total, grad_mixed, allowed):
    scores = general_score_block(queries, keys_in, allowed)
    attn_weights = jnp.exp(scores - log_total)
    grad_weights = jnp.einsum(
        "cqhd,ckhd->chqk", grad_mixed, values, preferred_element_type=jnp.float32
    )
    centre = jnp.sum(attn_weights * grad_weights, axis=-1, keepdims=True)
    grad_scores = (attn_weights * (grad_weights - centre)).astype(jnp.bfloat16)
    grad_queries = jnp.einsum(
        "chqk,ckhd->cqhd", grad_scores, keys_in, preferred_element_type=jnp.float32
    ) * HEAD_DIM ** (-0.5)
    grad_keys = jnp.einsum(
        "chqk,cqhd->ckhd", grad_scores, queries, preferred_element_type=jnp.float32
    ) * HEAD_DIM ** (-0.5)
    grad_values = jnp.einsum(
        "chqk,cqhd->ckhd",
        attn_weights.astype(jnp.bfloat16),
        grad_mixed,
        preferred_element_type=jnp.float32,
    )
    return (grad_queries, grad_keys, grad_values)


def general_unpack_params(gathered):
    (
        flat_qkv,
        flat_out,
        flat_cross_q,
        flat_cross_kv,
        flat_cross_out,
        flat_up,
        flat_down,
        flat_small,
    ) = gathered
    small_vals = flat_small.astype(jnp.float32)
    return (
        flat_qkv.reshape(D, 3 * D),
        flat_out.reshape(D, D),
        flat_cross_q.reshape(D, D),
        flat_cross_kv.reshape(V, 2 * D),
        flat_cross_out.reshape(D, D),
        flat_up.reshape(D, FF),
        flat_down.reshape(FF, D),
        small_vals[: 3 * D].reshape(3, D),
        small_vals[3 * D : 6 * D].reshape(3, D),
        small_vals[6 * D : 6 * D + FF],
        small_vals[6 * D + FF :],
    )


def general_forward(slotted, image_rows, params, allowed, open_mask):
    (
        mat_qkv,
        mat_out,
        mat_cross_q,
        mat_cross_kv,
        mat_cross_out,
        mat_up,
        mat_down,
        norm_gains,
        shifts,
        up_bias,
        down_bias,
    ) = params
    captions = slotted.shape[0] // CAP_LEN
    head_count = D // HEAD_DIM
    normed_self = general_norm_rows(slotted, norm_gains[0], shifts[0]).astype(jnp.bfloat16)
    projected = jnp.dot(normed_self, mat_qkv, preferred_element_type=jnp.float32).astype(
        jnp.bfloat16
    )
    projected = projected.reshape(captions, CAP_LEN, 3, head_count, HEAD_DIM)
    self_mixed, self_total = general_attention(
        projected[:, :, 0], projected[:, :, 1], projected[:, :, 2], allowed
    )
    self_mixed = self_mixed.reshape(-1, D)
    after_self = slotted + jnp.dot(self_mixed, mat_out, preferred_element_type=jnp.float32)
    normed_cross = general_norm_rows(after_self, norm_gains[1], shifts[1]).astype(jnp.bfloat16)
    cross_query = jnp.dot(normed_cross, mat_cross_q, preferred_element_type=jnp.float32).astype(
        jnp.bfloat16
    )
    cross_query = cross_query.reshape(captions, CAP_LEN, head_count, HEAD_DIM)
    image_kv = jnp.dot(image_rows, mat_cross_kv, preferred_element_type=jnp.float32).astype(
        jnp.bfloat16
    )
    image_kv = image_kv.reshape(captions, IMG, 2, head_count, HEAD_DIM)
    cross_mixed, cross_total = general_attention(
        cross_query, image_kv[:, :, 0], image_kv[:, :, 1], open_mask
    )
    cross_mixed = cross_mixed.reshape(-1, D)
    after_cross = after_self + jnp.dot(
        cross_mixed, mat_cross_out, preferred_element_type=jnp.float32
    )
    normed_mlp = general_norm_rows(after_cross, norm_gains[2], shifts[2]).astype(jnp.bfloat16)
    hidden = jnp.dot(normed_mlp, mat_up, preferred_element_type=jnp.float32) + up_bias
    activated = general_gelu_exact(hidden).astype(jnp.bfloat16)
    result = (
        after_cross + jnp.dot(activated, mat_down, preferred_element_type=jnp.float32) + down_bias
    )
    saved_state = (
        slotted,
        normed_self,
        projected,
        self_total,
        self_mixed,
        after_self,
        normed_cross,
        cross_query,
        image_kv,
        cross_total,
        cross_mixed,
        after_cross,
        normed_mlp,
        hidden,
        activated,
    )
    return (result, saved_state)


def general_backward(saved_state, grad_slot, image_rows, params, allowed, open_mask):
    (
        mat_qkv,
        mat_out,
        mat_cross_q,
        mat_cross_kv,
        mat_cross_out,
        mat_up,
        mat_down,
        norm_gains,
        shifts,
        up_bias,
        down_bias,
    ) = params
    (
        slotted,
        normed_self,
        projected,
        self_total,
        self_mixed,
        after_self,
        normed_cross,
        cross_query,
        image_kv,
        cross_total,
        cross_mixed,
        after_cross,
        normed_mlp,
        hidden,
        activated,
    ) = saved_state
    captions = slotted.shape[0] // CAP_LEN
    head_count = D // HEAD_DIM
    grad_branch = grad_slot.astype(jnp.bfloat16)
    grad_down = jnp.einsum("rf,rd->fd", activated, grad_branch, preferred_element_type=jnp.float32)
    grad_down_bias = jnp.sum(grad_slot, axis=0)
    grad_active = jnp.einsum("rd,fd->rf", grad_branch, mat_down, preferred_element_type=jnp.float32)
    grad_hidden = general_gelu_back(hidden, grad_active).astype(jnp.bfloat16)
    grad_up = jnp.einsum("rd,rf->df", normed_mlp, grad_hidden, preferred_element_type=jnp.float32)
    grad_up_bias = jnp.sum(grad_hidden.astype(jnp.float32), axis=0)
    grad_normed = jnp.einsum("rf,df->rd", grad_hidden, mat_up, preferred_element_type=jnp.float32)
    grad_cross_in, grad_gain3, grad_shift3 = general_norm_back(
        after_cross, norm_gains[2], shifts[2], grad_normed
    )
    grad_after_cross = grad_slot + grad_cross_in
    grad_branch = grad_after_cross.astype(jnp.bfloat16)
    grad_cross_out = jnp.einsum(
        "rd,re->de", cross_mixed, grad_branch, preferred_element_type=jnp.float32
    )
    grad_mixed = jnp.einsum(
        "re,de->rd", grad_branch, mat_cross_out, preferred_element_type=jnp.float32
    ).astype(jnp.bfloat16)
    grad_mixed = grad_mixed.reshape(captions, CAP_LEN, head_count, HEAD_DIM)
    grad_query, grad_key, grad_value = general_attention_back(
        cross_query, image_kv[:, :, 0], image_kv[:, :, 1], cross_total, grad_mixed, open_mask
    )
    grad_query = grad_query.reshape(-1, D).astype(jnp.bfloat16)
    grad_kv = jnp.stack([grad_key, grad_value], axis=2).reshape(-1, 2 * D).astype(jnp.bfloat16)
    grad_cross_q = jnp.einsum(
        "rd,re->de", normed_cross, grad_query, preferred_element_type=jnp.float32
    )
    grad_cross_kv = jnp.einsum("iv,ie->ve", image_rows, grad_kv, preferred_element_type=jnp.float32)
    grad_image = jnp.einsum(
        "ie,ve->iv", grad_kv, mat_cross_kv, preferred_element_type=jnp.float32
    ).astype(jnp.bfloat16)
    grad_normed = jnp.einsum(
        "re,de->rd", grad_query, mat_cross_q, preferred_element_type=jnp.float32
    )
    grad_self_in, grad_gain2, grad_shift2 = general_norm_back(
        after_self, norm_gains[1], shifts[1], grad_normed
    )
    grad_after_self = grad_after_cross + grad_self_in
    grad_branch = grad_after_self.astype(jnp.bfloat16)
    grad_out = jnp.einsum("rd,re->de", self_mixed, grad_branch, preferred_element_type=jnp.float32)
    grad_mixed = jnp.einsum(
        "re,de->rd", grad_branch, mat_out, preferred_element_type=jnp.float32
    ).astype(jnp.bfloat16)
    grad_mixed = grad_mixed.reshape(captions, CAP_LEN, head_count, HEAD_DIM)
    grad_query, grad_key, grad_value = general_attention_back(
        projected[:, :, 0], projected[:, :, 1], projected[:, :, 2], self_total, grad_mixed, allowed
    )
    grad_projected = (
        jnp.stack([grad_query, grad_key, grad_value], axis=2)
        .reshape(-1, 3 * D)
        .astype(jnp.bfloat16)
    )
    grad_w_qkv = jnp.einsum(
        "rd,re->de", normed_self, grad_projected, preferred_element_type=jnp.float32
    )
    grad_normed = jnp.einsum(
        "re,de->rd", grad_projected, mat_qkv, preferred_element_type=jnp.float32
    )
    grad_input, grad_gain1, grad_shift1 = general_norm_back(slotted, norm_gains[0], shifts[0], grad_normed)
    grad_input = grad_input + grad_after_self
    grad_small = jnp.concatenate(
        [
            grad_gain1,
            grad_gain2,
            grad_gain3,
            grad_shift1,
            grad_shift2,
            grad_shift3,
            grad_up_bias,
            grad_down_bias,
        ]
    )
    flat_grads = (
        grad_w_qkv.reshape(-1),
        grad_out.reshape(-1),
        grad_cross_q.reshape(-1),
        grad_cross_kv.reshape(-1),
        grad_cross_out.reshape(-1),
        grad_up.reshape(-1),
        grad_down.reshape(-1),
        grad_small,
    )
    return (grad_input, grad_image, flat_grads)


def general_sum_to_owners(flat_grads):
    summed = []
    for grad_vec in flat_grads:
        for axis in ("dp", "fsdp"):
            parts = grad_vec.reshape(lax.axis_size(axis), -1).astype(jnp.bfloat16)
            if axis == "dp":
                parts = grad_vec.reshape(lax.axis_size("dp"), lax.axis_size("fsdp"), -1)
                parts = parts.astype(jnp.bfloat16)
            got = lax.all_to_all(parts, axis, split_axis=0, concat_axis=0, tiled=True)
            grad_vec = jnp.sum(got.astype(jnp.float32), axis=0)
        summed.append(grad_vec)
    return tuple(summed)


def general_device(
    tokens,
    image_tokens,
    caption_lengths,
    arrival_order,
    w_qkv,
    w_out,
    w_cross_q,
    w_cross_kv,
    w_cross_out,
    w_up,
    w_down,
    small_params,
    cotangent,
):
    lengths = caption_lengths[0]
    slot_rows = general_slot_index(lengths, arrival_order[0])
    captions = lengths.shape[0]
    slot_total = captions * CAP_LEN
    arrived, arrived_grad = (
        lax.all_to_all(tokens, "fsdp", split_axis=0, concat_axis=0, tiled=True),
        lax.all_to_all(cotangent, "fsdp", split_axis=0, concat_axis=0, tiled=True),
    )
    slotted = jnp.zeros((slot_total, D), jnp.float32).at[slot_rows].set(arrived.astype(jnp.float32))
    grad_slot = (
        jnp.zeros((slot_total, D), jnp.float32).at[slot_rows].set(arrived_grad.astype(jnp.float32))
    )
    positions = jnp.arange(CAP_LEN, dtype=jnp.int32)
    allowed = (positions[None, :] <= positions[:, None])[None, None] & (
        positions[None, None, None, :] < lengths[:, None, None, None]
    )
    open_mask = jnp.ones((1, 1, 1, 1), jnp.bool_)
    image_rows = image_tokens.reshape(-1, V)
    owned_shards = (w_qkv, w_out, w_cross_q, w_cross_kv, w_cross_out, w_up, w_down, small_params)
    params = general_unpack_params(
        tuple(lax.all_gather(w, ("dp", "fsdp"), axis=0, tiled=True) for w in owned_shards)
    )
    result, saved_state = general_forward(slotted, image_rows, params, allowed, open_mask)
    grad_input, grad_image, flat_grads = general_backward(
        saved_state, grad_slot, image_rows, params, allowed, open_mask
    )
    summed = general_sum_to_owners(flat_grads)
    out_rows = result[slot_rows].astype(jnp.bfloat16)
    grad_rows = grad_input[slot_rows].astype(jnp.bfloat16)
    layer_out, grad_tokens = (
        lax.all_to_all(out_rows, "fsdp", split_axis=0, concat_axis=0, tiled=True),
        lax.all_to_all(grad_rows, "fsdp", split_axis=0, concat_axis=0, tiled=True),
    )
    return (layer_out, grad_tokens, grad_image.reshape(image_tokens.shape)) + tuple(summed)


def solution(mesh):
    dp, fsdp = mesh.shape["dp"], mesh.shape["fsdp"]
    inner, specs_of = on_device, ("dp", "fsdp")
    if fsdp == 4 and dp % 2 == 0 and D % (dp * fsdp * 8) == 0:
        mesh = Mesh(mesh.devices.reshape(dp // 2, 2, 2, 2), AXES)
        specs_of = AXES
    else:
        inner = general_device
    rows, flat, cube = P(specs_of, None), P(specs_of), P(specs_of, None, None)
    return jax.shard_map(
        inner,
        mesh=mesh,
        in_specs=(rows, cube, rows, rows) + (flat,) * 8 + (rows,),
        out_specs=(rows, rows, cube) + (flat,) * 8,
        check_vma=False,
    )
```

profile of v0, /device:TPU:0, one launch (start us, length us, event | category | flops | bytes accessed | tf_op | source)
XLA Modules:
  0.0 281.8 jit_solution(17995333157331352307)
XLA Ops:
  0.7 1.8 pack_self_kernel.1
  2.5 6.3 %all-to-all-start = ((bf16[8,24,1536]{2,1,0:T(8,128)(2,1)}), bf16[8,24,1536]{2,1,0:T(8,128)(2,1)S(1)}, u32[]{:S(2)}, u32[]{:S(2)}) async-start(bf16[8,24,1536]{2,1,0:T(8,128)(2,1)} %bitcast.59), calls=%async_computation | async-start | bytes 1179648 | tf_op jit(solution)/shard_map/all_to_all | solution.py:833
  9.5 2.9 %pack_group_kernel.1 = (bf16[80,1536]{1,0:T(8,128)(2,1)}, bf16[80,1536]{1,0:T(8,128)(2,1)}, bf16[2,80,1536]{2,1,0:T(8,128)(2,1)}) custom-call(s32[1,4]{1,0:T(1,128)} %add_bitcast_fusion.me.refs_0_, bf16[576,128]{1,0:T(8,128)(2,1)} %bitcast.64, bf16[576,128]{1,0:T(8,128)(2,1)} %bitcast.65, bf16[4,40,768]{2,1,0:T(8,128)(2,1)} %bitcast.62, ...), custom_call_target="tpu_custom_call" | custom-call | tf_op jit(solution)/shard_map/pack_group_kernel/pallas_call | solution.py:792
  12.4 1.5 collective-permute-start
  14.5 3.1 %transpose_kernel.1.refs_4_ = bf16[768,1024]{1,0:T(8,128)(2,1)} custom-call(bf16[1024,768]{1,0:T(8,128)(2,1)} %bitcast.50), custom_call_target="tpu_custom_call" | custom-call | tf_op jit(solution)/shard_map/transpose_kernel/pallas_call | solution.py:792
  17.6 1.9 pack_cross_kernel.1
  19.5 6.7 %collective-permute-done.chip = bf16[2,80,1536]{2,1,0:T(8,128)(2,1)S(1)} collective-permute-done((bf16[2,80,1536]{2,1,0:T(8,128)(2,1)}, bf16[2,80,1536]{2,1,0:T(8,128)(2,1)S(1)}, u32[]{:S(2)}, u32[]{:S(2)}) %collective-permute-start) | collective-permute-done | bytes 491552 | tf_op jit(solution)/shard_map/ppermute | solution.py:829
  26.3 4.8 %all-to-all-start.1 = ((bf16[8,24,1664]{2,1,0:T(8,128)(2,1)}), bf16[8,24,1664]{2,1,0:T(8,128)(2,1)S(1)}, u32[]{:S(2)}, u32[]{:S(2)}) async-start(bf16[8,24,1664]{2,1,0:T(8,128)(2,1)} %bitcast.58), calls=%async_computation.1 | async-start | bytes 1277952 | tf_op jit(solution)/shard_map/all_to_all | solution.py:833
  31.7 1.5 collective-permute-start.4
  33.2 1.5 collective-permute-start.3
  34.8 1.5 collective-permute-done.2.both
  38.5 2.9 %spread_kernel.1 = (bf16[4,4,24,1536]{3,2,1,0:T(8,128)(2,1)}, bf16[160,768]{1,0:T(8,128)(2,1)}, bf16[160,768]{1,0:T(8,128)(2,1)}) custom-call(s32[1,4]{1,0:T(1,128)} %add_bitcast_fusion.me.refs_0_, s32[1,160]{1,0:T(1,128)} %arr.3, bf16[80,1536]{1,0:T(8,128)(2,1)} %get-tuple-element.154.near, bf16[2,80,1536]{2,1,0:T(8,128)(2,1)} %copy-done.25, ...), custom_call_target="tpu_custom_call" | custom-call | tf_op jit(solution)/shard_map/spread_kernel/pallas_call | solution.py:792
  41.4 5.5 %collective-permute-done.4.refs_1_ = bf16[4,48,1536]{2,1,0:T(8,128)(2,1)S(1)} collective-permute-done((bf16[4,48,1536]{2,1,0:T(8,128)(2,1)S(1)}, bf16[4,48,1536]{2,1,0:T(8,128)(2,1)S(1)}, u32[]{:S(2)}, u32[]{:S(2)}) %collective-permute-start.4) | collective-permute-done | bytes 589856 | tf_op jit(solution)/shard_map/ppermute | solution.py:829
  50.2 4.5 %all-to-all-start.2 = ((bf16[4,96,1536]{2,1,0:T(8,128)(2,1)}), bf16[4,96,1536]{2,1,0:T(8,128)(2,1)}, u32[]{:S(2)}, u32[]{:S(2)}) async-start(bf16[4,96,1536]{2,1,0:T(8,128)(2,1)} %bitcast.61), calls=%async_computation.2 | async-start | bytes 2359296 | tf_op jit(solution)/shard_map/all_to_all | solution.py:833
  54.8 1.5 collective-permute-start.8
  58.3 1.7 collective-permute-done.9.refs_6_
  60.9 10.7 %collective-permute-done.8.refs_9_.refs_1_.refs_2_ = bf16[4,48,1664]{2,1,0:T(8,128)(2,1)S(1)} collective-permute-done((bf16[4,48,1664]{2,1,0:T(8,128)(2,1)S(1)}, bf16[4,48,1664]{2,1,0:T(8,128)(2,1)S(1)}, u32[]{:S(2)}, u32[]{:S(2)}) %collective-permute-start.8) | collective-permute-done | bytes 639008 | tf_op jit(solution)/shard_map/ppermute | solution.py:829
  75.4 14.6 %collective-permute-done.12.refs_3_ = bf16[4,48,1536]{2,1,0:T(8,128)(2,1)S(1)} collective-permute-done((bf16[4,48,1536]{2,1,0:T(8,128)(2,1)}, bf16[4,48,1536]{2,1,0:T(8,128)(2,1)S(1)}, u32[]{:S(2)}, u32[]{:S(2)}) %collective-permute-start.12) | collective-permute-done | bytes 589856 | tf_op jit(solution)/shard_map/ppermute | solution.py:829
  92.4 2.6 collective-permute-done.16.refs_7_
  96.2 14.6 %forward_kernel.1 = (f32[11,768]{1,0:T(8,128)}, bf16[160,2304]{1,0:T(8,128)(2,1)}, bf16[3,640,160]{2,1,0:T(8,128)(2,1)}, bf16[160,3072]{1,0:T(8,128)(2,1)}, f32[...) custom-call(s32[1,4]{1,0:T(1,128)} %lens.3, ...), custom_call_target="tpu_custom_call" | custom-call | tf_op jit(solution)/shard_map/forward_kernel/pallas_call | solution.py:792
  110.9 1.5 collective-permute-start.19
  113.1 6.4 %collective-permute-done.19.refs_2_ = bf16[160,768]{1,0:T(8,128)(2,1)S(1)} collective-permute-done((bf16[160,768]{1,0:T(8,128)(2,1)}, bf16[160,768]{1,0:T(8,128)(2,1)S(1)}, u32[]{:S(2)}, u32[]{:S(2)}) %collective-permute-start.19) | collective-permute-done | bytes 245792 | tf_op jit(solution)/shard_map/ppermute | solution.py:829
  121.0 2.2 collective-permute-done.24.refs_9_
  124.3 8.8 %mlp_kernel.1 = (f32[160,768]{1,0:T(8,128)}, bf16[160,768]{1,0:T(8,128)(2,1)}, bf16[160,768]{1,0:T(8,128)(2,1)}, bf16[160,768]{1,0:T(8,128)(2,1)}, f32[160,768]{...) custom-call(s32[1,4]{1,0:T(1,128)} %add_bitcast_fusion.me.refs_0_, ...), custom_call_target="tpu_custom_call" | custom-call | tf_op jit(solution)/shard_map/mlp_kernel/pallas_call | solution.py:792
  136.5 5.7 %hidden_grad_kernel.1 = bf16[768,1536]{1,0:T(8,128)(2,1)} custom-call(bf16[160,768]{1,0:T(8,128)(2,1)} %get-tuple-element.199.refs_0_, bf16[160,768]{1,0:T(8,128)(2,1)} %copy-done.29, bf16[160,768]{1,0:T(8,128)(2,1)} %copy-done.27, bf16[160,768]{1,0:T(8,128)(2,1)} %copy-done.30, bf16[160,768]{1,0:T(8,128)(2,1)} %get-tuple-element.200.refs_4_.grad_slot, ...), custom_call_target="tpu_custom_call" | custom-call | tf_op jit(solution)/shard_map/hidden_grad_kernel/pallas_call | solution.py:792
  142.2 1.7 collective-permute-done.26.grad_far
  144.6 5.3 %all-to-all-start.3 = ((bf16[8,96,1536]{2,1,0:T(8,128)(2,1)}), bf16[8,96,1536]{2,1,0:T(8,128)(2,1)S(1)}, u32[]{:S(2)}, u32[]{:S(2)}) async-start(bf16[8,96,1536]{2,1,0:T(8,128)(2,1)} %bitcast.49), calls=%async_computation.3 | async-start | bytes 4718592 | tf_op jit(solution)/shard_map/all_to_all | solution.py:833
  149.9 11.9 %cross_back_kernel.1 = (f32[160,768]{1,0:T(8,128)}, f32[66,128]{1,0:T(8,128)}, bf16[160,1152]{1,0:T(8,128)(2,1)}, bf16[160,1152]{1,0:T(8,128)(2,1)}, bf16[1024,7...) custom-call(s32[1,4]{1,0:T(1,128)} %lens.3, s32[1,4]{1,0:T(1,128)} %add_bitcast_fusion.me.refs_0_, ...), custom_call_target="tpu_custom_call" | custom-call | tf_op jit(solution)/shard_map/cross_back_kernel/pallas_call | solution.py:792
  163.2 8.2 %self_back_kernel.1 = (bf16[160,768]{1,0:T(8,128)(2,1)}, f32[66,128]{1,0:T(8,128)}, bf16[160,1152]{1,0:T(8,128)(2,1)}, bf16[160,1152]{1,0:T(8,128)(2,1)}) custom-call(s32[1,4]{1,0:T(1,128)} %add_bitcast_fusion.me.refs_0_, f32[160,768]{1,0:T(8,128)} %get-tuple-element.224.grad_state, bf16[3,640,160]{2,1,0:T(8,128)(2,1)} %get-tuple-element.225.probs, ...), custom_call_target="tpu_custom_call" | custom-call | tf_op jit(solution)/shard_map/self_back_kernel/pallas_call | solution.py:792
  172.7 9.7 %cross_grad_kernel.1 = (bf16[2,4,48,1152]{3,2,1,0:T(8,128)(2,1)}, bf16[2,4,48,1152]{3,2,1,0:T(8,128)(2,1)}, bf16[2,4,48,768]{3,2,1,0:T(8,128)(2,1)}, bf16[2,4,48,768]{3,2,1,0:T(8,128)(2,1)}) custom-call(s32[1,4]{1,0:T(1,128)} %add_bitcast_fusion.me.refs_0_, bf16[160,3072]{1,0:T(8,128)(2,1)} %get-tuple-element.208.refs_0_, bf16[160,3072]{1,0:T(8,128)(2,1)} %copy-done.11, ...), custom_call_target="tpu_custom_call" | custom-call | tf_op jit(solution)/shard_map/cross_grad_kernel/pallas_call | solution.py:792
  182.5 2.1 collective-permute-start.35
  184.6 4.8 %self_grad_kernel.1 = (bf16[2,4,48,768]{3,2,1,0:T(8,128)(2,1)}, bf16[2,4,48,768]{3,2,1,0:T(8,128)(2,1)}, bf16[2,4,48,512]{3,2,1,0:T(8,128)(2,1)}, bf16[2,4,48,512]{3,2,1,0:T(8,128)(2,1)}) custom-call(s32[1,4]{1,0:T(1,128)} %add_bitcast_fusion.me.refs_0_, f32[66,128]{1,0:T(8,128)} %get-tuple-element.235.small, bf16[160,3072]{1,0:T(8,128)(2,1)} %get-tuple-element.208.refs_0_, ...), custom_call_target="tpu_custom_call" | custom-call | tf_op jit(solution)/shard_map/self_grad_kernel/pallas_call | solution.py:792
  192.2 1.7 collective-permute-done.29.out_core
  194.6 2.6 return_kernel.1
  197.2 20.2 %collective-permute-done.38.refs_7_.refs_10_ = bf16[2,4,48,512]{3,2,1,0:T(8,128)(2,1)S(1)} collective-permute-done((bf16[2,4,48,512]{3,2,1,0:T(8,128)(2,1)}, bf16[2,4,48,512]{3,2,1,0:T(8,128)(2,1)S(1)}, u32[]{:S(2)}, u32[]{:S(2)}) %collective-permute-start.38) | collective-permute-done | bytes 393248 | tf_op jit(solution)/shard_map/ppermute | solution.py:829
  218.8 2.7 add_kernel.2
  221.5 1.6 collective-permute-start.39
  223.2 2.4 collective-permute-start.40
  226.0 11.4 %collective-permute-done.42.refs_11_ = bf16[4,48,512]{2,1,0:T(8,128)(2,1)S(1)} collective-permute-done((bf16[4,48,512]{2,1,0:T(8,128)(2,1)}, bf16[4,48,512]{2,1,0:T(8,128)(2,1)S(1)}, u32[]{:S(2)}, u32[]{:S(2)}) %collective-permute-start.42) | collective-permute-done | bytes 196640 | tf_op jit(solution)/shard_map/ppermute | solution.py:829
  239.2 4.3 %add_kernel.3 = bf16[4,48,3200]{2,1,0:T(8,128)(2,1)} custom-call(bf16[2,4,48,1152]{3,2,1,0:T(8,128)(2,1)} %get-tuple-element.257.refs_0_, bf16[2,4,48,1152]{3,2,1,0:T(8,128)(2,1)} %copy-done.12, bf16[4,48,1152]{2,1,0:T(8,128)(2,1)} %copy-done.32, bf16[2,4,48,768]{3,2,1,0:T(8,128)(2,1)} %get-tuple-element.264.refs_2_.refs_3_, ...), custom_call_target="tpu_custom_call" | custom-call | tf_op jit(solution)/shard_map/add_kernel/pallas_call | solution.py:817
  243.5 5.9 %all-to-all-start.4 = ((bf16[8,24,3200]{2,1,0:T(8,128)(2,1)}), bf16[8,24,3200]{2,1,0:T(8,128)(2,1)S(1)}, u32[]{:S(2)}, u32[]{:S(2)}) async-start(bf16[8,24,3200]{2,1,0:T(8,128)(2,1)} %bitcast.57), calls=%async_computation.4 | async-start | bytes 2457600 | tf_op jit(solution)/shard_map/all_to_all | solution.py:833
  251.1 2.9 %depth_sum_kernel.1 = (bf16[24,1536]{1,0:T(8,128)(2,1)}, bf16[24,1536]{1,0:T(8,128)(2,1)}, bf16[2,24,1536]{2,1,0:T(8,128)(2,1)}) custom-call(s32[1,4]{1,0:T(1,128)} %add_bitcast_fusion.me.refs_0_, bf16[8,96,1536]{2,1,0:T(8,128)(2,1)} %copy-done.3), custom_call_target="tpu_custom_call" | custom-call | tf_op jit(solution)/shard_map/depth_sum_kernel/pallas_call | solution.py:792
  254.9 3.4 %collective-permute-done.43.chip = bf16[2,40,1536]{2,1,0:T(8,128)(2,1)S(1)} collective-permute-done((bf16[2,40,1536]{2,1,0:T(8,128)(2,1)S(1)}, bf16[2,40,1536]{2,1,0:T(8,128)(2,1)S(1)}, u32[]{:S(2)}, u32[]{:S(2)}) %collective-permute-start.43) | collective-permute-done | bytes 245792 | tf_op jit(solution)/shard_map/ppermute | solution.py:829
  258.4 2.6 collective-permute-done.46.chip
  261.1 7.4 %image_grad_kernel.1 = bf16[1024,768]{1,0:T(8,128)(2,1)} custom-call(bf16[1024,768]{1,0:T(8,128)(2,1)} %get-tuple-element.241.refs_6_.kv_keep, bf16[1024,768]{1,0:T(8,128)(2,1)} %get-tuple-element.280.kv_send, s32[1,4]{1,0:T(1,128)} %add_bitcast_fusion.me.refs_0_, bf16[4,48,1664]{2,1,0:T(8,128)(2,1)} %bitcast.48, bf16[4,48,1664]{2,1,0:T(8,128)(2,1)} %copy-done.5, ...), custom_call_target="tpu_custom_call" | custom-call | tf_op jit(solution)/shard_map/image_grad_kernel/pallas_call | solution.py:792
  269.1 2.5 unpack_hidden_kernel.1
  272.3 2.0 collect_kernel.1
  274.3 5.7 %all-to-all-done.4 = bf16[8,24,3200]{2,1,0:T(8,128)(2,1)S(1)} async-done(((bf16[8,24,3200]{2,1,0:T(8,128)(2,1)}), bf16[8,24,3200]{2,1,0:T(8,128)(2,1)S(1)}, u32[]{:S(2)}, u32[]{:S(2)}) %all-to-all-start.4) | async-done | bytes 1228832 | tf_op jit(solution)/shard_map/all_to_all | solution.py:833
  (196 shorter events, 40.4 us)
Async XLA Ops:
  2.5 23.8 %all-to-all-start = ((bf16[8,24,1536]{2,1,0:T(8,128)(2,1)}), bf16[8,24,1536]{2,1,0:T(8,128)(2,1)S(1)}, u32[]{:S(2)}, u32[]{:S(2)}) async-start(bf16[8,24,1536]{2,1,0:T(8,128)(2,1)} %bitcast.59), calls=%async_computation | async-start | bytes 1179648 | tf_op jit(solution)/shard_map/all_to_all | solution.py:833
  12.4 13.8 %collective-permute-start = (bf16[2,80,1536]{2,1,0:T(8,128)(2,1)}, bf16[2,80,1536]{2,1,0:T(8,128)(2,1)S(1)}, u32[]{:S(2)}, u32[]{:S(2)}) collective-permute-start(bf16[2,80,1536]{2,1,0:T(8,128)(2,1)} %get-tuple-element.155), channel_id=1, source_target_pairs={{0,2},{2,0},{1,3},{3,1},{4,6},{6,4},{5,7},{7,5},{8,10},{10,8},{9,1... | collective-permute-start | bytes 1474568 | tf_op jit(solution)/shard_map/ppermute | solution.py:829
  26.2 22.7 %collective-permute-start.5 = (bf16[768,1024]{1,0:T(8,128)(2,1)}, bf16[768,1024]{1,0:T(8,128)(2,1)S(1)}, u32[]{:S(2)}, u32[]{:S(2)}) collective-permute-start(bf16[768,1024]{1,0:T(8,128)(2,1)} %transpose_kernel.1.refs_4_), channel_id=1, source_target_pairs={{0,1},{1,0},{2,3},{3,2},{4,5},{5,4},{6,7},{7,6},{8,9},{9,8},{10,11... | collective-permute-start | bytes 4718600 | tf_op jit(solution)/shard_map/ppermute | solution.py:829
  26.3 22.7 %all-to-all-start.1 = ((bf16[8,24,1664]{2,1,0:T(8,128)(2,1)}), bf16[8,24,1664]{2,1,0:T(8,128)(2,1)S(1)}, u32[]{:S(2)}, u32[]{:S(2)}) async-start(bf16[8,24,1664]{2,1,0:T(8,128)(2,1)} %bitcast.58), calls=%async_computation.1 | async-start | bytes 1277952 | tf_op jit(solution)/shard_map/all_to_all | solution.py:833
  31.2 10.2 %collective-permute-start.6 = (bf16[4,48,1536]{2,1,0:T(8,128)(2,1)S(1)}, bf16[4,48,1536]{2,1,0:T(8,128)(2,1)S(1)}, u32[]{:S(2)}, u32[]{:S(2)}) collective-permute-start(bf16[4,48,1536]{2,1,0:T(8,128)(2,1)S(1)} %bitcast.52), channel_id=1, source_target_pairs={{0,1},{1,0},{2,3},{3,2},{4,5},{5,4},{6,7},{7,6},{8,9},{9,8},{10,11... | collective-permute-start | bytes 1769480 | tf_op jit(solution)/shard_map/ppermute | solution.py:829
  31.7 15.2 %collective-permute-start.4 = (bf16[4,48,1536]{2,1,0:T(8,128)(2,1)S(1)}, bf16[4,48,1536]{2,1,0:T(8,128)(2,1)S(1)}, u32[]{:S(2)}, u32[]{:S(2)}) collective-permute-start(bf16[4,48,1536]{2,1,0:T(8,128)(2,1)S(1)} %bitcast.53), channel_id=1, source_target_pairs={{0,2},{2,0},{1,3},{3,1},{4,6},{6,4},{5,7},{7,5},{8,10},{10,8},{9,1... | collective-permute-start | bytes 1769480 | tf_op jit(solution)/shard_map/ppermute | solution.py:829
  33.2 15.1 %collective-permute-start.3 = (bf16[4,48,1536]{2,1,0:T(8,128)(2,1)S(1)}, bf16[4,48,1536]{2,1,0:T(8,128)(2,1)}, u32[]{:S(2)}, u32[]{:S(2)}) collective-permute-start(bf16[4,48,1536]{2,1,0:T(8,128)(2,1)S(1)} %bitcast.54), channel_id=1, source_target_pairs={{0,4},{4,0},{1,5},{5,1},{2,6},{6,2},{3,7},{7,3},{8,12},{12,8},{9,1... | collective-permute-start | bytes 1769480 | tf_op jit(solution)/shard_map/ppermute | solution.py:829
  50.2 41.6 %all-to-all-start.2 = ((bf16[4,96,1536]{2,1,0:T(8,128)(2,1)}), bf16[4,96,1536]{2,1,0:T(8,128)(2,1)}, u32[]{:S(2)}, u32[]{:S(2)}) async-start(bf16[4,96,1536]{2,1,0:T(8,128)(2,1)} %bitcast.61), calls=%async_computation.2 | async-start | bytes 2359296 | tf_op jit(solution)/shard_map/all_to_all | solution.py:833
  54.7 6.1 %collective-permute-start.11 = (bf16[4,48,1664]{2,1,0:T(8,128)(2,1)S(1)}, bf16[4,48,1664]{2,1,0:T(8,128)(2,1)S(1)}, u32[]{:S(2)}, u32[]{:S(2)}) collective-permute-start(bf16[4,48,1664]{2,1,0:T(8,128)(2,1)S(1)} %bitcast.43), channel_id=1, source_target_pairs={{0,1},{1,0},{2,3},{3,2},{4,5},{5,4},{6,7},{7,6},{8,9},{9,8},{10,11... | collective-permute-start | bytes 1916936 | tf_op jit(solution)/shard_map/ppermute | solution.py:829
  54.8 16.8 %collective-permute-start.8 = (bf16[4,48,1664]{2,1,0:T(8,128)(2,1)S(1)}, bf16[4,48,1664]{2,1,0:T(8,128)(2,1)S(1)}, u32[]{:S(2)}, u32[]{:S(2)}) collective-permute-start(bf16[4,48,1664]{2,1,0:T(8,128)(2,1)S(1)} %bitcast.44), channel_id=1, source_target_pairs={{0,2},{2,0},{1,3},{3,1},{4,6},{6,4},{5,7},{7,5},{8,10},{10,8},{9,1... | collective-permute-start | bytes 1916936 | tf_op jit(solution)/shard_map/ppermute | solution.py:829
  56.3 16.5 %collective-permute-start.7 = (bf16[4,48,1664]{2,1,0:T(8,128)(2,1)S(1)}, bf16[4,48,1664]{2,1,0:T(8,128)(2,1)S(1)}, u32[]{:S(2)}, u32[]{:S(2)}) collective-permute-start(bf16[4,48,1664]{2,1,0:T(8,128)(2,1)S(1)} %bitcast.45), channel_id=1, source_target_pairs={{0,4},{4,0},{1,5},{5,1},{2,6},{6,2},{3,7},{7,3},{8,12},{12,8},{9,1... | collective-permute-start | bytes 1916936 | tf_op jit(solution)/shard_map/ppermute | solution.py:829
  57.8 3.1 %collective-permute-start.10 = (bf16[4,48,1536]{2,1,0:T(8,128)(2,1)}, bf16[4,48,1536]{2,1,0:T(8,128)(2,1)S(1)}, u32[]{:S(2)}, u32[]{:S(2)}) collective-permute-start(bf16[4,48,1536]{2,1,0:T(8,128)(2,1)} %copy-done.14), channel_id=1, source_target_pairs={{0,1},{1,0},{2,3},{3,2},{4,5},{5,4},{6,7},{7,6},{8,9},{9,8},{10,11... | collective-permute-start | bytes 1769480 | tf_op jit(solution)/shard_map/ppermute | solution.py:829
  72.8 17.2 %collective-permute-start.15 = (bf16[4,48,1664]{2,1,0:T(8,128)(2,1)S(1)}, bf16[4,48,1664]{2,1,0:T(8,128)(2,1)S(1)}, u32[]{:S(2)}, u32[]{:S(2)}) collective-permute-start(bf16[4,48,1664]{2,1,0:T(8,128)(2,1)S(1)} %collective-permute-done.7.refs_10_.refs_2_.refs_3_), channel_id=1, source_target_pairs={{0,1},{1,0},{2,3},{3,2},{4,5},{5,4},{6,7},{7,6},{8,9},{9,8},{10,11... | collective-permute-start | bytes 1916936 | tf_op jit(solution)/shard_map/ppermute | solution.py:829
  72.8 17.2 %collective-permute-start.14 = (bf16[4,48,1664]{2,1,0:T(8,128)(2,1)S(1)}, bf16[4,48,1664]{2,1,0:T(8,128)(2,1)S(1)}, u32[]{:S(2)}, u32[]{:S(2)}) collective-permute-start(bf16[4,48,1664]{2,1,0:T(8,128)(2,1)S(1)} %collective-permute-done.8.refs_9_.refs_1_.refs_2_), channel_id=1, source_target_pairs={{0,1},{1,0},{2,3},{3,2},{4,5},{5,4},{6,7},{7,6},{8,9},{9,8},{10,11... | collective-permute-start | bytes 1916936 | tf_op jit(solution)/shard_map/ppermute | solution.py:829
  73.3 18.5 %collective-permute-start.13 = (bf16[4,48,1664]{2,1,0:T(8,128)(2,1)S(1)}, bf16[4,48,1664]{2,1,0:T(8,128)(2,1)}, u32[]{:S(2)}, u32[]{:S(2)}) collective-permute-start(bf16[4,48,1664]{2,1,0:T(8,128)(2,1)S(1)} %collective-permute-done.8.refs_9_.refs_1_.refs_2_), channel_id=1, source_target_pairs={{0,4},{4,0},{1,5},{5,1},{2,6},{6,2},{3,7},{7,3},{8,12},{12,8},{9,1... | collective-permute-start | bytes 1916936 | tf_op jit(solution)/shard_map/ppermute | solution.py:829
  74.8 15.2 %collective-permute-start.12 = (bf16[4,48,1536]{2,1,0:T(8,128)(2,1)}, bf16[4,48,1536]{2,1,0:T(8,128)(2,1)S(1)}, u32[]{:S(2)}, u32[]{:S(2)}) collective-permute-start(bf16[4,48,1536]{2,1,0:T(8,128)(2,1)} %collective-permute-done.3.refs_2_), channel_id=1, source_target_pairs={{0,2},{2,0},{1,3},{3,1},{4,6},{6,4},{5,7},{7,5},{8,10},{10,8},{9,1... | collective-permute-start | bytes 1769480 | tf_op jit(solution)/shard_map/ppermute | solution.py:829
  91.8 3.1 %collective-permute-start.17 = (bf16[4,48,1664]{2,1,0:T(8,128)(2,1)}, bf16[4,48,1664]{2,1,0:T(8,128)(2,1)S(1)}, u32[]{:S(2)}, u32[]{:S(2)}) collective-permute-start(bf16[4,48,1664]{2,1,0:T(8,128)(2,1)} %collective-permute-done.13.refs_11_.refs_3_.refs_4_), channel_id=1, source_target_pairs={{0,1},{1,0},{2,3},{3,2},{4,5},{5,4},{6,7},{7,6},{8,9},{9,8},{10,11... | collective-permute-start | bytes 1916936 | tf_op jit(solution)/shard_map/ppermute | solution.py:829
  91.9 3.1 %collective-permute-start.16 = (bf16[4,48,1536]{2,1,0:T(8,128)(2,1)}, bf16[4,48,1536]{2,1,0:T(8,128)(2,1)S(1)}, u32[]{:S(2)}, u32[]{:S(2)}) collective-permute-start(bf16[4,48,1536]{2,1,0:T(8,128)(2,1)} %copy-done.17), channel_id=1, source_target_pairs={{0,1},{1,0},{2,3},{3,2},{4,5},{5,4},{6,7},{7,6},{8,9},{9,8},{10,11... | collective-permute-start | bytes 1769480 | tf_op jit(solution)/shard_map/ppermute | solution.py:829
  95.0 28.2 %collective-permute-start.24 = (bf16[4,96,1536]{2,1,0:T(8,128)(2,1)}, bf16[4,96,1536]{2,1,0:T(8,128)(2,1)S(1)}, u32[]{:S(2)}, u32[]{:S(2)}) collective-permute-start(bf16[4,96,1536]{2,1,0:T(8,128)(2,1)} %all-to-all-done.2.refs_8_), channel_id=1, source_target_pairs={{0,4},{4,0},{1,5},{5,1},{2,6},{6,2},{3,7},{7,3},{8,12},{12,8},{9,1... | collective-permute-start | bytes 3538952 | tf_op jit(solution)/shard_map/ppermute | solution.py:829
  95.6 17.0 %collective-permute-start.22 = (bf16[160,768]{1,0:T(8,128)(2,1)}, bf16[160,768]{1,0:T(8,128)(2,1)S(1)}, u32[]{:S(2)}, u32[]{:S(2)}) collective-permute-start(bf16[160,768]{1,0:T(8,128)(2,1)} %get-tuple-element.200.refs_4_.grad_slot), channel_id=1, source_target_pairs={{0,2},{2,0},{1,3},{3,1},{4,6},{6,4},{5,7},{7,5},{8,10},{10,8},{9,1... | collective-permute-start | bytes 737288 | tf_op jit(solution)/shard_map/ppermute | solution.py:829
  96.2 16.7 %collective-permute-start.21 = (bf16[160,768]{1,0:T(8,128)(2,1)}, bf16[160,768]{1,0:T(8,128)(2,1)}, u32[]{:S(2)}, u32[]{:S(2)}) collective-permute-start(bf16[160,768]{1,0:T(8,128)(2,1)} %get-tuple-element.200.refs_4_.grad_slot), channel_id=1, source_target_pairs={{0,1},{1,0},{2,3},{3,2},{4,5},{5,4},{6,7},{7,6},{8,9},{9,8},{10,11... | collective-permute-start | bytes 737288 | tf_op jit(solution)/shard_map/ppermute | solution.py:829
  110.9 8.6 %collective-permute-start.19 = (bf16[160,768]{1,0:T(8,128)(2,1)}, bf16[160,768]{1,0:T(8,128)(2,1)S(1)}, u32[]{:S(2)}, u32[]{:S(2)}) collective-permute-start(bf16[160,768]{1,0:T(8,128)(2,1)} %get-tuple-element.199.refs_0_), channel_id=1, source_target_pairs={{0,2},{2,0},{1,3},{3,1},{4,6},{6,4},{5,7},{7,5},{8,10},{10,8},{9,1... | collective-permute-start | bytes 737288 | tf_op jit(solution)/shard_map/ppermute | solution.py:829
  112.4 29.8 %collective-permute-start.28 = (bf16[160,3072]{1,0:T(8,128)(2,1)}, bf16[160,3072]{1,0:T(8,128)(2,1)S(1)}, u32[]{:S(2)}, u32[]{:S(2)}) collective-permute-start(bf16[160,3072]{1,0:T(8,128)(2,1)} %get-tuple-element.208.refs_0_), channel_id=1, source_target_pairs={{0,1},{1,0},{2,3},{3,2},{4,5},{5,4},{6,7},{7,6},{8,9},{9,8},{10,11... | collective-permute-start | bytes 2949128 | tf_op jit(solution)/shard_map/ppermute | solution.py:829
  112.6 6.9 %collective-permute-start.23 = (bf16[160,768]{1,0:T(8,128)(2,1)S(1)}, bf16[160,768]{1,0:T(8,128)(2,1)S(1)}, u32[]{:S(2)}, u32[]{:S(2)}) collective-permute-start(bf16[160,768]{1,0:T(8,128)(2,1)S(1)} %collective-permute-done.22.refs_6_), channel_id=1, source_target_pairs={{0,1},{1,0},{2,3},{3,2},{4,5},{5,4},{6,7},{7,6},{8,9},{9,8},{10,11... | collective-permute-start | bytes 737288 | tf_op jit(solution)/shard_map/ppermute | solution.py:829
  112.9 6.6 %collective-permute-start.18 = (bf16[160,768]{1,0:T(8,128)(2,1)}, bf16[160,768]{1,0:T(8,128)(2,1)S(1)}, u32[]{:S(2)}, u32[]{:S(2)}) collective-permute-start(bf16[160,768]{1,0:T(8,128)(2,1)} %get-tuple-element.199.refs_0_), channel_id=1, source_target_pairs={{0,1},{1,0},{2,3},{3,2},{4,5},{5,4},{6,7},{7,6},{8,9},{9,8},{10,11... | collective-permute-start | bytes 737288 | tf_op jit(solution)/shard_map/ppermute | solution.py:829
  133.1 9.1 %collective-permute-start.27 = (bf16[160,768]{1,0:T(8,128)(2,1)}, bf16[160,768]{1,0:T(8,128)(2,1)S(1)}, u32[]{:S(2)}, u32[]{:S(2)}) collective-permute-start(bf16[160,768]{1,0:T(8,128)(2,1)} %get-tuple-element.205), channel_id=1, source_target_pairs={{0,1},{1,0},{2,3},{3,2},{4,5},{5,4},{6,7},{7,6},{8,9},{9,8},{10,11... | collective-permute-start | bytes 737288 | tf_op jit(solution)/shard_map/ppermute | solution.py:829
  135.8 8.1 %collective-permute-start.26 = (bf16[160,768]{1,0:T(8,128)(2,1)S(1)}, bf16[160,768]{1,0:T(8,128)(2,1)S(1)}, u32[]{:S(2)}, u32[]{:S(2)}) collective-permute-start(bf16[160,768]{1,0:T(8,128)(2,1)S(1)} %combine_kernel.2), channel_id=1, source_target_pairs={{0,2},{2,0},{1,3},{3,1},{4,6},{6,4},{5,7},{7,5},{8,10},{10,8},{9,1... | collective-permute-start | bytes 737288 | tf_op jit(solution)/shard_map/ppermute | solution.py:829
  144.6 93.7 %all-to-all-start.3 = ((bf16[8,96,1536]{2,1,0:T(8,128)(2,1)}), bf16[8,96,1536]{2,1,0:T(8,128)(2,1)S(1)}, u32[]{:S(2)}, u32[]{:S(2)}) async-start(bf16[8,96,1536]{2,1,0:T(8,128)(2,1)} %bitcast.49), calls=%async_computation.3 | async-start | bytes 4718592 | tf_op jit(solution)/shard_map/all_to_all | solution.py:833
  149.9 12.0 %collective-permute-start.30 = (bf16[160,768]{1,0:T(8,128)(2,1)}, bf16[160,768]{1,0:T(8,128)(2,1)S(1)}, u32[]{:S(2)}, u32[]{:S(2)}) collective-permute-start(bf16[160,768]{1,0:T(8,128)(2,1)} %get-tuple-element.223), channel_id=1, source_target_pairs={{0,1},{1,0},{2,3},{3,2},{4,5},{5,4},{6,7},{7,6},{8,9},{9,8},{10,11... | collective-permute-start | bytes 737288 | tf_op jit(solution)/shard_map/ppermute | solution.py:829
  161.9 9.6 %collective-permute-start.32 = (bf16[1024,768]{1,0:T(8,128)(2,1)}, bf16[1024,768]{1,0:T(8,128)(2,1)S(1)}, u32[]{:S(2)}, u32[]{:S(2)}) collective-permute-start(bf16[1024,768]{1,0:T(8,128)(2,1)} %get-tuple-element.280.kv_send), channel_id=1, source_target_pairs={{0,1},{1,0},{2,3},{3,2},{4,5},{5,4},{6,7},{7,6},{8,9},{9,8},{10,11... | collective-permute-start | bytes 4718600 | tf_op jit(solution)/shard_map/ppermute | solution.py:829
  162.4 9.0 %collective-permute-start.31 = (bf16[160,1152]{1,0:T(8,128)(2,1)}, bf16[160,1152]{1,0:T(8,128)(2,1)S(1)}, u32[]{:S(2)}, u32[]{:S(2)}) collective-permute-start(bf16[160,1152]{1,0:T(8,128)(2,1)} %get-tuple-element.230), channel_id=1, source_target_pairs={{0,1},{1,0},{2,3},{3,2},{4,5},{5,4},{6,7},{7,6},{8,9},{9,8},{10,11... | collective-permute-start | bytes 1105928 | tf_op jit(solution)/shard_map/ppermute | solution.py:829
  162.5 8.9 %collective-permute-start.33 = (bf16[160,768]{1,0:T(8,128)(2,1)S(1)}, bf16[160,768]{1,0:T(8,128)(2,1)S(1)}, u32[]{:S(2)}, u32[]{:S(2)}) collective-permute-start(bf16[160,768]{1,0:T(8,128)(2,1)S(1)} %combine_kernel.3), channel_id=1, source_target_pairs={{0,2},{2,0},{1,3},{3,1},{4,6},{6,4},{5,7},{7,5},{8,10},{10,8},{9,1... | collective-permute-start | bytes 737288 | tf_op jit(solution)/shard_map/ppermute | solution.py:829
  171.5 11.0 %collective-permute-start.34 = (bf16[160,1152]{1,0:T(8,128)(2,1)}, bf16[160,1152]{1,0:T(8,128)(2,1)S(1)}, u32[]{:S(2)}, u32[]{:S(2)}) collective-permute-start(bf16[160,1152]{1,0:T(8,128)(2,1)} %get-tuple-element.247), channel_id=1, source_target_pairs={{0,1},{1,0},{2,3},{3,2},{4,5},{5,4},{6,7},{7,6},{8,9},{9,8},{10,11... | collective-permute-start | bytes 1105928 | tf_op jit(solution)/shard_map/ppermute | solution.py:829
  182.5 35.0 %collective-permute-start.35 = (bf16[2,4,48,1152]{3,2,1,0:T(8,128)(2,1)}, bf16[2,4,48,1152]{3,2,1,0:T(8,128)(2,1)S(1)}, u32[]{:S(2)}, u32[]{:S(2)}) collective-permute-start(bf16[2,4,48,1152]{3,2,1,0:T(8,128)(2,1)} %get-tuple-element.258), channel_id=1, source_target_pairs={{0,4},{4,0},{1,5},{5,1},{2,6},{6,2},{3,7},{7,3},{8,12},{12,8},{9,1... | collective-permute-start | bytes 2654216 | tf_op jit(solution)/shard_map/ppermute | solution.py:829
  189.4 28.0 %collective-permute-start.37 = (bf16[2,4,48,768]{3,2,1,0:T(8,128)(2,1)}, bf16[2,4,48,768]{3,2,1,0:T(8,128)(2,1)S(1)}, u32[]{:S(2)}, u32[]{:S(2)}) collective-permute-start(bf16[2,4,48,768]{3,2,1,0:T(8,128)(2,1)} %get-tuple-element.260), channel_id=1, source_target_pairs={{0,2},{2,0},{1,3},{3,1},{4,6},{6,4},{5,7},{7,5},{8,10},{10,8},{9,1... | collective-permute-start | bytes 1769480 | tf_op jit(solution)/shard_map/ppermute | solution.py:829
  190.9 26.6 %collective-permute-start.36 = (bf16[2,4,48,768]{3,2,1,0:T(8,128)(2,1)S(1)}, bf16[2,4,48,768]{3,2,1,0:T(8,128)(2,1)S(1)}, u32[]{:S(2)}, u32[]{:S(2)}) collective-permute-start(bf16[2,4,48,768]{3,2,1,0:T(8,128)(2,1)S(1)} %copy-done.50), channel_id=1, source_target_pairs={{0,2},{2,0},{1,3},{3,1},{4,6},{6,4},{5,7},{7,5},{8,10},{10,8},{9,1... | collective-permute-start | bytes 1769480 | tf_op jit(solution)/shard_map/ppermute | solution.py:829
  191.5 25.9 %collective-permute-start.38 = (bf16[2,4,48,512]{3,2,1,0:T(8,128)(2,1)}, bf16[2,4,48,512]{3,2,1,0:T(8,128)(2,1)S(1)}, u32[]{:S(2)}, u32[]{:S(2)}) collective-permute-start(bf16[2,4,48,512]{3,2,1,0:T(8,128)(2,1)} %get-tuple-element.261), channel_id=1, source_target_pairs={{0,4},{4,0},{1,5},{5,1},{2,6},{6,2},{3,7},{7,3},{8,12},{12,8},{9,1... | collective-permute-start | bytes 1179656 | tf_op jit(solution)/shard_map/ppermute | solution.py:829
  221.5 16.8 %collective-permute-start.39 = (bf16[4,48,1152]{2,1,0:T(8,128)(2,1)}, bf16[4,48,1152]{2,1,0:T(8,128)(2,1)S(1)}, u32[]{:S(2)}, u32[]{:S(2)}) collective-permute-start(bf16[4,48,1152]{2,1,0:T(8,128)(2,1)} %get-tuple-element.270), channel_id=1, source_target_pairs={{0,2},{2,0},{1,3},{3,1},{4,6},{6,4},{5,7},{7,5},{8,10},{10,8},{9,1... | collective-permute-start | bytes 1327112 | tf_op jit(solution)/shard_map/ppermute | solution.py:829
  223.2 14.2 %collective-permute-start.40 = (bf16[4,48,768]{2,1,0:T(8,128)(2,1)}, bf16[4,48,768]{2,1,0:T(8,128)(2,1)S(1)}, u32[]{:S(2)}, u32[]{:S(2)}) collective-permute-start(bf16[4,48,768]{2,1,0:T(8,128)(2,1)} %get-tuple-element.271), channel_id=1, source_target_pairs={{0,4},{4,0},{1,5},{5,1},{2,6},{6,2},{3,7},{7,3},{8,12},{12,8},{9,1... | collective-permute-start | bytes 884744 | tf_op jit(solution)/shard_map/ppermute | solution.py:829
  225.5 12.8 %collective-permute-start.41 = (bf16[4,48,768]{2,1,0:T(8,128)(2,1)}, bf16[4,48,768]{2,1,0:T(8,128)(2,1)S(1)}, u32[]{:S(2)}, u32[]{:S(2)}) collective-permute-start(bf16[4,48,768]{2,1,0:T(8,128)(2,1)} %get-tuple-element.272), channel_id=1, source_target_pairs={{0,4},{4,0},{1,5},{5,1},{2,6},{6,2},{3,7},{7,3},{8,12},{12,8},{9,1... | collective-permute-start | bytes 884744 | tf_op jit(solution)/shard_map/ppermute | solution.py:829
  225.6 11.8 %collective-permute-start.42 = (bf16[4,48,512]{2,1,0:T(8,128)(2,1)}, bf16[4,48,512]{2,1,0:T(8,128)(2,1)S(1)}, u32[]{:S(2)}, u32[]{:S(2)}) collective-permute-start(bf16[4,48,512]{2,1,0:T(8,128)(2,1)} %get-tuple-element.273), channel_id=1, source_target_pairs={{0,2},{2,0},{1,3},{3,1},{4,6},{6,4},{5,7},{7,5},{8,10},{10,8},{9,1... | collective-permute-start | bytes 589832 | tf_op jit(solution)/shard_map/ppermute | solution.py:829
  243.5 36.4 %all-to-all-start.4 = ((bf16[8,24,3200]{2,1,0:T(8,128)(2,1)}), bf16[8,24,3200]{2,1,0:T(8,128)(2,1)S(1)}, u32[]{:S(2)}, u32[]{:S(2)}) async-start(bf16[8,24,3200]{2,1,0:T(8,128)(2,1)} %bitcast.57), calls=%async_computation.4 | async-start | bytes 2457600 | tf_op jit(solution)/shard_map/all_to_all | solution.py:833
  249.5 8.8 %collective-permute-start.43 = (bf16[2,40,1536]{2,1,0:T(8,128)(2,1)S(1)}, bf16[2,40,1536]{2,1,0:T(8,128)(2,1)S(1)}, u32[]{:S(2)}, u32[]{:S(2)}) collective-permute-start(bf16[2,40,1536]{2,1,0:T(8,128)(2,1)S(1)} %copy-done.51), channel_id=1, source_target_pairs={{0,2},{2,0},{1,3},{3,1},{4,6},{6,4},{5,7},{7,5},{8,10},{10,8},{9,1... | collective-permute-start | bytes 737288 | tf_op jit(solution)/shard_map/ppermute | solution.py:829
  250.9 20.7 %collective-permute-start.44 = (bf16[40,1536]{1,0:T(8,128)(2,1)S(1)}, bf16[40,1536]{1,0:T(8,128)(2,1)S(1)}, u32[]{:S(2)}, u32[]{:S(2)}) collective-permute-start(bf16[40,1536]{1,0:T(8,128)(2,1)S(1)} %copy-done.53), channel_id=1, source_target_pairs={{0,1},{1,0},{2,3},{3,2},{4,5},{5,4},{6,7},{7,6},{8,9},{9,8},{10,11... | collective-permute-start | bytes 368648 | tf_op jit(solution)/shard_map/ppermute | solution.py:829
  253.9 14.5 %collective-permute-start.47 = (bf16[24,1536]{1,0:T(8,128)(2,1)}, bf16[24,1536]{1,0:T(8,128)(2,1)S(1)}, u32[]{:S(2)}, u32[]{:S(2)}) collective-permute-start(bf16[24,1536]{1,0:T(8,128)(2,1)} %get-tuple-element.293), channel_id=1, source_target_pairs={{0,1},{1,0},{2,3},{3,2},{4,5},{5,4},{6,7},{7,6},{8,9},{9,8},{10,11... | collective-permute-start | bytes 221192 | tf_op jit(solution)/shard_map/ppermute | solution.py:829
  254.3 6.7 %collective-permute-start.46 = (bf16[2,24,1536]{2,1,0:T(8,128)(2,1)}, bf16[2,24,1536]{2,1,0:T(8,128)(2,1)S(1)}, u32[]{:S(2)}, u32[]{:S(2)}) collective-permute-start(bf16[2,24,1536]{2,1,0:T(8,128)(2,1)} %get-tuple-element.292), channel_id=1, source_target_pairs={{0,2},{2,0},{1,3},{3,1},{4,6},{6,4},{5,7},{7,5},{8,10},{10,8},{9,1... | collective-permute-start | bytes 442376 | tf_op jit(solution)/shard_map/ppermute | solution.py:829
  258.3 13.3 %collective-permute-start.45 = (bf16[40,1536]{1,0:T(8,128)(2,1)S(1)}, bf16[40,1536]{1,0:T(8,128)(2,1)S(1)}, u32[]{:S(2)}, u32[]{:S(2)}) collective-permute-start(bf16[40,1536]{1,0:T(8,128)(2,1)S(1)} %slice_bitcast_fusion.1), channel_id=1, source_target_pairs={{0,1},{1,0},{2,3},{3,2},{4,5},{5,4},{6,7},{7,6},{8,9},{9,8},{10,11... | collective-permute-start | bytes 368648 | tf_op jit(solution)/shard_map/ppermute | solution.py:829
  261.0 7.5 %collective-permute-start.48 = (bf16[24,1536]{1,0:T(8,128)(2,1)S(1)}, bf16[24,1536]{1,0:T(8,128)(2,1)S(1)}, u32[]{:S(2)}, u32[]{:S(2)}) collective-permute-start(bf16[24,1536]{1,0:T(8,128)(2,1)S(1)} %slice_bitcast_fusion.2), channel_id=1, source_target_pairs={{0,1},{1,0},{2,3},{3,2},{4,5},{5,4},{6,7},{7,6},{8,9},{9,8},{10,11... | collective-permute-start | bytes 221192 | tf_op jit(solution)/shard_map/ppermute | solution.py:829
  (60 other events, 388.8 us)
where the time goes:
time: 285 us; the launch traced here: 282 us
  waiting for transfers between devices  107 us (38%)
  Pallas kernels  102 us (36%)
  starting transfers between devices  57.1 us (20%)
  local copies, waits for them, and re-layouts  13.8 us (5%)
    ppermute x49, waiting for transfers between devices, flip(): return lax.ppermute(value, axis, [(0, 1), (1, 0)])  101 us
    pallas_call x20, Pallas kernels, run(): pl.pallas_call(kernel, out_shape=[jax.ShapeDtypeStruct(s, t) for s, t in...  94.6 us
    ppermute x49, starting transfers between devices, flip(): return lax.ppermute(value, axis, [(0, 1), (1, 0)])  30.2 us
    all_to_all x5, starting transfers between devices, swap_all(): return lax.all_to_all(value, axes, split_axis=0, concat_axis=0, tiled=True)  26.9 us
    unnamed x108, local copies, waits for them, and re-layouts  12.6 us
    pallas_call x2, Pallas kernels, add_up(): pl.pallas_call(functools.partial(add_kernel, [len(terms) for terms in sum...  7.03 us
    all_to_all x5, waiting for transfers between devices, swap_all(): return lax.all_to_all(value, axes, split_axis=0, concat_axis=0, tiled=True)  6.41 us
  transfers between devices with their start and end apart: 54, of which 25 were waited for; matrix products, arithmetic and copies ran while one was open for 0% of the time, Pallas kernels for 34%

commit v1 on v0

--- a/solution.py
+++ b/solution.py
@@ -692,23 +692,14 @@
         blocks[owner * height : owner * height + 3, :] = value
 
 
-def self_grad_kernel(share, me, small, *refs):
-    sources, targets, landed, made, grads, sems = (
-        refs[:4], refs[4:8], refs[8:12], refs[12:16], refs[16], refs[17],
-    )
-    fetch = Fetch(sems)
-    sources = [sources[0].at[:, pl.ds(0, D)], sources[1].at[:, pl.ds(0, D)], *sources[2:]]
-    copies = [fetch.start(source, target) for source, target in zip(sources, landed)]
-    own, far, half, half_far = landed
-    wait(copies)
-    half_grads([(own[...], far[...], half[:, :D], half_far[:, :D])], me, made[:2], grads, "y")
-    sent = [fetch.start(made[n], targets[n]) for n in (1, 0)]
-    half_grads([(own[...], far[...], half[:, D:], half_far[:, D:])], me, made[2:], grads, "x")
+def self_grad_kernel(share, me, saved, saved_far, half, half_far, small, *refs):
+    first, second, grads = refs[:2], refs[2:4], refs[4]
+    own, far = saved[:, :D], saved_far[:, :D]
+    half_grads([(own, far, half[:, :D], half_far[:, :D])], me, first, grads, "y")
+    half_grads([(own, far, half[:, D:], half_far[:, D:])], me, second, grads, "x")
     blocks = grads.at[:, :LANES]
     owner_rows(small, blocks, share)
-    put_quadrants(blocks, me, made[2:], HALF, "x")
-    sent += [fetch.start(made[n], targets[n]) for n in (3, 2)]
-    wait(sent)
+    put_quadrants(blocks, me, second, HALF, "x")
 
 
 def unpack_kernel(got, *outs):
@@ -914,11 +905,11 @@
     bx, by, ax, ax_far, ay_far, b_far = tie(bx, by, ax, ax_far, ay_far, b_far)
     axy, byx = flip(ax, "y"), flip(by, "x")
     by_far, bx_far = flip(by, "c"), flip(bx, "c")
-    axy, byx, by_far, bx_far, hidden = tie(axy, byx, by_far, bx_far, hidden)
+    axy, byx, by_far, bx_far = tie(axy, byx, by_far, bx_far)
     pieces_a = (a, ay, ax, axy, a_far, ay_far, ax_far, flip(axy, "c"))
     pieces_b = (b, by, bx, byx, b_far, by_far, bx_far, flip(byx, "c"))
-    hidden, pieces_a, pieces_b = tie(hidden, pieces_a, pieces_b)
     hidden_far = flip(hidden, "x")
+    pieces_a, pieces_b = tie(pieces_a, pieces_b)
     grad_slots = group_rows(grad_slot)
 
     weight_shape = lambda n: vmem((depth, 2, 2, 2 * height, n * D), BF)
@@ -1087,13 +1078,9 @@
     q_0, q_1, v_0, v_1 = run(
         functools.partial(self_grad_kernel, share),
         [block(D)] * 2 + [block(HALF + LANES)] * 2,
-        [SM, VM] + [HB] * 4,
-        [vmem((rows, D), BF)] * 2
-        + [vmem((rows, 3 * HALF), BF)] * 2
-        + [vmem(block(n)[0], BF) for n in (D, D, HALF + LANES, HALF + LANES)]
-        + [vmem((D, D), F32), sems(8)],
-        me, small, saved, saved_far, self_keep, self_far,
-        copied=4,
+        [SM] + [VM] * 5,
+        [vmem((D, D), F32)],
+        me, saved, saved_far, self_keep, self_far, small,
     )
     q_0, q_1, v_0, v_1, grad_rows = tie(q_0, q_1, v_0, v_1, grad_rows)
     q_1, v_1 = flip(q_1, "y"), flip(v_1, "x")

time: 285 us -> 282 us (0.989)
  waiting for transfers between devices: 107 us -> 104 us
    ppermute x49, waiting for transfers between devices: 101 us -> 90.1 us  [flip(): return lax.ppermute(value, axis, [(0, 1), (1, 0)])]
    all_to_all x5, waiting for transfers between devices: 6.41 us -> 14.4 us  [swap_all(): return lax.all_to_all(value, axes, split_axis=0, concat_axis=0, tiled=True)]
    unnamed x108 -> x102, local copies, waits for them, and re-layouts: 12.6 us -> 11.7 us
where the time goes in v1:
time: 282 us; the launch traced here: 279 us
  waiting for transfers between devices  104 us (37%)
  Pallas kernels  101 us (36%)
  starting transfers between devices  58 us (21%)
  local copies, waits for them, and re-layouts  12.9 us (5%)
    pallas_call x20, Pallas kernels, run(): pl.pallas_call(kernel, out_shape=[jax.ShapeDtypeStruct(s, t) for s, t in...  94 us
    ppermute x49, waiting for transfers between devices, flip(): return lax.ppermute(value, axis, [(0, 1), (1, 0)])  90.1 us
    ppermute x49, starting transfers between devices, flip(): return lax.ppermute(value, axis, [(0, 1), (1, 0)])  30.1 us
    all_to_all x5, starting transfers between devices, swap_all(): return lax.all_to_all(value, axes, split_axis=0, concat_axis=0, tiled=True)  27.9 us
    all_to_all x5, waiting for transfers between devices, swap_all(): return lax.all_to_all(value, axes, split_axis=0, concat_axis=0, tiled=True)  14.4 us
    unnamed x102, local copies, waits for them, and re-layouts  11.7 us
    pallas_call x2, Pallas kernels, add_up(): pl.pallas_call(functools.partial(add_kernel, [len(terms) for terms in sum...  7.01 us
  transfers between devices with their start and end apart: 54, of which 25 were waited for; matrix products, arithmetic and copies ran while one was open for 0% of the time, Pallas kernels for 34%

profile of v1, /device:TPU:0, one launch (start us, length us, event | category | flops | bytes accessed | tf_op | source)
XLA Modules:
  0.0 278.7 jit_solution(9867424383169253568)
XLA Ops:
  0.7 1.8 pack_self_kernel.1
  2.5 6.3 %all-to-all-start = ((bf16[8,24,1536]{2,1,0:T(8,128)(2,1)}), bf16[8,24,1536]{2,1,0:T(8,128)(2,1)S(1)}, u32[]{:S(2)}, u32[]{:S(2)}) async-start(bf16[8,24,1536]{2,1,0:T(8,128)(2,1)} %bitcast.59), calls=%async_computation | async-start | bytes 1179648 | tf_op jit(solution)/shard_map/all_to_all | solution.py:824
  9.5 2.9 %pack_group_kernel.1 = (bf16[80,1536]{1,0:T(8,128)(2,1)}, bf16[80,1536]{1,0:T(8,128)(2,1)}, bf16[2,80,1536]{2,1,0:T(8,128)(2,1)}) custom-call(s32[1,4]{1,0:T(1,128)} %add_bitcast_fusion.me.refs_0_, bf16[576,128]{1,0:T(8,128)(2,1)} %bitcast.64, bf16[576,128]{1,0:T(8,128)(2,1)} %bitcast.65, bf16[4,40,768]{2,1,0:T(8,128)(2,1)} %bitcast.62, ...), custom_call_target="tpu_custom_call" | custom-call | tf_op jit(solution)/shard_map/pack_group_kernel/pallas_call | solution.py:783
  12.4 1.5 collective-permute-start
  14.5 3.2 %transpose_kernel.1.refs_4_ = bf16[768,1024]{1,0:T(8,128)(2,1)} custom-call(bf16[1024,768]{1,0:T(8,128)(2,1)} %bitcast.50), custom_call_target="tpu_custom_call" | custom-call | tf_op jit(solution)/shard_map/transpose_kernel/pallas_call | solution.py:783
  17.6 1.9 pack_cross_kernel.1
  19.5 6.7 %collective-permute-done.chip = bf16[2,80,1536]{2,1,0:T(8,128)(2,1)S(1)} collective-permute-done((bf16[2,80,1536]{2,1,0:T(8,128)(2,1)}, bf16[2,80,1536]{2,1,0:T(8,128)(2,1)S(1)}, u32[]{:S(2)}, u32[]{:S(2)}) %collective-permute-start) | collective-permute-done | bytes 491552 | tf_op jit(solution)/shard_map/ppermute | solution.py:820
  26.3 4.8 %all-to-all-start.1 = ((bf16[8,24,1664]{2,1,0:T(8,128)(2,1)}), bf16[8,24,1664]{2,1,0:T(8,128)(2,1)S(1)}, u32[]{:S(2)}, u32[]{:S(2)}) async-start(bf16[8,24,1664]{2,1,0:T(8,128)(2,1)} %bitcast.58), calls=%async_computation.1 | async-start | bytes 1277952 | tf_op jit(solution)/shard_map/all_to_all | solution.py:824
  31.7 1.5 collective-permute-start.4
  33.2 1.5 collective-permute-start.3
  34.8 1.5 collective-permute-done.2.both
  38.5 2.9 %spread_kernel.1 = (bf16[4,4,24,1536]{3,2,1,0:T(8,128)(2,1)}, bf16[160,768]{1,0:T(8,128)(2,1)}, bf16[160,768]{1,0:T(8,128)(2,1)}) custom-call(s32[1,4]{1,0:T(1,128)} %add_bitcast_fusion.me.refs_0_, s32[1,160]{1,0:T(1,128)} %arr.3, bf16[80,1536]{1,0:T(8,128)(2,1)} %get-tuple-element.152.near, bf16[2,80,1536]{2,1,0:T(8,128)(2,1)} %copy-done.22, ...), custom_call_target="tpu_custom_call" | custom-call | tf_op jit(solution)/shard_map/spread_kernel/pallas_call | solution.py:783
  41.4 5.5 %collective-permute-done.4.refs_1_ = bf16[4,48,1536]{2,1,0:T(8,128)(2,1)S(1)} collective-permute-done((bf16[4,48,1536]{2,1,0:T(8,128)(2,1)S(1)}, bf16[4,48,1536]{2,1,0:T(8,128)(2,1)S(1)}, u32[]{:S(2)}, u32[]{:S(2)}) %collective-permute-start.4) | collective-permute-done | bytes 589856 | tf_op jit(solution)/shard_map/ppermute | solution.py:820
  50.2 4.5 %all-to-all-start.2 = ((bf16[4,96,1536]{2,1,0:T(8,128)(2,1)}), bf16[4,96,1536]{2,1,0:T(8,128)(2,1)}, u32[]{:S(2)}, u32[]{:S(2)}) async-start(bf16[4,96,1536]{2,1,0:T(8,128)(2,1)} %bitcast.61), calls=%async_computation.2 | async-start | bytes 2359296 | tf_op jit(solution)/shard_map/all_to_all | solution.py:824
  56.3 1.5 collective-permute-start.7
  58.3 1.7 collective-permute-done.10.refs_5_
  60.8 10.8 %collective-permute-done.8.refs_9_.refs_1_.refs_2_ = bf16[4,48,1664]{2,1,0:T(8,128)(2,1)S(1)} collective-permute-done((bf16[4,48,1664]{2,1,0:T(8,128)(2,1)S(1)}, bf16[4,48,1664]{2,1,0:T(8,128)(2,1)S(1)}, u32[]{:S(2)}, u32[]{:S(2)}) %collective-permute-start.8) | collective-permute-done | bytes 639008 | tf_op jit(solution)/shard_map/ppermute | solution.py:820
  73.3 1.5 collective-permute-start.13
  75.4 7.9 %all-to-all-done.2.refs_8_ = bf16[4,96,1536]{2,1,0:T(8,128)(2,1)} async-done(((bf16[4,96,1536]{2,1,0:T(8,128)(2,1)}), bf16[4,96,1536]{2,1,0:T(8,128)(2,1)}, u32[]{:S(2)}, u32[]{:S(2)}) %all-to-all-start.2) | async-done | bytes 1179680 | tf_op jit(solution)/shard_map/all_to_all | solution.py:824
  84.8 5.3 %collective-permute-done.12.refs_3_ = bf16[4,48,1536]{2,1,0:T(8,128)(2,1)} collective-permute-done((bf16[4,48,1536]{2,1,0:T(8,128)(2,1)}, bf16[4,48,1536]{2,1,0:T(8,128)(2,1)}, u32[]{:S(2)}, u32[]{:S(2)}) %collective-permute-start.12) | collective-permute-done | bytes 589856 | tf_op jit(solution)/shard_map/ppermute | solution.py:820
  91.7 2.0 collective-permute-done.16.refs_7_
  94.8 14.6 %forward_kernel.1 = (f32[11,768]{1,0:T(8,128)}, bf16[160,2304]{1,0:T(8,128)(2,1)}, bf16[3,640,160]{2,1,0:T(8,128)(2,1)}, bf16[160,3072]{1,0:T(8,128)(2,1)}, f32[...) custom-call(s32[1,4]{1,0:T(1,128)} %lens.3, ...), custom_call_target="tpu_custom_call" | custom-call | tf_op jit(solution)/shard_map/forward_kernel/pallas_call | solution.py:783
  110.6 7.0 %collective-permute-done.19.refs_2_ = bf16[160,768]{1,0:T(8,128)(2,1)S(1)} collective-permute-done((bf16[160,768]{1,0:T(8,128)(2,1)}, bf16[160,768]{1,0:T(8,128)(2,1)S(1)}, u32[]{:S(2)}, u32[]{:S(2)}) %collective-permute-start.19) | collective-permute-done | bytes 245792 | tf_op jit(solution)/shard_map/ppermute | solution.py:820
  120.2 8.8 %mlp_kernel.1 = (f32[160,768]{1,0:T(8,128)}, bf16[160,768]{1,0:T(8,128)(2,1)}, bf16[160,768]{1,0:T(8,128)(2,1)}, bf16[160,768]{1,0:T(8,128)(2,1)}, f32[160,768]{...) custom-call(s32[1,4]{1,0:T(1,128)} %add_bitcast_fusion.me.refs_0_, ...), custom_call_target="tpu_custom_call" | custom-call | tf_op jit(solution)/shard_map/mlp_kernel/pallas_call | solution.py:783
  132.5 5.7 %hidden_grad_kernel.1 = bf16[768,1536]{1,0:T(8,128)(2,1)} custom-call(bf16[160,768]{1,0:T(8,128)(2,1)} %get-tuple-element.195.refs_0_, bf16[160,768]{1,0:T(8,128)(2,1)} %copy-done.26, bf16[160,768]{1,0:T(8,128)(2,1)} %copy-done.24, bf16[160,768]{1,0:T(8,128)(2,1)} %copy-done.27, bf16[160,768]{1,0:T(8,128)(2,1)} %get-tuple-element.196.refs_4_.grad_slot, ...), custom_call_target="tpu_custom_call" | custom-call | tf_op jit(solution)/shard_map/hidden_grad_kernel/pallas_call | solution.py:783
  138.2 1.7 collective-permute-done.26.grad_far
  140.6 6.2 %all-to-all-start.3 = ((bf16[8,96,1536]{2,1,0:T(8,128)(2,1)}), bf16[8,96,1536]{2,1,0:T(8,128)(2,1)S(1)}, u32[]{:S(2)}, u32[]{:S(2)}) async-start(bf16[8,96,1536]{2,1,0:T(8,128)(2,1)} %bitcast.49), calls=%async_computation.3 | async-start | bytes 4718592 | tf_op jit(solution)/shard_map/all_to_all | solution.py:824
  146.8 11.9 %cross_back_kernel.1 = (f32[160,768]{1,0:T(8,128)}, f32[66,128]{1,0:T(8,128)}, bf16[160,1152]{1,0:T(8,128)(2,1)}, bf16[160,1152]{1,0:T(8,128)(2,1)}, bf16[1024,7...) custom-call(s32[1,4]{1,0:T(1,128)} %lens.3, s32[1,4]{1,0:T(1,128)} %add_bitcast_fusion.me.refs_0_, ...), custom_call_target="tpu_custom_call" | custom-call | tf_op jit(solution)/shard_map/cross_back_kernel/pallas_call | solution.py:783
  160.1 8.2 %self_back_kernel.1 = (bf16[160,768]{1,0:T(8,128)(2,1)}, f32[66,128]{1,0:T(8,128)}, bf16[160,1152]{1,0:T(8,128)(2,1)}, bf16[160,1152]{1,0:T(8,128)(2,1)}) custom-call(s32[1,4]{1,0:T(1,128)} %add_bitcast_fusion.me.refs_0_, f32[160,768]{1,0:T(8,128)} %get-tuple-element.220.grad_state, bf16[3,640,160]{2,1,0:T(8,128)(2,1)} %get-tuple-element.221.probs, ...), custom_call_target="tpu_custom_call" | custom-call | tf_op jit(solution)/shard_map/self_back_kernel/pallas_call | solution.py:783
  169.6 9.8 %cross_grad_kernel.1 = (bf16[2,4,48,1152]{3,2,1,0:T(8,128)(2,1)}, bf16[2,4,48,1152]{3,2,1,0:T(8,128)(2,1)}, bf16[2,4,48,768]{3,2,1,0:T(8,128)(2,1)}, bf16[2,4,48,768]{3,2,1,0:T(8,128)(2,1)}) custom-call(s32[1,4]{1,0:T(1,128)} %add_bitcast_fusion.me.refs_0_, bf16[160,3072]{1,0:T(8,128)(2,1)} %get-tuple-element.204.refs_0_.saved, bf16[160,3072]{1,0:T(8,128)(2,1)} %copy-done.9, ...), custom_call_target="tpu_custom_call" | custom-call | tf_op jit(solution)/shard_map/cross_grad_kernel/pallas_call | solution.py:783
  179.4 2.1 collective-permute-start.35
  181.5 4.2 %self_grad_kernel.1 = (bf16[2,4,48,768]{3,2,1,0:T(8,128)(2,1)}, bf16[2,4,48,768]{3,2,1,0:T(8,128)(2,1)}, bf16[2,4,48,512]{3,2,1,0:T(8,128)(2,1)}, bf16[2,4,48,512]{3,2,1,0:T(8,128)(2,1)}) custom-call(s32[1,4]{1,0:T(1,128)} %add_bitcast_fusion.me.refs_0_, bf16[160,3072]{1,0:T(8,128)(2,1)} %get-tuple-element.204.refs_0_.saved, bf16[160,3072]{1,0:T(8,128)(2,1)} %copy-done.9, ...), custom_call_target="tpu_custom_call" | custom-call | tf_op jit(solution)/shard_map/self_grad_kernel/pallas_call | solution.py:783
  188.4 1.7 collective-permute-done.29.out_core
  190.9 2.6 return_kernel.1
  193.4 20.8 %collective-permute-done.38.refs_7_.refs_10_ = bf16[2,4,48,512]{3,2,1,0:T(8,128)(2,1)S(1)} collective-permute-done((bf16[2,4,48,512]{3,2,1,0:T(8,128)(2,1)}, bf16[2,4,48,512]{3,2,1,0:T(8,128)(2,1)S(1)}, u32[]{:S(2)}, u32[]{:S(2)}) %collective-permute-start.38) | collective-permute-done | bytes 393248 | tf_op jit(solution)/shard_map/ppermute | solution.py:820
  215.7 2.7 add_kernel.2
  218.4 1.6 collective-permute-start.39
  220.0 2.4 collective-permute-start.40
  222.9 11.4 %collective-permute-done.42.refs_11_ = bf16[4,48,512]{2,1,0:T(8,128)(2,1)S(1)} collective-permute-done((bf16[4,48,512]{2,1,0:T(8,128)(2,1)}, bf16[4,48,512]{2,1,0:T(8,128)(2,1)S(1)}, u32[]{:S(2)}, u32[]{:S(2)}) %collective-permute-start.42) | collective-permute-done | bytes 196640 | tf_op jit(solution)/shard_map/ppermute | solution.py:820
  236.0 4.3 %add_kernel.3 = bf16[4,48,3200]{2,1,0:T(8,128)(2,1)} custom-call(bf16[2,4,48,1152]{3,2,1,0:T(8,128)(2,1)} %get-tuple-element.253.refs_0_, bf16[2,4,48,1152]{3,2,1,0:T(8,128)(2,1)} %copy-done.10, bf16[4,48,1152]{2,1,0:T(8,128)(2,1)} %copy-done.29, bf16[2,4,48,768]{3,2,1,0:T(8,128)(2,1)} %get-tuple-element.260.refs_2_.refs_3_, ...), custom_call_target="tpu_custom_call" | custom-call | tf_op jit(solution)/shard_map/add_kernel/pallas_call | solution.py:808
  240.4 6.0 %all-to-all-start.4 = ((bf16[8,24,3200]{2,1,0:T(8,128)(2,1)}), bf16[8,24,3200]{2,1,0:T(8,128)(2,1)S(1)}, u32[]{:S(2)}, u32[]{:S(2)}) async-start(bf16[8,24,3200]{2,1,0:T(8,128)(2,1)} %bitcast.57), calls=%async_computation.4 | async-start | bytes 2457600 | tf_op jit(solution)/shard_map/all_to_all | solution.py:824
  247.9 2.9 %depth_sum_kernel.1 = (bf16[24,1536]{1,0:T(8,128)(2,1)}, bf16[24,1536]{1,0:T(8,128)(2,1)}, bf16[2,24,1536]{2,1,0:T(8,128)(2,1)}) custom-call(s32[1,4]{1,0:T(1,128)} %add_bitcast_fusion.me.refs_0_, bf16[8,96,1536]{2,1,0:T(8,128)(2,1)} %copy-done.3), custom_call_target="tpu_custom_call" | custom-call | tf_op jit(solution)/shard_map/depth_sum_kernel/pallas_call | solution.py:783
  251.8 3.4 %collective-permute-done.43.chip = bf16[2,40,1536]{2,1,0:T(8,128)(2,1)S(1)} collective-permute-done((bf16[2,40,1536]{2,1,0:T(8,128)(2,1)S(1)}, bf16[2,40,1536]{2,1,0:T(8,128)(2,1)S(1)}, u32[]{:S(2)}, u32[]{:S(2)}) %collective-permute-start.43) | collective-permute-done | bytes 245792 | tf_op jit(solution)/shard_map/ppermute | solution.py:820
  255.3 2.6 collective-permute-done.46.chip
  258.0 7.4 %image_grad_kernel.1 = bf16[1024,768]{1,0:T(8,128)(2,1)} custom-call(bf16[1024,768]{1,0:T(8,128)(2,1)} %get-tuple-element.236.refs_6_.kv_keep, bf16[1024,768]{1,0:T(8,128)(2,1)} %get-tuple-element.276.kv_send, s32[1,4]{1,0:T(1,128)} %add_bitcast_fusion.me.refs_0_, bf16[4,48,1664]{2,1,0:T(8,128)(2,1)} %bitcast.48, bf16[4,48,1664]{2,1,0:T(8,128)(2,1)} %copy-done.5, ...), custom_call_target="tpu_custom_call" | custom-call | tf_op jit(solution)/shard_map/image_grad_kernel/pallas_call | solution.py:783
  266.0 2.5 unpack_hidden_kernel.1
  269.2 2.0 collect_kernel.1
  271.1 5.7 %all-to-all-done.4 = bf16[8,24,3200]{2,1,0:T(8,128)(2,1)S(1)} async-done(((bf16[8,24,3200]{2,1,0:T(8,128)(2,1)}), bf16[8,24,3200]{2,1,0:T(8,128)(2,1)S(1)}, u32[]{:S(2)}, u32[]{:S(2)}) %all-to-all-start.4) | async-done | bytes 1228832 | tf_op jit(solution)/shard_map/all_to_all | solution.py:824
  (190 shorter events, 39.9 us)
Async XLA Ops:
  2.5 23.8 %all-to-all-start = ((bf16[8,24,1536]{2,1,0:T(8,128)(2,1)}), bf16[8,24,1536]{2,1,0:T(8,128)(2,1)S(1)}, u32[]{:S(2)}, u32[]{:S(2)}) async-start(bf16[8,24,1536]{2,1,0:T(8,128)(2,1)} %bitcast.59), calls=%async_computation | async-start | bytes 1179648 | tf_op jit(solution)/shard_map/all_to_all | solution.py:824
  12.4 13.8 %collective-permute-start = (bf16[2,80,1536]{2,1,0:T(8,128)(2,1)}, bf16[2,80,1536]{2,1,0:T(8,128)(2,1)S(1)}, u32[]{:S(2)}, u32[]{:S(2)}) collective-permute-start(bf16[2,80,1536]{2,1,0:T(8,128)(2,1)} %get-tuple-element.153), channel_id=1, source_target_pairs={{0,2},{2,0},{1,3},{3,1},{4,6},{6,4},{5,7},{7,5},{8,10},{10,8},{9,1... | collective-permute-start | bytes 1474568 | tf_op jit(solution)/shard_map/ppermute | solution.py:820
  26.2 22.7 %collective-permute-start.5 = (bf16[768,1024]{1,0:T(8,128)(2,1)}, bf16[768,1024]{1,0:T(8,128)(2,1)S(1)}, u32[]{:S(2)}, u32[]{:S(2)}) collective-permute-start(bf16[768,1024]{1,0:T(8,128)(2,1)} %transpose_kernel.1.refs_4_), channel_id=1, source_target_pairs={{0,1},{1,0},{2,3},{3,2},{4,5},{5,4},{6,7},{7,6},{8,9},{9,8},{10,11... | collective-permute-start | bytes 4718600 | tf_op jit(solution)/shard_map/ppermute | solution.py:820
  26.3 22.7 %all-to-all-start.1 = ((bf16[8,24,1664]{2,1,0:T(8,128)(2,1)}), bf16[8,24,1664]{2,1,0:T(8,128)(2,1)S(1)}, u32[]{:S(2)}, u32[]{:S(2)}) async-start(bf16[8,24,1664]{2,1,0:T(8,128)(2,1)} %bitcast.58), calls=%async_computation.1 | async-start | bytes 1277952 | tf_op jit(solution)/shard_map/all_to_all | solution.py:824
  31.2 10.2 %collective-permute-start.6 = (bf16[4,48,1536]{2,1,0:T(8,128)(2,1)S(1)}, bf16[4,48,1536]{2,1,0:T(8,128)(2,1)S(1)}, u32[]{:S(2)}, u32[]{:S(2)}) collective-permute-start(bf16[4,48,1536]{2,1,0:T(8,128)(2,1)S(1)} %bitcast.52), channel_id=1, source_target_pairs={{0,1},{1,0},{2,3},{3,2},{4,5},{5,4},{6,7},{7,6},{8,9},{9,8},{10,11... | collective-permute-start | bytes 1769480 | tf_op jit(solution)/shard_map/ppermute | solution.py:820
  31.7 15.2 %collective-permute-start.4 = (bf16[4,48,1536]{2,1,0:T(8,128)(2,1)S(1)}, bf16[4,48,1536]{2,1,0:T(8,128)(2,1)S(1)}, u32[]{:S(2)}, u32[]{:S(2)}) collective-permute-start(bf16[4,48,1536]{2,1,0:T(8,128)(2,1)S(1)} %bitcast.53), channel_id=1, source_target_pairs={{0,2},{2,0},{1,3},{3,1},{4,6},{6,4},{5,7},{7,5},{8,10},{10,8},{9,1... | collective-permute-start | bytes 1769480 | tf_op jit(solution)/shard_map/ppermute | solution.py:820
  33.2 15.1 %collective-permute-start.3 = (bf16[4,48,1536]{2,1,0:T(8,128)(2,1)S(1)}, bf16[4,48,1536]{2,1,0:T(8,128)(2,1)}, u32[]{:S(2)}, u32[]{:S(2)}) collective-permute-start(bf16[4,48,1536]{2,1,0:T(8,128)(2,1)S(1)} %bitcast.54), channel_id=1, source_target_pairs={{0,4},{4,0},{1,5},{5,1},{2,6},{6,2},{3,7},{7,3},{8,12},{12,8},{9,1... | collective-permute-start | bytes 1769480 | tf_op jit(solution)/shard_map/ppermute | solution.py:820
  50.2 33.1 %all-to-all-start.2 = ((bf16[4,96,1536]{2,1,0:T(8,128)(2,1)}), bf16[4,96,1536]{2,1,0:T(8,128)(2,1)}, u32[]{:S(2)}, u32[]{:S(2)}) async-start(bf16[4,96,1536]{2,1,0:T(8,128)(2,1)} %bitcast.61), calls=%async_computation.2 | async-start | bytes 2359296 | tf_op jit(solution)/shard_map/all_to_all | solution.py:824
  54.7 6.1 %collective-permute-start.11 = (bf16[4,48,1664]{2,1,0:T(8,128)(2,1)S(1)}, bf16[4,48,1664]{2,1,0:T(8,128)(2,1)S(1)}, u32[]{:S(2)}, u32[]{:S(2)}) collective-permute-start(bf16[4,48,1664]{2,1,0:T(8,128)(2,1)S(1)} %bitcast.43), channel_id=1, source_target_pairs={{0,1},{1,0},{2,3},{3,2},{4,5},{5,4},{6,7},{7,6},{8,9},{9,8},{10,11... | collective-permute-start | bytes 1916936 | tf_op jit(solution)/shard_map/ppermute | solution.py:820
  54.8 16.8 %collective-permute-start.8 = (bf16[4,48,1664]{2,1,0:T(8,128)(2,1)S(1)}, bf16[4,48,1664]{2,1,0:T(8,128)(2,1)S(1)}, u32[]{:S(2)}, u32[]{:S(2)}) collective-permute-start(bf16[4,48,1664]{2,1,0:T(8,128)(2,1)S(1)} %bitcast.44), channel_id=1, source_target_pairs={{0,2},{2,0},{1,3},{3,1},{4,6},{6,4},{5,7},{7,5},{8,10},{10,8},{9,1... | collective-permute-start | bytes 1916936 | tf_op jit(solution)/shard_map/ppermute | solution.py:820
  56.3 16.5 %collective-permute-start.7 = (bf16[4,48,1664]{2,1,0:T(8,128)(2,1)S(1)}, bf16[4,48,1664]{2,1,0:T(8,128)(2,1)S(1)}, u32[]{:S(2)}, u32[]{:S(2)}) collective-permute-start(bf16[4,48,1664]{2,1,0:T(8,128)(2,1)S(1)} %bitcast.45), channel_id=1, source_target_pairs={{0,4},{4,0},{1,5},{5,1},{2,6},{6,2},{3,7},{7,3},{8,12},{12,8},{9,1... | collective-permute-start | bytes 1916936 | tf_op jit(solution)/shard_map/ppermute | solution.py:820
  57.8 3.1 %collective-permute-start.9 = (bf16[4,48,1536]{2,1,0:T(8,128)(2,1)}, bf16[4,48,1536]{2,1,0:T(8,128)(2,1)S(1)}, u32[]{:S(2)}, u32[]{:S(2)}) collective-permute-start(bf16[4,48,1536]{2,1,0:T(8,128)(2,1)} %collective-permute-done.3.refs_2_), channel_id=1, source_target_pairs={{0,1},{1,0},{2,3},{3,2},{4,5},{5,4},{6,7},{7,6},{8,9},{9,8},{10,11... | collective-permute-start | bytes 1769480 | tf_op jit(solution)/shard_map/ppermute | solution.py:820
  72.7 17.3 %collective-permute-start.15 = (bf16[4,48,1664]{2,1,0:T(8,128)(2,1)S(1)}, bf16[4,48,1664]{2,1,0:T(8,128)(2,1)}, u32[]{:S(2)}, u32[]{:S(2)}) collective-permute-start(bf16[4,48,1664]{2,1,0:T(8,128)(2,1)S(1)} %collective-permute-done.7.refs_10_.refs_2_.refs_3_), channel_id=1, source_target_pairs={{0,1},{1,0},{2,3},{3,2},{4,5},{5,4},{6,7},{7,6},{8,9},{9,8},{10,11... | collective-permute-start | bytes 1916936 | tf_op jit(solution)/shard_map/ppermute | solution.py:820
  72.8 17.3 %collective-permute-start.14 = (bf16[4,48,1664]{2,1,0:T(8,128)(2,1)S(1)}, bf16[4,48,1664]{2,1,0:T(8,128)(2,1)}, u32[]{:S(2)}, u32[]{:S(2)}) collective-permute-start(bf16[4,48,1664]{2,1,0:T(8,128)(2,1)S(1)} %collective-permute-done.8.refs_9_.refs_1_.refs_2_), channel_id=1, source_target_pairs={{0,1},{1,0},{2,3},{3,2},{4,5},{5,4},{6,7},{7,6},{8,9},{9,8},{10,11... | collective-permute-start | bytes 1916936 | tf_op jit(solution)/shard_map/ppermute | solution.py:820
  73.3 17.3 %collective-permute-start.13 = (bf16[4,48,1664]{2,1,0:T(8,128)(2,1)S(1)}, bf16[4,48,1664]{2,1,0:T(8,128)(2,1)}, u32[]{:S(2)}, u32[]{:S(2)}) collective-permute-start(bf16[4,48,1664]{2,1,0:T(8,128)(2,1)S(1)} %collective-permute-done.8.refs_9_.refs_1_.refs_2_), channel_id=1, source_target_pairs={{0,4},{4,0},{1,5},{5,1},{2,6},{6,2},{3,7},{7,3},{8,12},{12,8},{9,1... | collective-permute-start | bytes 1916936 | tf_op jit(solution)/shard_map/ppermute | solution.py:820
  74.7 15.3 %collective-permute-start.12 = (bf16[4,48,1536]{2,1,0:T(8,128)(2,1)}, bf16[4,48,1536]{2,1,0:T(8,128)(2,1)}, u32[]{:S(2)}, u32[]{:S(2)}) collective-permute-start(bf16[4,48,1536]{2,1,0:T(8,128)(2,1)} %collective-permute-done.3.refs_2_), channel_id=1, source_target_pairs={{0,2},{2,0},{1,3},{3,1},{4,6},{6,4},{5,7},{7,5},{8,10},{10,8},{9,1... | collective-permute-start | bytes 1769480 | tf_op jit(solution)/shard_map/ppermute | solution.py:820
  83.3 35.8 %collective-permute-start.24 = (bf16[4,96,1536]{2,1,0:T(8,128)(2,1)}, bf16[4,96,1536]{2,1,0:T(8,128)(2,1)S(1)}, u32[]{:S(2)}, u32[]{:S(2)}) collective-permute-start(bf16[4,96,1536]{2,1,0:T(8,128)(2,1)} %all-to-all-done.2.refs_8_), channel_id=1, source_target_pairs={{0,4},{4,0},{1,5},{5,1},{2,6},{6,2},{3,7},{7,3},{8,12},{12,8},{9,1... | collective-permute-start | bytes 3538952 | tf_op jit(solution)/shard_map/ppermute | solution.py:820
  90.6 3.1 %collective-permute-start.17 = (bf16[4,48,1664]{2,1,0:T(8,128)(2,1)}, bf16[4,48,1664]{2,1,0:T(8,128)(2,1)S(1)}, u32[]{:S(2)}, u32[]{:S(2)}) collective-permute-start(bf16[4,48,1664]{2,1,0:T(8,128)(2,1)} %collective-permute-done.13.refs_11_.refs_3_.refs_4_), channel_id=1, source_target_pairs={{0,1},{1,0},{2,3},{3,2},{4,5},{5,4},{6,7},{7,6},{8,9},{9,8},{10,11... | collective-permute-start | bytes 1916936 | tf_op jit(solution)/shard_map/ppermute | solution.py:820
  90.6 3.1 %collective-permute-start.16 = (bf16[4,48,1536]{2,1,0:T(8,128)(2,1)}, bf16[4,48,1536]{2,1,0:T(8,128)(2,1)S(1)}, u32[]{:S(2)}, u32[]{:S(2)}) collective-permute-start(bf16[4,48,1536]{2,1,0:T(8,128)(2,1)} %collective-permute-done.12.refs_3_), channel_id=1, source_target_pairs={{0,1},{1,0},{2,3},{3,2},{4,5},{5,4},{6,7},{7,6},{8,9},{9,8},{10,11... | collective-permute-start | bytes 1769480 | tf_op jit(solution)/shard_map/ppermute | solution.py:820
  91.1 18.9 %collective-permute-start.22 = (bf16[160,768]{1,0:T(8,128)(2,1)}, bf16[160,768]{1,0:T(8,128)(2,1)S(1)}, u32[]{:S(2)}, u32[]{:S(2)}) collective-permute-start(bf16[160,768]{1,0:T(8,128)(2,1)} %get-tuple-element.196.refs_4_.grad_slot), channel_id=1, source_target_pairs={{0,2},{2,0},{1,3},{3,1},{4,6},{6,4},{5,7},{7,5},{8,10},{10,8},{9,1... | collective-permute-start | bytes 737288 | tf_op jit(solution)/shard_map/ppermute | solution.py:820
  91.7 18.8 %collective-permute-start.21 = (bf16[160,768]{1,0:T(8,128)(2,1)}, bf16[160,768]{1,0:T(8,128)(2,1)}, u32[]{:S(2)}, u32[]{:S(2)}) collective-permute-start(bf16[160,768]{1,0:T(8,128)(2,1)} %get-tuple-element.196.refs_4_.grad_slot), channel_id=1, source_target_pairs={{0,1},{1,0},{2,3},{3,2},{4,5},{5,4},{6,7},{7,6},{8,9},{9,8},{10,11... | collective-permute-start | bytes 737288 | tf_op jit(solution)/shard_map/ppermute | solution.py:820
  109.3 8.3 %collective-permute-start.19 = (bf16[160,768]{1,0:T(8,128)(2,1)}, bf16[160,768]{1,0:T(8,128)(2,1)S(1)}, u32[]{:S(2)}, u32[]{:S(2)}) collective-permute-start(bf16[160,768]{1,0:T(8,128)(2,1)} %get-tuple-element.195.refs_0_), channel_id=1, source_target_pairs={{0,2},{2,0},{1,3},{3,1},{4,6},{6,4},{5,7},{7,5},{8,10},{10,8},{9,1... | collective-permute-start | bytes 737288 | tf_op jit(solution)/shard_map/ppermute | solution.py:820
  110.0 28.2 %collective-permute-start.28 = (bf16[160,3072]{1,0:T(8,128)(2,1)}, bf16[160,3072]{1,0:T(8,128)(2,1)S(1)}, u32[]{:S(2)}, u32[]{:S(2)}) collective-permute-start(bf16[160,3072]{1,0:T(8,128)(2,1)} %get-tuple-element.204.refs_0_.saved), channel_id=1, source_target_pairs={{0,1},{1,0},{2,3},{3,2},{4,5},{5,4},{6,7},{7,6},{8,9},{9,8},{10,11... | collective-permute-start | bytes 2949128 | tf_op jit(solution)/shard_map/ppermute | solution.py:820
  110.0 7.6 %collective-permute-start.23 = (bf16[160,768]{1,0:T(8,128)(2,1)S(1)}, bf16[160,768]{1,0:T(8,128)(2,1)S(1)}, u32[]{:S(2)}, u32[]{:S(2)}) collective-permute-start(bf16[160,768]{1,0:T(8,128)(2,1)S(1)} %collective-permute-done.22.refs_6_), channel_id=1, source_target_pairs={{0,1},{1,0},{2,3},{3,2},{4,5},{5,4},{6,7},{7,6},{8,9},{9,8},{10,11... | collective-permute-start | bytes 737288 | tf_op jit(solution)/shard_map/ppermute | solution.py:820
  110.5 7.1 %collective-permute-start.18 = (bf16[160,768]{1,0:T(8,128)(2,1)}, bf16[160,768]{1,0:T(8,128)(2,1)S(1)}, u32[]{:S(2)}, u32[]{:S(2)}) collective-permute-start(bf16[160,768]{1,0:T(8,128)(2,1)} %get-tuple-element.195.refs_0_), channel_id=1, source_target_pairs={{0,1},{1,0},{2,3},{3,2},{4,5},{5,4},{6,7},{7,6},{8,9},{9,8},{10,11... | collective-permute-start | bytes 737288 | tf_op jit(solution)/shard_map/ppermute | solution.py:820
  129.2 9.0 %collective-permute-start.27 = (bf16[160,768]{1,0:T(8,128)(2,1)}, bf16[160,768]{1,0:T(8,128)(2,1)S(1)}, u32[]{:S(2)}, u32[]{:S(2)}) collective-permute-start(bf16[160,768]{1,0:T(8,128)(2,1)} %get-tuple-element.201), channel_id=1, source_target_pairs={{0,1},{1,0},{2,3},{3,2},{4,5},{5,4},{6,7},{7,6},{8,9},{9,8},{10,11... | collective-permute-start | bytes 737288 | tf_op jit(solution)/shard_map/ppermute | solution.py:820
  131.8 8.1 %collective-permute-start.26 = (bf16[160,768]{1,0:T(8,128)(2,1)S(1)}, bf16[160,768]{1,0:T(8,128)(2,1)S(1)}, u32[]{:S(2)}, u32[]{:S(2)}) collective-permute-start(bf16[160,768]{1,0:T(8,128)(2,1)S(1)} %combine_kernel.2), channel_id=1, source_target_pairs={{0,2},{2,0},{1,3},{3,1},{4,6},{6,4},{5,7},{7,5},{8,10},{10,8},{9,1... | collective-permute-start | bytes 737288 | tf_op jit(solution)/shard_map/ppermute | solution.py:820
  140.6 94.6 %all-to-all-start.3 = ((bf16[8,96,1536]{2,1,0:T(8,128)(2,1)}), bf16[8,96,1536]{2,1,0:T(8,128)(2,1)S(1)}, u32[]{:S(2)}, u32[]{:S(2)}) async-start(bf16[8,96,1536]{2,1,0:T(8,128)(2,1)} %bitcast.49), calls=%async_computation.3 | async-start | bytes 4718592 | tf_op jit(solution)/shard_map/all_to_all | solution.py:824
  146.8 12.0 %collective-permute-start.30 = (bf16[160,768]{1,0:T(8,128)(2,1)}, bf16[160,768]{1,0:T(8,128)(2,1)S(1)}, u32[]{:S(2)}, u32[]{:S(2)}) collective-permute-start(bf16[160,768]{1,0:T(8,128)(2,1)} %get-tuple-element.219), channel_id=1, source_target_pairs={{0,1},{1,0},{2,3},{3,2},{4,5},{5,4},{6,7},{7,6},{8,9},{9,8},{10,11... | collective-permute-start | bytes 737288 | tf_op jit(solution)/shard_map/ppermute | solution.py:820
  158.8 9.6 %collective-permute-start.32 = (bf16[1024,768]{1,0:T(8,128)(2,1)}, bf16[1024,768]{1,0:T(8,128)(2,1)S(1)}, u32[]{:S(2)}, u32[]{:S(2)}) collective-permute-start(bf16[1024,768]{1,0:T(8,128)(2,1)} %get-tuple-element.276.kv_send), channel_id=1, source_target_pairs={{0,1},{1,0},{2,3},{3,2},{4,5},{5,4},{6,7},{7,6},{8,9},{9,8},{10,11... | collective-permute-start | bytes 4718600 | tf_op jit(solution)/shard_map/ppermute | solution.py:820
  159.3 9.1 %collective-permute-start.31 = (bf16[160,1152]{1,0:T(8,128)(2,1)}, bf16[160,1152]{1,0:T(8,128)(2,1)S(1)}, u32[]{:S(2)}, u32[]{:S(2)}) collective-permute-start(bf16[160,1152]{1,0:T(8,128)(2,1)} %get-tuple-element.226), channel_id=1, source_target_pairs={{0,1},{1,0},{2,3},{3,2},{4,5},{5,4},{6,7},{7,6},{8,9},{9,8},{10,11... | collective-permute-start | bytes 1105928 | tf_op jit(solution)/shard_map/ppermute | solution.py:820
  159.4 8.9 %collective-permute-start.33 = (bf16[160,768]{1,0:T(8,128)(2,1)S(1)}, bf16[160,768]{1,0:T(8,128)(2,1)S(1)}, u32[]{:S(2)}, u32[]{:S(2)}) collective-permute-start(bf16[160,768]{1,0:T(8,128)(2,1)S(1)} %combine_kernel.3), channel_id=1, source_target_pairs={{0,2},{2,0},{1,3},{3,1},{4,6},{6,4},{5,7},{7,5},{8,10},{10,8},{9,1... | collective-permute-start | bytes 737288 | tf_op jit(solution)/shard_map/ppermute | solution.py:820
  168.4 11.0 %collective-permute-start.34 = (bf16[160,1152]{1,0:T(8,128)(2,1)}, bf16[160,1152]{1,0:T(8,128)(2,1)S(1)}, u32[]{:S(2)}, u32[]{:S(2)}) collective-permute-start(bf16[160,1152]{1,0:T(8,128)(2,1)} %get-tuple-element.242), channel_id=1, source_target_pairs={{0,1},{1,0},{2,3},{3,2},{4,5},{5,4},{6,7},{7,6},{8,9},{9,8},{10,11... | collective-permute-start | bytes 1105928 | tf_op jit(solution)/shard_map/ppermute | solution.py:820
  179.4 34.9 %collective-permute-start.35 = (bf16[2,4,48,1152]{3,2,1,0:T(8,128)(2,1)}, bf16[2,4,48,1152]{3,2,1,0:T(8,128)(2,1)S(1)}, u32[]{:S(2)}, u32[]{:S(2)}) collective-permute-start(bf16[2,4,48,1152]{3,2,1,0:T(8,128)(2,1)} %get-tuple-element.254), channel_id=1, source_target_pairs={{0,4},{4,0},{1,5},{5,1},{2,6},{6,2},{3,7},{7,3},{8,12},{12,8},{9,1... | collective-permute-start | bytes 2654216 | tf_op jit(solution)/shard_map/ppermute | solution.py:820
  185.8 28.5 %collective-permute-start.37 = (bf16[2,4,48,768]{3,2,1,0:T(8,128)(2,1)}, bf16[2,4,48,768]{3,2,1,0:T(8,128)(2,1)S(1)}, u32[]{:S(2)}, u32[]{:S(2)}) collective-permute-start(bf16[2,4,48,768]{3,2,1,0:T(8,128)(2,1)} %get-tuple-element.256), channel_id=1, source_target_pairs={{0,2},{2,0},{1,3},{3,1},{4,6},{6,4},{5,7},{7,5},{8,10},{10,8},{9,1... | collective-permute-start | bytes 1769480 | tf_op jit(solution)/shard_map/ppermute | solution.py:820
  187.1 27.2 %collective-permute-start.36 = (bf16[2,4,48,768]{3,2,1,0:T(8,128)(2,1)S(1)}, bf16[2,4,48,768]{3,2,1,0:T(8,128)(2,1)S(1)}, u32[]{:S(2)}, u32[]{:S(2)}) collective-permute-start(bf16[2,4,48,768]{3,2,1,0:T(8,128)(2,1)S(1)} %copy-done.47), channel_id=1, source_target_pairs={{0,2},{2,0},{1,3},{3,1},{4,6},{6,4},{5,7},{7,5},{8,10},{10,8},{9,1... | collective-permute-start | bytes 1769480 | tf_op jit(solution)/shard_map/ppermute | solution.py:820
  187.8 26.5 %collective-permute-start.38 = (bf16[2,4,48,512]{3,2,1,0:T(8,128)(2,1)}, bf16[2,4,48,512]{3,2,1,0:T(8,128)(2,1)S(1)}, u32[]{:S(2)}, u32[]{:S(2)}) collective-permute-start(bf16[2,4,48,512]{3,2,1,0:T(8,128)(2,1)} %get-tuple-element.257), channel_id=1, source_target_pairs={{0,4},{4,0},{1,5},{5,1},{2,6},{6,2},{3,7},{7,3},{8,12},{12,8},{9,1... | collective-permute-start | bytes 1179656 | tf_op jit(solution)/shard_map/ppermute | solution.py:820
  218.4 16.7 %collective-permute-start.39 = (bf16[4,48,1152]{2,1,0:T(8,128)(2,1)}, bf16[4,48,1152]{2,1,0:T(8,128)(2,1)S(1)}, u32[]{:S(2)}, u32[]{:S(2)}) collective-permute-start(bf16[4,48,1152]{2,1,0:T(8,128)(2,1)} %get-tuple-element.266), channel_id=1, source_target_pairs={{0,2},{2,0},{1,3},{3,1},{4,6},{6,4},{5,7},{7,5},{8,10},{10,8},{9,1... | collective-permute-start | bytes 1327112 | tf_op jit(solution)/shard_map/ppermute | solution.py:820
  220.0 14.2 %collective-permute-start.40 = (bf16[4,48,768]{2,1,0:T(8,128)(2,1)}, bf16[4,48,768]{2,1,0:T(8,128)(2,1)S(1)}, u32[]{:S(2)}, u32[]{:S(2)}) collective-permute-start(bf16[4,48,768]{2,1,0:T(8,128)(2,1)} %get-tuple-element.267), channel_id=1, source_target_pairs={{0,4},{4,0},{1,5},{5,1},{2,6},{6,2},{3,7},{7,3},{8,12},{12,8},{9,1... | collective-permute-start | bytes 884744 | tf_op jit(solution)/shard_map/ppermute | solution.py:820
  222.4 12.8 %collective-permute-start.41 = (bf16[4,48,768]{2,1,0:T(8,128)(2,1)}, bf16[4,48,768]{2,1,0:T(8,128)(2,1)S(1)}, u32[]{:S(2)}, u32[]{:S(2)}) collective-permute-start(bf16[4,48,768]{2,1,0:T(8,128)(2,1)} %get-tuple-element.268), channel_id=1, source_target_pairs={{0,4},{4,0},{1,5},{5,1},{2,6},{6,2},{3,7},{7,3},{8,12},{12,8},{9,1... | collective-permute-start | bytes 884744 | tf_op jit(solution)/shard_map/ppermute | solution.py:820
  222.4 11.8 %collective-permute-start.42 = (bf16[4,48,512]{2,1,0:T(8,128)(2,1)}, bf16[4,48,512]{2,1,0:T(8,128)(2,1)S(1)}, u32[]{:S(2)}, u32[]{:S(2)}) collective-permute-start(bf16[4,48,512]{2,1,0:T(8,128)(2,1)} %get-tuple-element.269), channel_id=1, source_target_pairs={{0,2},{2,0},{1,3},{3,1},{4,6},{6,4},{5,7},{7,5},{8,10},{10,8},{9,1... | collective-permute-start | bytes 589832 | tf_op jit(solution)/shard_map/ppermute | solution.py:820
  240.4 36.4 %all-to-all-start.4 = ((bf16[8,24,3200]{2,1,0:T(8,128)(2,1)}), bf16[8,24,3200]{2,1,0:T(8,128)(2,1)S(1)}, u32[]{:S(2)}, u32[]{:S(2)}) async-start(bf16[8,24,3200]{2,1,0:T(8,128)(2,1)} %bitcast.57), calls=%async_computation.4 | async-start | bytes 2457600 | tf_op jit(solution)/shard_map/all_to_all | solution.py:824
  246.3 8.8 %collective-permute-start.43 = (bf16[2,40,1536]{2,1,0:T(8,128)(2,1)S(1)}, bf16[2,40,1536]{2,1,0:T(8,128)(2,1)S(1)}, u32[]{:S(2)}, u32[]{:S(2)}) collective-permute-start(bf16[2,40,1536]{2,1,0:T(8,128)(2,1)S(1)} %copy-done.48), channel_id=1, source_target_pairs={{0,2},{2,0},{1,3},{3,1},{4,6},{6,4},{5,7},{7,5},{8,10},{10,8},{9,1... | collective-permute-start | bytes 737288 | tf_op jit(solution)/shard_map/ppermute | solution.py:820
  247.8 20.7 %collective-permute-start.44 = (bf16[40,1536]{1,0:T(8,128)(2,1)S(1)}, bf16[40,1536]{1,0:T(8,128)(2,1)S(1)}, u32[]{:S(2)}, u32[]{:S(2)}) collective-permute-start(bf16[40,1536]{1,0:T(8,128)(2,1)S(1)} %copy-done.50), channel_id=1, source_target_pairs={{0,1},{1,0},{2,3},{3,2},{4,5},{5,4},{6,7},{7,6},{8,9},{9,8},{10,11... | collective-permute-start | bytes 368648 | tf_op jit(solution)/shard_map/ppermute | solution.py:820
  250.8 14.5 %collective-permute-start.47 = (bf16[24,1536]{1,0:T(8,128)(2,1)}, bf16[24,1536]{1,0:T(8,128)(2,1)S(1)}, u32[]{:S(2)}, u32[]{:S(2)}) collective-permute-start(bf16[24,1536]{1,0:T(8,128)(2,1)} %get-tuple-element.289), channel_id=1, source_target_pairs={{0,1},{1,0},{2,3},{3,2},{4,5},{5,4},{6,7},{7,6},{8,9},{9,8},{10,11... | collective-permute-start | bytes 221192 | tf_op jit(solution)/shard_map/ppermute | solution.py:820
  251.2 6.7 %collective-permute-start.46 = (bf16[2,24,1536]{2,1,0:T(8,128)(2,1)}, bf16[2,24,1536]{2,1,0:T(8,128)(2,1)S(1)}, u32[]{:S(2)}, u32[]{:S(2)}) collective-permute-start(bf16[2,24,1536]{2,1,0:T(8,128)(2,1)} %get-tuple-element.288), channel_id=1, source_target_pairs={{0,2},{2,0},{1,3},{3,1},{4,6},{6,4},{5,7},{7,5},{8,10},{10,8},{9,1... | collective-permute-start | bytes 442376 | tf_op jit(solution)/shard_map/ppermute | solution.py:820
  255.2 13.3 %collective-permute-start.45 = (bf16[40,1536]{1,0:T(8,128)(2,1)S(1)}, bf16[40,1536]{1,0:T(8,128)(2,1)S(1)}, u32[]{:S(2)}, u32[]{:S(2)}) collective-permute-start(bf16[40,1536]{1,0:T(8,128)(2,1)S(1)} %slice_bitcast_fusion.1), channel_id=1, source_target_pairs={{0,1},{1,0},{2,3},{3,2},{4,5},{5,4},{6,7},{7,6},{8,9},{9,8},{10,11... | collective-permute-start | bytes 368648 | tf_op jit(solution)/shard_map/ppermute | solution.py:820
  257.9 7.5 %collective-permute-start.48 = (bf16[24,1536]{1,0:T(8,128)(2,1)S(1)}, bf16[24,1536]{1,0:T(8,128)(2,1)S(1)}, u32[]{:S(2)}, u32[]{:S(2)}) collective-permute-start(bf16[24,1536]{1,0:T(8,128)(2,1)S(1)} %slice_bitcast_fusion.2), channel_id=1, source_target_pairs={{0,1},{1,0},{2,3},{3,2},{4,5},{5,4},{6,7},{7,6},{8,9},{9,8},{10,11... | collective-permute-start | bytes 221192 | tf_op jit(solution)/shard_map/ppermute | solution.py:820
  (57 other events, 363.9 us)

commit v2 on v1

--- a/solution.py
+++ b/solution.py
@@ -779,7 +779,20 @@
 HB = pl.BlockSpec(memory_space=pl.ANY)
 
 
-def run(kernel, outs, specs, scratch, *args, mib=58, copied=0):
+COST_US = {
+    "forward_kernel": 12, "mlp_kernel": 9, "hidden_grad_kernel": 6, "cross_back_kernel": 12,
+    "self_back_kernel": 8, "cross_grad_kernel": 10, "self_grad_kernel": 4, "return_kernel": 3,
+    "image_grad_kernel": 7, "spread_kernel": 3,
+}
+
+
+def costs(kernel):
+    name = (kernel.func if isinstance(kernel, functools.partial) else kernel).__name__
+    flops = int(COST_US.get(name, 2) * 0.4 * 1e9)
+    return pl.CostEstimate(flops=flops, bytes_accessed=2**20, transcendentals=0)
+
+
+def run(kernel, outs, specs, scratch, *args, mib=58, copied=0, cost=None):
     return pl.pallas_call(
         kernel,
         out_shape=[jax.ShapeDtypeStruct(s, t) for s, t in outs],
@@ -787,6 +800,7 @@
         out_specs=[VM] * (len(outs) - copied) + [HB] * copied,
         scratch_shapes=scratch,
         compiler_params=pltpu.CompilerParams(vmem_limit_bytes=mib * 2**20),
+        cost_estimate=cost or costs(kernel),
         name=(kernel.func if isinstance(kernel, functools.partial) else kernel).__name__,
     )(*args)
 
@@ -946,6 +960,7 @@
         ],
         lens, me, slotted, img, *pieces_a, *pieces_b,
         copied=2,
+        cost=pl.CostEstimate(flops=13200000000, bytes_accessed=20 * 2**20, transcendentals=0),
     )
     inputs = group_rows(normed_mlp)
     small_shape = ((11 * PAIRS, LANES), F32)

time: 282 us -> 274 us (0.972)
  waiting for transfers between devices: 104 us -> 99.7 us
    all_to_all x5, waiting for transfers between devices: 14.4 us -> 2.66 us  [swap_all(): return lax.all_to_all(value, axes, split_axis=0, concat_axis=0, tiled=True)]
    ppermute x49, waiting for transfers between devices: 90.1 us -> 97.1 us  [flip(): return lax.ppermute(value, axis, [(0, 1), (1, 0)])]
  transfers between devices with their start and end apart: 54 -> 54, of which waited for: 25 -> 21; matrix products, arithmetic and copies ran while one was open for 0% -> 0% of each run, Pallas kernels for 34% -> 35%
where the time goes in v2:
time: 274 us; the launch traced here: 271 us
  Pallas kernels  100 us (36%)
  waiting for transfers between devices  99.7 us (36%)
  starting transfers between devices  57.3 us (21%)
  local copies, waits for them, and re-layouts  11.2 us (4%)
    ppermute x49, waiting for transfers between devices, flip(): return lax.ppermute(value, axis, [(0, 1), (1, 0)])  97.1 us
    pallas_call x20, Pallas kernels, run(): pl.pallas_call(kernel, out_shape=[jax.ShapeDtypeStruct(s, t) for s, t in...  94.2 us
    ppermute x49, starting transfers between devices, flip(): return lax.ppermute(value, axis, [(0, 1), (1, 0)])  30.5 us
    all_to_all x5, starting transfers between devices, swap_all(): return lax.all_to_all(value, axes, split_axis=0, concat_axis=0, tiled=True)  26.8 us
    unnamed x102, local copies, waits for them, and re-layouts  10 us
    pallas_call x2, Pallas kernels, add_up(): pl.pallas_call(functools.partial(add_kernel, [len(terms) for terms in sum...  6.17 us
  transfers between devices with their start and end apart: 54, of which 21 were waited for; matrix products, arithmetic and copies ran while one was open for 0% of the time, Pallas kernels for 35%

profile of v2, /device:TPU:0, one launch (start us, length us, event | category | flops | bytes accessed | tf_op | source)
XLA Modules:
  0.0 270.8 jit_solution(3125657872966467203)
XLA Ops:
  0.6 1.8 pack_self_kernel.1
  2.5 6.3 %all-to-all-start = ((bf16[8,24,1536]{2,1,0:T(8,128)(2,1)}), bf16[8,24,1536]{2,1,0:T(8,128)(2,1)S(1)}, u32[]{:S(2)}, u32[]{:S(2)}) async-start(bf16[8,24,1536]{2,1,0:T(8,128)(2,1)} %bitcast.60), calls=%async_computation | async-start | bytes 1179648 | tf_op jit(solution)/shard_map/all_to_all | solution.py:838
  9.4 2.9 %pack_group_kernel.1 = (bf16[80,1536]{1,0:T(8,128)(2,1)}, bf16[80,1536]{1,0:T(8,128)(2,1)}, bf16[2,80,1536]{2,1,0:T(8,128)(2,1)}) custom-call(s32[1,4]{1,0:T(1,128)} %add_bitcast_fusion.me.refs_0_, bf16[576,128]{1,0:T(8,128)(2,1)} %bitcast.63, bf16[576,128]{1,0:T(8,128)(2,1)} %bitcast.64, bf16[4,40,768]{2,1,0:T(8,128)(2,1)} %bitcast.61, ...), custom_call_target="tpu_custom_call" | custom-call | flops 800000000 | bytes 1048576 | tf_op jit(solution)/shard_map/pack_group_kernel/pallas_call | solution.py:796
  12.3 1.5 collective-permute-start
  14.4 3.1 %transpose_kernel.1.refs_4_ = bf16[768,1024]{1,0:T(8,128)(2,1)} custom-call(bf16[1024,768]{1,0:T(8,128)(2,1)} %bitcast.45), custom_call_target="tpu_custom_call" | custom-call | flops 800000000 | bytes 1048576 | tf_op jit(solution)/shard_map/transpose_kernel/pallas_call | solution.py:796
  17.5 1.9 pack_cross_kernel.1
  19.4 6.7 %collective-permute-done.chip = bf16[2,80,1536]{2,1,0:T(8,128)(2,1)S(1)} collective-permute-done((bf16[2,80,1536]{2,1,0:T(8,128)(2,1)}, bf16[2,80,1536]{2,1,0:T(8,128)(2,1)S(1)}, u32[]{:S(2)}, u32[]{:S(2)}) %collective-permute-start) | collective-permute-done | bytes 491552 | tf_op jit(solution)/shard_map/ppermute | solution.py:834
  26.2 4.8 %all-to-all-start.1 = ((bf16[8,24,1664]{2,1,0:T(8,128)(2,1)}), bf16[8,24,1664]{2,1,0:T(8,128)(2,1)S(1)}, u32[]{:S(2)}, u32[]{:S(2)}) async-start(bf16[8,24,1664]{2,1,0:T(8,128)(2,1)} %bitcast.54), calls=%async_computation.1 | async-start | bytes 1277952 | tf_op jit(solution)/shard_map/all_to_all | solution.py:838
  31.8 1.5 collective-permute-start.4
  33.3 1.5 collective-permute-start.3
  34.9 1.5 collective-permute-done.1.core
  37.0 2.9 %spread_kernel.1 = (bf16[4,4,24,1536]{3,2,1,0:T(8,128)(2,1)}, bf16[160,768]{1,0:T(8,128)(2,1)}, bf16[160,768]{1,0:T(8,128)(2,1)}) custom-call(s32[1,4]{1,0:T(1,128)} %add_bitcast_fusion.me.refs_0_, s32[1,160]{1,0:T(1,128)} %arr.3, bf16[80,1536]{1,0:T(8,128)(2,1)} %get-tuple-element.152.near, bf16[2,80,1536]{2,1,0:T(8,128)(2,1)} %copy-done.14, ...), custom_call_target="tpu_custom_call" | custom-call | flops 1200000000 | bytes 1048576 | tf_op jit(solution)/shard_map/spread_kernel/pallas_call | solution.py:796
  39.9 7.5 %collective-permute-done.4.refs_1_ = bf16[4,48,1536]{2,1,0:T(8,128)(2,1)S(1)} collective-permute-done((bf16[4,48,1536]{2,1,0:T(8,128)(2,1)S(1)}, bf16[4,48,1536]{2,1,0:T(8,128)(2,1)S(1)}, u32[]{:S(2)}, u32[]{:S(2)}) %collective-permute-start.4) | collective-permute-done | bytes 589856 | tf_op jit(solution)/shard_map/ppermute | solution.py:834
  48.9 1.6 collective-permute-start.8
  50.5 1.5 collective-permute-start.7
  52.5 4.3 %all-to-all-start.2 = ((bf16[4,96,1536]{2,1,0:T(8,128)(2,1)}), bf16[4,96,1536]{2,1,0:T(8,128)(2,1)S(1)}, u32[]{:S(2)}, u32[]{:S(2)}) async-start(bf16[4,96,1536]{2,1,0:T(8,128)(2,1)} %bitcast.47), calls=%async_computation.2 | async-start | bytes 2359296 | tf_op jit(solution)/shard_map/all_to_all | solution.py:838
  56.9 8.8 %collective-permute-done.8.refs_9_.refs_1_.refs_2_ = bf16[4,48,1664]{2,1,0:T(8,128)(2,1)S(1)} collective-permute-done((bf16[4,48,1664]{2,1,0:T(8,128)(2,1)S(1)}, bf16[4,48,1664]{2,1,0:T(8,128)(2,1)S(1)}, u32[]{:S(2)}, u32[]{:S(2)}) %collective-permute-start.8) | collective-permute-done | bytes 639008 | tf_op jit(solution)/shard_map/ppermute | solution.py:834
  65.7 1.3 collective-permute-done.7.refs_10_.refs_2_.refs_3_
  67.6 1.5 collective-permute-start.13
  69.6 14.8 %collective-permute-done.12.refs_3_ = bf16[4,48,1536]{2,1,0:T(8,128)(2,1)} collective-permute-done((bf16[4,48,1536]{2,1,0:T(8,128)(2,1)}, bf16[4,48,1536]{2,1,0:T(8,128)(2,1)}, u32[]{:S(2)}, u32[]{:S(2)}) %collective-permute-start.12) | collective-permute-done | bytes 589856 | tf_op jit(solution)/shard_map/ppermute | solution.py:834
  86.5 1.1 collective-permute-done.16.refs_7_
  87.7 14.6 %forward_kernel.1 = (f32[11,768]{1,0:T(8,128)}, bf16[160,2304]{1,0:T(8,128)(2,1)}, bf16[3,640,160]{2,1,0:T(8,128)(2,1)}, bf16[160,3072]{1,0:T(8,128)(2,1)}, f32[...) custom-call(s32[1,4]{1,0:T(1,128)} %lens.3, ...), custom_call_target="tpu_custom_call" | custom-call | flops 13200000000 | bytes 20971520 | tf_op jit(solution)/shard_map/forward_kernel/pallas_call | solution.py:796
  103.4 7.2 %collective-permute-done.19.refs_2_ = bf16[160,768]{1,0:T(8,128)(2,1)S(1)} collective-permute-done((bf16[160,768]{1,0:T(8,128)(2,1)}, bf16[160,768]{1,0:T(8,128)(2,1)S(1)}, u32[]{:S(2)}, u32[]{:S(2)}) %collective-permute-start.19) | collective-permute-done | bytes 245792 | tf_op jit(solution)/shard_map/ppermute | solution.py:834
  114.2 8.8 %mlp_kernel.1 = (f32[160,768]{1,0:T(8,128)}, bf16[160,768]{1,0:T(8,128)(2,1)}, bf16[160,768]{1,0:T(8,128)(2,1)}, bf16[160,768]{1,0:T(8,128)(2,1)}, f32[160,768]{...) custom-call(s32[1,4]{1,0:T(1,128)} %add_bitcast_fusion.me.refs_0_, ...), custom_call_target="tpu_custom_call" | custom-call | flops 3600000000 | bytes 1048576 | tf_op jit(solution)/shard_map/mlp_kernel/pallas_call | solution.py:796
  123.6 1.2 collective-permute-done.25.far
  125.8 1.6 collective-permute-start.26
  127.4 5.8 %hidden_grad_kernel.1 = bf16[768,1536]{1,0:T(8,128)(2,1)} custom-call(bf16[160,768]{1,0:T(8,128)(2,1)} %get-tuple-element.195.refs_0_, bf16[160,768]{1,0:T(8,128)(2,1)} %copy-done.38, bf16[160,768]{1,0:T(8,128)(2,1)} %copy-done.34, bf16[160,768]{1,0:T(8,128)(2,1)} %copy-done.39, bf16[160,768]{1,0:T(8,128)(2,1)} %get-tuple-element.196.refs_4_.grad_slot, ...), custom_call_target="tpu_custom_call" | custom-call | flops 2400000000 | bytes 1048576 | tf_op jit(solution)/shard_map/hidden_grad_kernel/pallas_call | solution.py:796
  134.6 5.3 %all-to-all-start.3 = ((bf16[8,96,1536]{2,1,0:T(8,128)(2,1)}), bf16[8,96,1536]{2,1,0:T(8,128)(2,1)}, u32[]{:S(2)}, u32[]{:S(2)}) async-start(bf16[8,96,1536]{2,1,0:T(8,128)(2,1)} %bitcast.44), calls=%async_computation.3 | async-start | bytes 4718592 | tf_op jit(solution)/shard_map/all_to_all | solution.py:838
  139.9 11.9 %cross_back_kernel.1 = (f32[160,768]{1,0:T(8,128)}, f32[66,128]{1,0:T(8,128)}, bf16[160,1152]{1,0:T(8,128)(2,1)}, bf16[160,1152]{1,0:T(8,128)(2,1)}, bf16[1024,7...) custom-call(s32[1,4]{1,0:T(1,128)} %lens.3, s32[1,4]{1,0:T(1,128)} %add_bitcast_fusion.me.refs_0_, ...), custom_call_target="tpu_custom_call" | custom-call | flops 4800000000 | bytes 1048576 | tf_op jit(solution)/shard_map/cross_back_kernel/pallas_call | solution.py:796
  153.6 8.2 %self_back_kernel.1 = (bf16[160,768]{1,0:T(8,128)(2,1)}, f32[66,128]{1,0:T(8,128)}, bf16[160,1152]{1,0:T(8,128)(2,1)}, bf16[160,1152]{1,0:T(8,128)(2,1)}) custom-call(s32[1,4]{1,0:T(1,128)} %add_bitcast_fusion.me.refs_0_, f32[160,768]{1,0:T(8,128)} %get-tuple-element.220.grad_state, bf16[3,640,160]{2,1,0:T(8,128)(2,1)} %get-tuple-element.221.probs, ...), custom_call_target="tpu_custom_call" | custom-call | flops 3200000000 | bytes 1048576 | tf_op jit(solution)/shard_map/self_back_kernel/pallas_call | solution.py:796
  163.1 9.8 %cross_grad_kernel.1 = (bf16[2,4,48,1152]{3,2,1,0:T(8,128)(2,1)}, bf16[2,4,48,1152]{3,2,1,0:T(8,128)(2,1)}, bf16[2,4,48,768]{3,2,1,0:T(8,128)(2,1)}, bf16[2,4,48,768]{3,2,1,0:T(8,128)(2,1)}) custom-call(s32[1,4]{1,0:T(1,128)} %add_bitcast_fusion.me.refs_0_, bf16[160,3072]{1,0:T(8,128)(2,1)} %get-tuple-element.204.refs_0_.saved, ...), custom_call_target="tpu_custom_call" | custom-call | flops 4000000000 | bytes 1048576 | tf_op jit(solution)/shard_map/cross_grad_kernel/pallas_call | solution.py:796
  172.9 2.1 collective-permute-start.35
  175.0 4.3 %self_grad_kernel.1 = (bf16[2,4,48,768]{3,2,1,0:T(8,128)(2,1)}, bf16[2,4,48,768]{3,2,1,0:T(8,128)(2,1)}, bf16[2,4,48,512]{3,2,1,0:T(8,128)(2,1)}, bf16[2,4,48,512]{3,2,1,0:T(8,128)(2,1)}) custom-call(s32[1,4]{1,0:T(1,128)} %add_bitcast_fusion.me.refs_0_, bf16[160,3072]{1,0:T(8,128)(2,1)} %get-tuple-element.204.refs_0_.saved, bf16[160,3072]{1,0:T(8,128)(2,1)} %copy-done.20, ...), custom_call_target="tpu_custom_call" | custom-call | flops 1600000000 | bytes 1048576 | tf_op jit(solution)/shard_map/self_grad_kernel/pallas_call | solution.py:796
  182.0 1.5 collective-permute-done.29.out_core
  184.2 2.6 return_kernel.1
  186.8 21.0 %collective-permute-done.38.refs_7_.refs_10_ = bf16[2,4,48,512]{3,2,1,0:T(8,128)(2,1)S(1)} collective-permute-done((bf16[2,4,48,512]{3,2,1,0:T(8,128)(2,1)}, bf16[2,4,48,512]{3,2,1,0:T(8,128)(2,1)S(1)}, u32[]{:S(2)}, u32[]{:S(2)}) %collective-permute-start.38) | collective-permute-done | bytes 393248 | tf_op jit(solution)/shard_map/ppermute | solution.py:834
  209.2 2.7 add_kernel.2
  212.9 2.4 collective-permute-start.40
  216.4 11.4 %collective-permute-done.42.refs_11_ = bf16[4,48,512]{2,1,0:T(8,128)(2,1)S(1)} collective-permute-done((bf16[4,48,512]{2,1,0:T(8,128)(2,1)}, bf16[4,48,512]{2,1,0:T(8,128)(2,1)S(1)}, u32[]{:S(2)}, u32[]{:S(2)}) %collective-permute-start.42) | collective-permute-done | bytes 196640 | tf_op jit(solution)/shard_map/ppermute | solution.py:834
  229.0 3.5 %add_kernel.3 = bf16[4,48,3200]{2,1,0:T(8,128)(2,1)} custom-call(bf16[2,4,48,1152]{3,2,1,0:T(8,128)(2,1)} %get-tuple-element.253.refs_0_, bf16[2,4,48,1152]{3,2,1,0:T(8,128)(2,1)} %copy-done.2, bf16[4,48,1152]{2,1,0:T(8,128)(2,1)} %copy-done.10, bf16[2,4,48,768]{3,2,1,0:T(8,128)(2,1)} %get-tuple-element.260.refs_2_.refs_3_, ...), custom_call_target="tpu_custom_call" | custom-call | tf_op jit(solution)/shard_map/add_kernel/pallas_call | solution.py:822
  232.4 6.0 %all-to-all-start.4 = ((bf16[8,24,3200]{2,1,0:T(8,128)(2,1)}), bf16[8,24,3200]{2,1,0:T(8,128)(2,1)S(1)}, u32[]{:S(2)}, u32[]{:S(2)}) async-start(bf16[8,24,3200]{2,1,0:T(8,128)(2,1)} %bitcast.43), calls=%async_computation.4 | async-start | bytes 2457600 | tf_op jit(solution)/shard_map/all_to_all | solution.py:838
  238.5 2.9 %depth_sum_kernel.1 = (bf16[24,1536]{1,0:T(8,128)(2,1)}, bf16[24,1536]{1,0:T(8,128)(2,1)}, bf16[2,24,1536]{2,1,0:T(8,128)(2,1)}) custom-call(s32[1,4]{1,0:T(1,128)} %add_bitcast_fusion.me.refs_0_, bf16[8,96,1536]{2,1,0:T(8,128)(2,1)} %all-to-all-done.3.got), custom_call_target="tpu_custom_call" | custom-call | flops 800000000 | bytes 1048576 | tf_op jit(solution)/shard_map/depth_sum_kernel/pallas_call | solution.py:796
  243.6 4.6 %collective-permute-done.46.chip = bf16[2,24,1536]{2,1,0:T(8,128)(2,1)S(1)} collective-permute-done((bf16[2,24,1536]{2,1,0:T(8,128)(2,1)}, bf16[2,24,1536]{2,1,0:T(8,128)(2,1)S(1)}, u32[]{:S(2)}, u32[]{:S(2)}) %collective-permute-start.46) | collective-permute-done | bytes 147488 | tf_op jit(solution)/shard_map/ppermute | solution.py:834
  248.3 4.8 %collective-permute-done.43.chip = bf16[2,40,1536]{2,1,0:T(8,128)(2,1)S(1)} collective-permute-done((bf16[2,40,1536]{2,1,0:T(8,128)(2,1)S(1)}, bf16[2,40,1536]{2,1,0:T(8,128)(2,1)S(1)}, u32[]{:S(2)}, u32[]{:S(2)}) %collective-permute-start.43) | collective-permute-done | bytes 245792 | tf_op jit(solution)/shard_map/ppermute | solution.py:834
  253.2 7.4 %image_grad_kernel.1 = bf16[1024,768]{1,0:T(8,128)(2,1)} custom-call(bf16[1024,768]{1,0:T(8,128)(2,1)} %get-tuple-element.236.refs_6_.kv_keep, bf16[1024,768]{1,0:T(8,128)(2,1)} %get-tuple-element.276.kv_send, s32[1,4]{1,0:T(1,128)} %add_bitcast_fusion.me.refs_0_, bf16[4,48,1664]{2,1,0:T(8,128)(2,1)} %bitcast.53, bf16[4,48,1664]{2,1,0:T(8,128)(2,1)} %copy-done.22, ...), custom_call_target="tpu_custom_call" | custom-call | flops 2800000000 | bytes 1048576 | tf_op jit(solution)/shard_map/image_grad_kernel/pallas_call | solution.py:796
  261.3 2.5 unpack_hidden_kernel.1
  264.4 2.0 collect_kernel.1
  266.4 2.5 all-to-all-done.4
  (190 shorter events, 31.8 us)
Async XLA Ops:
  2.5 23.7 %all-to-all-start = ((bf16[8,24,1536]{2,1,0:T(8,128)(2,1)}), bf16[8,24,1536]{2,1,0:T(8,128)(2,1)S(1)}, u32[]{:S(2)}, u32[]{:S(2)}) async-start(bf16[8,24,1536]{2,1,0:T(8,128)(2,1)} %bitcast.60), calls=%async_computation | async-start | bytes 1179648 | tf_op jit(solution)/shard_map/all_to_all | solution.py:838
  12.3 13.8 %collective-permute-start = (bf16[2,80,1536]{2,1,0:T(8,128)(2,1)}, bf16[2,80,1536]{2,1,0:T(8,128)(2,1)S(1)}, u32[]{:S(2)}, u32[]{:S(2)}) collective-permute-start(bf16[2,80,1536]{2,1,0:T(8,128)(2,1)} %get-tuple-element.153), channel_id=1, source_target_pairs={{0,2},{2,0},{1,3},{3,1},{4,6},{6,4},{5,7},{7,5},{8,10},{10,8},{9,1... | collective-permute-start | bytes 1474568 | tf_op jit(solution)/shard_map/ppermute | solution.py:834
  26.2 22.7 %collective-permute-start.5 = (bf16[768,1024]{1,0:T(8,128)(2,1)S(1)}, bf16[768,1024]{1,0:T(8,128)(2,1)}, u32[]{:S(2)}, u32[]{:S(2)}) collective-permute-start(bf16[768,1024]{1,0:T(8,128)(2,1)S(1)} %copy-done.6), channel_id=1, source_target_pairs={{0,1},{1,0},{2,3},{3,2},{4,5},{5,4},{6,7},{7,6},{8,9},{9,8},{10,11... | collective-permute-start | bytes 4718600 | tf_op jit(solution)/shard_map/ppermute | solution.py:834
  26.2 22.7 %all-to-all-start.1 = ((bf16[8,24,1664]{2,1,0:T(8,128)(2,1)}), bf16[8,24,1664]{2,1,0:T(8,128)(2,1)S(1)}, u32[]{:S(2)}, u32[]{:S(2)}) async-start(bf16[8,24,1664]{2,1,0:T(8,128)(2,1)} %bitcast.54), calls=%async_computation.1 | async-start | bytes 1277952 | tf_op jit(solution)/shard_map/all_to_all | solution.py:838
  31.1 3.7 %collective-permute-start.2 = (bf16[80,1536]{1,0:T(8,128)(2,1)S(1)}, bf16[80,1536]{1,0:T(8,128)(2,1)S(1)}, u32[]{:S(2)}, u32[]{:S(2)}) collective-permute-start(bf16[80,1536]{1,0:T(8,128)(2,1)S(1)} %slice_bitcast_fusion), channel_id=1, source_target_pairs={{0,1},{1,0},{2,3},{3,2},{4,5},{5,4},{6,7},{7,6},{8,9},{9,8},{10,11... | collective-permute-start | bytes 737288 | tf_op jit(solution)/shard_map/ppermute | solution.py:834
  31.7 8.2 %collective-permute-start.6 = (bf16[4,48,1536]{2,1,0:T(8,128)(2,1)S(1)}, bf16[4,48,1536]{2,1,0:T(8,128)(2,1)S(1)}, u32[]{:S(2)}, u32[]{:S(2)}) collective-permute-start(bf16[4,48,1536]{2,1,0:T(8,128)(2,1)S(1)} %bitcast.55), channel_id=1, source_target_pairs={{0,1},{1,0},{2,3},{3,2},{4,5},{5,4},{6,7},{7,6},{8,9},{9,8},{10,11... | collective-permute-start | bytes 1769480 | tf_op jit(solution)/shard_map/ppermute | solution.py:834
  31.8 15.7 %collective-permute-start.4 = (bf16[4,48,1536]{2,1,0:T(8,128)(2,1)S(1)}, bf16[4,48,1536]{2,1,0:T(8,128)(2,1)S(1)}, u32[]{:S(2)}, u32[]{:S(2)}) collective-permute-start(bf16[4,48,1536]{2,1,0:T(8,128)(2,1)S(1)} %bitcast.56), channel_id=1, source_target_pairs={{0,2},{2,0},{1,3},{3,1},{4,6},{6,4},{5,7},{7,5},{8,10},{10,8},{9,1... | collective-permute-start | bytes 1769480 | tf_op jit(solution)/shard_map/ppermute | solution.py:834
  33.3 15.5 %collective-permute-start.3 = (bf16[4,48,1536]{2,1,0:T(8,128)(2,1)S(1)}, bf16[4,48,1536]{2,1,0:T(8,128)(2,1)}, u32[]{:S(2)}, u32[]{:S(2)}) collective-permute-start(bf16[4,48,1536]{2,1,0:T(8,128)(2,1)S(1)} %bitcast.57), channel_id=1, source_target_pairs={{0,4},{4,0},{1,5},{5,1},{2,6},{6,2},{3,7},{7,3},{8,12},{12,8},{9,1... | collective-permute-start | bytes 1769480 | tf_op jit(solution)/shard_map/ppermute | solution.py:834
  48.9 8.0 %collective-permute-start.11 = (bf16[4,48,1664]{2,1,0:T(8,128)(2,1)S(1)}, bf16[4,48,1664]{2,1,0:T(8,128)(2,1)S(1)}, u32[]{:S(2)}, u32[]{:S(2)}) collective-permute-start(bf16[4,48,1664]{2,1,0:T(8,128)(2,1)S(1)} %bitcast.48), channel_id=1, source_target_pairs={{0,1},{1,0},{2,3},{3,2},{4,5},{5,4},{6,7},{7,6},{8,9},{9,8},{10,11... | collective-permute-start | bytes 1916936 | tf_op jit(solution)/shard_map/ppermute | solution.py:834
  48.9 16.8 %collective-permute-start.8 = (bf16[4,48,1664]{2,1,0:T(8,128)(2,1)S(1)}, bf16[4,48,1664]{2,1,0:T(8,128)(2,1)S(1)}, u32[]{:S(2)}, u32[]{:S(2)}) collective-permute-start(bf16[4,48,1664]{2,1,0:T(8,128)(2,1)S(1)} %bitcast.49), channel_id=1, source_target_pairs={{0,2},{2,0},{1,3},{3,1},{4,6},{6,4},{5,7},{7,5},{8,10},{10,8},{9,1... | collective-permute-start | bytes 1916936 | tf_op jit(solution)/shard_map/ppermute | solution.py:834
  50.5 16.6 %collective-permute-start.7 = (bf16[4,48,1664]{2,1,0:T(8,128)(2,1)S(1)}, bf16[4,48,1664]{2,1,0:T(8,128)(2,1)}, u32[]{:S(2)}, u32[]{:S(2)}) collective-permute-start(bf16[4,48,1664]{2,1,0:T(8,128)(2,1)S(1)} %bitcast.50), channel_id=1, source_target_pairs={{0,4},{4,0},{1,5},{5,1},{2,6},{6,2},{3,7},{7,3},{8,12},{12,8},{9,1... | collective-permute-start | bytes 1916936 | tf_op jit(solution)/shard_map/ppermute | solution.py:834
  52.0 4.9 %collective-permute-start.10 = (bf16[4,48,1536]{2,1,0:T(8,128)(2,1)}, bf16[4,48,1536]{2,1,0:T(8,128)(2,1)}, u32[]{:S(2)}, u32[]{:S(2)}) collective-permute-start(bf16[4,48,1536]{2,1,0:T(8,128)(2,1)} %copy-done.26), channel_id=1, source_target_pairs={{0,1},{1,0},{2,3},{3,2},{4,5},{5,4},{6,7},{7,6},{8,9},{9,8},{10,11... | collective-permute-start | bytes 1769480 | tf_op jit(solution)/shard_map/ppermute | solution.py:834
  52.0 4.9 %collective-permute-start.9 = (bf16[4,48,1536]{2,1,0:T(8,128)(2,1)}, bf16[4,48,1536]{2,1,0:T(8,128)(2,1)}, u32[]{:S(2)}, u32[]{:S(2)}) collective-permute-start(bf16[4,48,1536]{2,1,0:T(8,128)(2,1)} %collective-permute-done.3.refs_2_), channel_id=1, source_target_pairs={{0,1},{1,0},{2,3},{3,2},{4,5},{5,4},{6,7},{7,6},{8,9},{9,8},{10,11... | collective-permute-start | bytes 1769480 | tf_op jit(solution)/shard_map/ppermute | solution.py:834
  52.5 33.4 %all-to-all-start.2 = ((bf16[4,96,1536]{2,1,0:T(8,128)(2,1)}), bf16[4,96,1536]{2,1,0:T(8,128)(2,1)S(1)}, u32[]{:S(2)}, u32[]{:S(2)}) async-start(bf16[4,96,1536]{2,1,0:T(8,128)(2,1)} %bitcast.47), calls=%async_computation.2 | async-start | bytes 2359296 | tf_op jit(solution)/shard_map/all_to_all | solution.py:838
  67.1 17.3 %collective-permute-start.15 = (bf16[4,48,1664]{2,1,0:T(8,128)(2,1)}, bf16[4,48,1664]{2,1,0:T(8,128)(2,1)S(1)}, u32[]{:S(2)}, u32[]{:S(2)}) collective-permute-start(bf16[4,48,1664]{2,1,0:T(8,128)(2,1)} %collective-permute-done.7.refs_10_.refs_2_.refs_3_), channel_id=1, source_target_pairs={{0,1},{1,0},{2,3},{3,2},{4,5},{5,4},{6,7},{7,6},{8,9},{9,8},{10,11... | collective-permute-start | bytes 1916936 | tf_op jit(solution)/shard_map/ppermute | solution.py:834
  67.1 17.3 %collective-permute-start.14 = (bf16[4,48,1664]{2,1,0:T(8,128)(2,1)S(1)}, bf16[4,48,1664]{2,1,0:T(8,128)(2,1)S(1)}, u32[]{:S(2)}, u32[]{:S(2)}) collective-permute-start(bf16[4,48,1664]{2,1,0:T(8,128)(2,1)S(1)} %collective-permute-done.8.refs_9_.refs_1_.refs_2_), channel_id=1, source_target_pairs={{0,1},{1,0},{2,3},{3,2},{4,5},{5,4},{6,7},{7,6},{8,9},{9,8},{10,11... | collective-permute-start | bytes 1916936 | tf_op jit(solution)/shard_map/ppermute | solution.py:834
  67.6 16.8 %collective-permute-start.13 = (bf16[4,48,1664]{2,1,0:T(8,128)(2,1)S(1)}, bf16[4,48,1664]{2,1,0:T(8,128)(2,1)}, u32[]{:S(2)}, u32[]{:S(2)}) collective-permute-start(bf16[4,48,1664]{2,1,0:T(8,128)(2,1)S(1)} %collective-permute-done.8.refs_9_.refs_1_.refs_2_), channel_id=1, source_target_pairs={{0,4},{4,0},{1,5},{5,1},{2,6},{6,2},{3,7},{7,3},{8,12},{12,8},{9,1... | collective-permute-start | bytes 1916936 | tf_op jit(solution)/shard_map/ppermute | solution.py:834
  69.1 15.3 %collective-permute-start.12 = (bf16[4,48,1536]{2,1,0:T(8,128)(2,1)}, bf16[4,48,1536]{2,1,0:T(8,128)(2,1)}, u32[]{:S(2)}, u32[]{:S(2)}) collective-permute-start(bf16[4,48,1536]{2,1,0:T(8,128)(2,1)} %collective-permute-done.3.refs_2_), channel_id=1, source_target_pairs={{0,2},{2,0},{1,3},{3,1},{4,6},{6,4},{5,7},{7,5},{8,10},{10,8},{9,1... | collective-permute-start | bytes 1769480 | tf_op jit(solution)/shard_map/ppermute | solution.py:834
  85.4 17.5 %collective-permute-start.22 = (bf16[160,768]{1,0:T(8,128)(2,1)S(1)}, bf16[160,768]{1,0:T(8,128)(2,1)}, u32[]{:S(2)}, u32[]{:S(2)}) collective-permute-start(bf16[160,768]{1,0:T(8,128)(2,1)S(1)} %copy-done.30), channel_id=1, source_target_pairs={{0,2},{2,0},{1,3},{3,1},{4,6},{6,4},{5,7},{7,5},{8,10},{10,8},{9,1... | collective-permute-start | bytes 737288 | tf_op jit(solution)/shard_map/ppermute | solution.py:834
  85.9 27.3 %collective-permute-start.24 = (bf16[4,96,1536]{2,1,0:T(8,128)(2,1)S(1)}, bf16[4,96,1536]{2,1,0:T(8,128)(2,1)S(1)}, u32[]{:S(2)}, u32[]{:S(2)}) collective-permute-start(bf16[4,96,1536]{2,1,0:T(8,128)(2,1)S(1)} %all-to-all-done.2.refs_8_), channel_id=1, source_target_pairs={{0,4},{4,0},{1,5},{5,1},{2,6},{6,2},{3,7},{7,3},{8,12},{12,8},{9,1... | collective-permute-start | bytes 3538952 | tf_op jit(solution)/shard_map/ppermute | solution.py:834
  102.3 8.3 %collective-permute-start.19 = (bf16[160,768]{1,0:T(8,128)(2,1)}, bf16[160,768]{1,0:T(8,128)(2,1)S(1)}, u32[]{:S(2)}, u32[]{:S(2)}) collective-permute-start(bf16[160,768]{1,0:T(8,128)(2,1)} %get-tuple-element.195.refs_0_), channel_id=1, source_target_pairs={{0,2},{2,0},{1,3},{3,1},{4,6},{6,4},{5,7},{7,5},{8,10},{10,8},{9,1... | collective-permute-start | bytes 737288 | tf_op jit(solution)/shard_map/ppermute | solution.py:834
  102.9 7.7 %collective-permute-start.21 = (bf16[160,768]{1,0:T(8,128)(2,1)S(1)}, bf16[160,768]{1,0:T(8,128)(2,1)S(1)}, u32[]{:S(2)}, u32[]{:S(2)}) collective-permute-start(bf16[160,768]{1,0:T(8,128)(2,1)S(1)} %copy-done.30), channel_id=1, source_target_pairs={{0,1},{1,0},{2,3},{3,2},{4,5},{5,4},{6,7},{7,6},{8,9},{9,8},{10,11... | collective-permute-start | bytes 737288 | tf_op jit(solution)/shard_map/ppermute | solution.py:834
  102.9 8.2 %collective-permute-start.23 = (bf16[160,768]{1,0:T(8,128)(2,1)}, bf16[160,768]{1,0:T(8,128)(2,1)S(1)}, u32[]{:S(2)}, u32[]{:S(2)}) collective-permute-start(bf16[160,768]{1,0:T(8,128)(2,1)} %collective-permute-done.22.refs_6_), channel_id=1, source_target_pairs={{0,1},{1,0},{2,3},{3,2},{4,5},{5,4},{6,7},{7,6},{8,9},{9,8},{10,11... | collective-permute-start | bytes 737288 | tf_op jit(solution)/shard_map/ppermute | solution.py:834
  103.4 7.7 %collective-permute-start.18 = (bf16[160,768]{1,0:T(8,128)(2,1)}, bf16[160,768]{1,0:T(8,128)(2,1)S(1)}, u32[]{:S(2)}, u32[]{:S(2)}) collective-permute-start(bf16[160,768]{1,0:T(8,128)(2,1)} %get-tuple-element.195.refs_0_), channel_id=1, source_target_pairs={{0,1},{1,0},{2,3},{3,2},{4,5},{5,4},{6,7},{7,6},{8,9},{9,8},{10,11... | collective-permute-start | bytes 737288 | tf_op jit(solution)/shard_map/ppermute | solution.py:834
  110.6 22.5 %collective-permute-start.28 = (bf16[160,3072]{1,0:T(8,128)(2,1)}, bf16[160,3072]{1,0:T(8,128)(2,1)S(1)}, u32[]{:S(2)}, u32[]{:S(2)}) collective-permute-start(bf16[160,3072]{1,0:T(8,128)(2,1)} %get-tuple-element.204.refs_0_.saved), channel_id=1, source_target_pairs={{0,1},{1,0},{2,3},{3,2},{4,5},{5,4},{6,7},{7,6},{8,9},{9,8},{10,11... | collective-permute-start | bytes 2949128 | tf_op jit(solution)/shard_map/ppermute | solution.py:834
  123.1 10.1 %collective-permute-start.27 = (bf16[160,768]{1,0:T(8,128)(2,1)}, bf16[160,768]{1,0:T(8,128)(2,1)S(1)}, u32[]{:S(2)}, u32[]{:S(2)}) collective-permute-start(bf16[160,768]{1,0:T(8,128)(2,1)} %get-tuple-element.201), channel_id=1, source_target_pairs={{0,1},{1,0},{2,3},{3,2},{4,5},{5,4},{6,7},{7,6},{8,9},{9,8},{10,11... | collective-permute-start | bytes 737288 | tf_op jit(solution)/shard_map/ppermute | solution.py:834
  125.8 8.1 %collective-permute-start.26 = (bf16[160,768]{1,0:T(8,128)(2,1)S(1)}, bf16[160,768]{1,0:T(8,128)(2,1)S(1)}, u32[]{:S(2)}, u32[]{:S(2)}) collective-permute-start(bf16[160,768]{1,0:T(8,128)(2,1)S(1)} %combine_kernel.2), channel_id=1, source_target_pairs={{0,2},{2,0},{1,3},{3,1},{4,6},{6,4},{5,7},{7,5},{8,10},{10,8},{9,1... | collective-permute-start | bytes 737288 | tf_op jit(solution)/shard_map/ppermute | solution.py:834
  134.6 93.5 %all-to-all-start.3 = ((bf16[8,96,1536]{2,1,0:T(8,128)(2,1)}), bf16[8,96,1536]{2,1,0:T(8,128)(2,1)}, u32[]{:S(2)}, u32[]{:S(2)}) async-start(bf16[8,96,1536]{2,1,0:T(8,128)(2,1)} %bitcast.44), calls=%async_computation.3 | async-start | bytes 4718592 | tf_op jit(solution)/shard_map/all_to_all | solution.py:838
  139.9 12.0 %collective-permute-start.30 = (bf16[160,768]{1,0:T(8,128)(2,1)S(1)}, bf16[160,768]{1,0:T(8,128)(2,1)S(1)}, u32[]{:S(2)}, u32[]{:S(2)}) collective-permute-start(bf16[160,768]{1,0:T(8,128)(2,1)S(1)} %copy-done.36), channel_id=1, source_target_pairs={{0,1},{1,0},{2,3},{3,2},{4,5},{5,4},{6,7},{7,6},{8,9},{9,8},{10,11... | collective-permute-start | bytes 737288 | tf_op jit(solution)/shard_map/ppermute | solution.py:834
  151.8 10.0 %collective-permute-start.32 = (bf16[1024,768]{1,0:T(8,128)(2,1)}, bf16[1024,768]{1,0:T(8,128)(2,1)S(1)}, u32[]{:S(2)}, u32[]{:S(2)}) collective-permute-start(bf16[1024,768]{1,0:T(8,128)(2,1)} %get-tuple-element.276.kv_send), channel_id=1, source_target_pairs={{0,1},{1,0},{2,3},{3,2},{4,5},{5,4},{6,7},{7,6},{8,9},{9,8},{10,11... | collective-permute-start | bytes 4718600 | tf_op jit(solution)/shard_map/ppermute | solution.py:834
  152.4 9.4 %collective-permute-start.31 = (bf16[160,1152]{1,0:T(8,128)(2,1)}, bf16[160,1152]{1,0:T(8,128)(2,1)S(1)}, u32[]{:S(2)}, u32[]{:S(2)}) collective-permute-start(bf16[160,1152]{1,0:T(8,128)(2,1)} %get-tuple-element.226), channel_id=1, source_target_pairs={{0,1},{1,0},{2,3},{3,2},{4,5},{5,4},{6,7},{7,6},{8,9},{9,8},{10,11... | collective-permute-start | bytes 1105928 | tf_op jit(solution)/shard_map/ppermute | solution.py:834
  152.5 9.3 %collective-permute-start.33 = (bf16[160,768]{1,0:T(8,128)(2,1)S(1)}, bf16[160,768]{1,0:T(8,128)(2,1)S(1)}, u32[]{:S(2)}, u32[]{:S(2)}) collective-permute-start(bf16[160,768]{1,0:T(8,128)(2,1)S(1)} %combine_kernel.3), channel_id=1, source_target_pairs={{0,2},{2,0},{1,3},{3,1},{4,6},{6,4},{5,7},{7,5},{8,10},{10,8},{9,1... | collective-permute-start | bytes 737288 | tf_op jit(solution)/shard_map/ppermute | solution.py:834
  161.8 11.1 %collective-permute-start.34 = (bf16[160,1152]{1,0:T(8,128)(2,1)}, bf16[160,1152]{1,0:T(8,128)(2,1)S(1)}, u32[]{:S(2)}, u32[]{:S(2)}) collective-permute-start(bf16[160,1152]{1,0:T(8,128)(2,1)} %get-tuple-element.242), channel_id=1, source_target_pairs={{0,1},{1,0},{2,3},{3,2},{4,5},{5,4},{6,7},{7,6},{8,9},{9,8},{10,11... | collective-permute-start | bytes 1105928 | tf_op jit(solution)/shard_map/ppermute | solution.py:834
  172.9 34.9 %collective-permute-start.35 = (bf16[2,4,48,1152]{3,2,1,0:T(8,128)(2,1)}, bf16[2,4,48,1152]{3,2,1,0:T(8,128)(2,1)S(1)}, u32[]{:S(2)}, u32[]{:S(2)}) collective-permute-start(bf16[2,4,48,1152]{3,2,1,0:T(8,128)(2,1)} %get-tuple-element.254), channel_id=1, source_target_pairs={{0,4},{4,0},{1,5},{5,1},{2,6},{6,2},{3,7},{7,3},{8,12},{12,8},{9,1... | collective-permute-start | bytes 2654216 | tf_op jit(solution)/shard_map/ppermute | solution.py:834
  179.3 28.5 %collective-permute-start.37 = (bf16[2,4,48,768]{3,2,1,0:T(8,128)(2,1)}, bf16[2,4,48,768]{3,2,1,0:T(8,128)(2,1)S(1)}, u32[]{:S(2)}, u32[]{:S(2)}) collective-permute-start(bf16[2,4,48,768]{3,2,1,0:T(8,128)(2,1)} %get-tuple-element.256), channel_id=1, source_target_pairs={{0,2},{2,0},{1,3},{3,1},{4,6},{6,4},{5,7},{7,5},{8,10},{10,8},{9,1... | collective-permute-start | bytes 1769480 | tf_op jit(solution)/shard_map/ppermute | solution.py:834
  180.4 27.5 %collective-permute-start.36 = (bf16[2,4,48,768]{3,2,1,0:T(8,128)(2,1)S(1)}, bf16[2,4,48,768]{3,2,1,0:T(8,128)(2,1)S(1)}, u32[]{:S(2)}, u32[]{:S(2)}) collective-permute-start(bf16[2,4,48,768]{3,2,1,0:T(8,128)(2,1)S(1)} %copy-done.27), channel_id=1, source_target_pairs={{0,2},{2,0},{1,3},{3,1},{4,6},{6,4},{5,7},{7,5},{8,10},{10,8},{9,1... | collective-permute-start | bytes 1769480 | tf_op jit(solution)/shard_map/ppermute | solution.py:834
  181.4 26.4 %collective-permute-start.38 = (bf16[2,4,48,512]{3,2,1,0:T(8,128)(2,1)}, bf16[2,4,48,512]{3,2,1,0:T(8,128)(2,1)S(1)}, u32[]{:S(2)}, u32[]{:S(2)}) collective-permute-start(bf16[2,4,48,512]{3,2,1,0:T(8,128)(2,1)} %get-tuple-element.257), channel_id=1, source_target_pairs={{0,4},{4,0},{1,5},{5,1},{2,6},{6,2},{3,7},{7,3},{8,12},{12,8},{9,1... | collective-permute-start | bytes 1179656 | tf_op jit(solution)/shard_map/ppermute | solution.py:834
  211.9 16.2 %collective-permute-start.39 = (bf16[4,48,1152]{2,1,0:T(8,128)(2,1)}, bf16[4,48,1152]{2,1,0:T(8,128)(2,1)S(1)}, u32[]{:S(2)}, u32[]{:S(2)}) collective-permute-start(bf16[4,48,1152]{2,1,0:T(8,128)(2,1)} %get-tuple-element.266), channel_id=1, source_target_pairs={{0,2},{2,0},{1,3},{3,1},{4,6},{6,4},{5,7},{7,5},{8,10},{10,8},{9,1... | collective-permute-start | bytes 1327112 | tf_op jit(solution)/shard_map/ppermute | solution.py:834
  212.9 14.8 %collective-permute-start.40 = (bf16[4,48,768]{2,1,0:T(8,128)(2,1)}, bf16[4,48,768]{2,1,0:T(8,128)(2,1)S(1)}, u32[]{:S(2)}, u32[]{:S(2)}) collective-permute-start(bf16[4,48,768]{2,1,0:T(8,128)(2,1)} %get-tuple-element.267), channel_id=1, source_target_pairs={{0,4},{4,0},{1,5},{5,1},{2,6},{6,2},{3,7},{7,3},{8,12},{12,8},{9,1... | collective-permute-start | bytes 884744 | tf_op jit(solution)/shard_map/ppermute | solution.py:834
  215.3 12.8 %collective-permute-start.41 = (bf16[4,48,768]{2,1,0:T(8,128)(2,1)}, bf16[4,48,768]{2,1,0:T(8,128)(2,1)S(1)}, u32[]{:S(2)}, u32[]{:S(2)}) collective-permute-start(bf16[4,48,768]{2,1,0:T(8,128)(2,1)} %get-tuple-element.268), channel_id=1, source_target_pairs={{0,4},{4,0},{1,5},{5,1},{2,6},{6,2},{3,7},{7,3},{8,12},{12,8},{9,1... | collective-permute-start | bytes 884744 | tf_op jit(solution)/shard_map/ppermute | solution.py:834
  215.4 12.4 %collective-permute-start.42 = (bf16[4,48,512]{2,1,0:T(8,128)(2,1)}, bf16[4,48,512]{2,1,0:T(8,128)(2,1)S(1)}, u32[]{:S(2)}, u32[]{:S(2)}) collective-permute-start(bf16[4,48,512]{2,1,0:T(8,128)(2,1)} %get-tuple-element.269), channel_id=1, source_target_pairs={{0,2},{2,0},{1,3},{3,1},{4,6},{6,4},{5,7},{7,5},{8,10},{10,8},{9,1... | collective-permute-start | bytes 589832 | tf_op jit(solution)/shard_map/ppermute | solution.py:834
  232.4 36.5 %all-to-all-start.4 = ((bf16[8,24,3200]{2,1,0:T(8,128)(2,1)}), bf16[8,24,3200]{2,1,0:T(8,128)(2,1)S(1)}, u32[]{:S(2)}, u32[]{:S(2)}) async-start(bf16[8,24,3200]{2,1,0:T(8,128)(2,1)} %bitcast.43), calls=%async_computation.4 | async-start | bytes 2457600 | tf_op jit(solution)/shard_map/all_to_all | solution.py:838
  241.4 6.9 %collective-permute-start.46 = (bf16[2,24,1536]{2,1,0:T(8,128)(2,1)}, bf16[2,24,1536]{2,1,0:T(8,128)(2,1)S(1)}, u32[]{:S(2)}, u32[]{:S(2)}) collective-permute-start(bf16[2,24,1536]{2,1,0:T(8,128)(2,1)} %get-tuple-element.288), channel_id=1, source_target_pairs={{0,2},{2,0},{1,3},{3,1},{4,6},{6,4},{5,7},{7,5},{8,10},{10,8},{9,1... | collective-permute-start | bytes 442376 | tf_op jit(solution)/shard_map/ppermute | solution.py:834
  242.4 21.3 %collective-permute-start.44 = (bf16[40,1536]{1,0:T(8,128)(2,1)S(1)}, bf16[40,1536]{1,0:T(8,128)(2,1)S(1)}, u32[]{:S(2)}, u32[]{:S(2)}) collective-permute-start(bf16[40,1536]{1,0:T(8,128)(2,1)S(1)} %copy-done.46), channel_id=1, source_target_pairs={{0,1},{1,0},{2,3},{3,2},{4,5},{5,4},{6,7},{7,6},{8,9},{9,8},{10,11... | collective-permute-start | bytes 368648 | tf_op jit(solution)/shard_map/ppermute | solution.py:834
  242.7 10.5 %collective-permute-start.43 = (bf16[2,40,1536]{2,1,0:T(8,128)(2,1)S(1)}, bf16[2,40,1536]{2,1,0:T(8,128)(2,1)S(1)}, u32[]{:S(2)}, u32[]{:S(2)}) collective-permute-start(bf16[2,40,1536]{2,1,0:T(8,128)(2,1)S(1)} %copy-done.32), channel_id=1, source_target_pairs={{0,2},{2,0},{1,3},{3,1},{4,6},{6,4},{5,7},{7,5},{8,10},{10,8},{9,1... | collective-permute-start | bytes 737288 | tf_op jit(solution)/shard_map/ppermute | solution.py:834
  243.6 17.0 %collective-permute-start.47 = (bf16[24,1536]{1,0:T(8,128)(2,1)}, bf16[24,1536]{1,0:T(8,128)(2,1)S(1)}, u32[]{:S(2)}, u32[]{:S(2)}) collective-permute-start(bf16[24,1536]{1,0:T(8,128)(2,1)} %get-tuple-element.289), channel_id=1, source_target_pairs={{0,1},{1,0},{2,3},{3,2},{4,5},{5,4},{6,7},{7,6},{8,9},{9,8},{10,11... | collective-permute-start | bytes 221192 | tf_op jit(solution)/shard_map/ppermute | solution.py:834
  248.3 12.4 %collective-permute-start.48 = (bf16[24,1536]{1,0:T(8,128)(2,1)S(1)}, bf16[24,1536]{1,0:T(8,128)(2,1)S(1)}, u32[]{:S(2)}, u32[]{:S(2)}) collective-permute-start(bf16[24,1536]{1,0:T(8,128)(2,1)S(1)} %slice_bitcast_fusion.2), channel_id=1, source_target_pairs={{0,1},{1,0},{2,3},{3,2},{4,5},{5,4},{6,7},{7,6},{8,9},{9,8},{10,11... | collective-permute-start | bytes 221192 | tf_op jit(solution)/shard_map/ppermute | solution.py:834
  253.1 10.6 %collective-permute-start.45 = (bf16[40,1536]{1,0:T(8,128)(2,1)S(1)}, bf16[40,1536]{1,0:T(8,128)(2,1)S(1)}, u32[]{:S(2)}, u32[]{:S(2)}) collective-permute-start(bf16[40,1536]{1,0:T(8,128)(2,1)S(1)} %slice_bitcast_fusion.1), channel_id=1, source_target_pairs={{0,1},{1,0},{2,3},{3,2},{4,5},{5,4},{6,7},{7,6},{8,9},{9,8},{10,11... | collective-permute-start | bytes 368648 | tf_op jit(solution)/shard_map/ppermute | solution.py:834
  (57 other events, 322.9 us)

commit v3 on v2

--- a/solution.py
+++ b/solution.py
@@ -774,6 +774,15 @@
         first += count
 
 
+def last_add_kernel(so_far, *refs):
+    out, at = refs[-1], 0
+    for ref in refs[:-1]:
+        lanes = slice(at, at + ref.shape[-1])
+        for z in range(out.shape[0]):
+            out[z, :, lanes] = (wide(so_far[z, :, lanes]) + wide(ref[z])).astype(BF)
+        at += ref.shape[-1]
+
+
 VM = pl.BlockSpec(memory_space=pltpu.VMEM)
 SM = pl.BlockSpec(memory_space=pltpu.SMEM)
 HB = pl.BlockSpec(memory_space=pl.ANY)
@@ -1112,15 +1121,15 @@
         *([(near, 1), (got, 1)] for near, got in ((kv_0, kv_1), (mix_0, mix_1), (q_0, q_1), (v_0, v_1)))
     )
     kv_2, mix_2, q_2, v_2 = flip(kv_2, "y"), flip(mix_2, "x"), flip(q_2, "x"), flip(v_2, "y")
-    kv_2, mix_2, q_2, v_2, hidden_got, kv_send, chip = tie(
-        kv_2, mix_2, q_2, v_2, hidden_got, kv_send, chip
-    )
-    (got,) = add_up(
-        [(kv_0, 0), (kv_1, 0), kv_2],
-        [(mix_0, 0), (mix_1, 0), mix_2],
-        [(q_0, 0), (q_1, 0), q_2],
-        [(v_0, 0), (v_1, 0), v_2],
+    (so_far,) = add_up(
+        *([(near, 0), (got, 0)] for near, got in ((kv_0, kv_1), (mix_0, mix_1), (q_0, q_1), (v_0, v_1))),
         joined=True,
+    )
+    kv_2, mix_2, q_2, v_2, hidden_got, kv_send, chip, so_far = tie(
+        kv_2, mix_2, q_2, v_2, hidden_got, kv_send, chip, so_far
+    )
+    (got,) = run(
+        last_add_kernel, [(so_far.shape, BF)], [VM] * 5, [], so_far, kv_2, mix_2, q_2, v_2
     )
     got = owned(got, 2, ("z", "c"))
     chip = flip(chip, "y")

time: 274 us -> 275 us (level)
  Pallas kernels: 100 us -> 104 us
  waiting for transfers between devices: 99.7 us -> 96.8 us
    pallas_call x20 -> x21, Pallas kernels: 94.2 us -> 98.1 us  [run(): pl.pallas_call(kernel, out_shape=[jax.ShapeDtypeStruct(s, t) for s, t in...]
    ppermute x49, waiting for transfers between devices: 97.1 us -> 94.2 us  [flip(): return lax.ppermute(value, axis, [(0, 1), (1, 0)])]
    unnamed x102 -> x98, local copies, waits for them, and re-layouts: 10 us -> 10.3 us
  transfers between devices with their start and end apart: 54 -> 54, of which waited for: 21 -> 21; matrix products, arithmetic and copies ran while one was open for 0% -> 0% of each run, Pallas kernels for 35% -> 36%
where the time goes in v3:
time: 275 us; the launch traced here: 271 us
  Pallas kernels  104 us (38%)
  waiting for transfers between devices  96.8 us (35%)
  starting transfers between devices  57.2 us (21%)
  local copies, waits for them, and re-layouts  11.5 us (4%)
    pallas_call x21, Pallas kernels, run(): pl.pallas_call(kernel, out_shape=[jax.ShapeDtypeStruct(s, t) for s, t in...  98.1 us
    ppermute x49, waiting for transfers between devices, flip(): return lax.ppermute(value, axis, [(0, 1), (1, 0)])  94.2 us
    ppermute x49, starting transfers between devices, flip(): return lax.ppermute(value, axis, [(0, 1), (1, 0)])  30.3 us
    all_to_all x5, starting transfers between devices, swap_all(): return lax.all_to_all(value, axes, split_axis=0, concat_axis=0, tiled=True)  26.8 us
    unnamed x98, local copies, waits for them, and re-layouts  10.3 us
    pallas_call x2, Pallas kernels, add_up(): pl.pallas_call(functools.partial(add_kernel, [len(terms) for terms in sum...  5.62 us
  transfers between devices with their start and end apart: 54, of which 21 were waited for; matrix products, arithmetic and copies ran while one was open for 0% of the time, Pallas kernels for 36%

profile of v3, /device:TPU:0, one launch (start us, length us, event | category | flops | bytes accessed | tf_op | source)
XLA Modules:
  0.0 271.4 jit_solution(5764784969824200060)
XLA Ops:
  0.6 1.8 pack_self_kernel.1
  2.5 6.3 %all-to-all-start = ((bf16[8,24,1536]{2,1,0:T(8,128)(2,1)}), bf16[8,24,1536]{2,1,0:T(8,128)(2,1)S(1)}, u32[]{:S(2)}, u32[]{:S(2)}) async-start(bf16[8,24,1536]{2,1,0:T(8,128)(2,1)} %bitcast.60), calls=%async_computation | async-start | bytes 1179648 | tf_op jit(solution)/shard_map/all_to_all | solution.py:847
  9.4 2.9 %pack_group_kernel.1 = (bf16[80,1536]{1,0:T(8,128)(2,1)}, bf16[80,1536]{1,0:T(8,128)(2,1)}, bf16[2,80,1536]{2,1,0:T(8,128)(2,1)}) custom-call(s32[1,4]{1,0:T(1,128)} %add_bitcast_fusion.me.refs_0_, bf16[576,128]{1,0:T(8,128)(2,1)} %bitcast.63, bf16[576,128]{1,0:T(8,128)(2,1)} %bitcast.64, bf16[4,40,768]{2,1,0:T(8,128)(2,1)} %bitcast.61, ...), custom_call_target="tpu_custom_call" | custom-call | flops 800000000 | bytes 1048576 | tf_op jit(solution)/shard_map/pack_group_kernel/pallas_call | solution.py:805
  12.3 1.5 collective-permute-start
  14.4 3.2 %transpose_kernel.1.refs_4_ = bf16[768,1024]{1,0:T(8,128)(2,1)} custom-call(bf16[1024,768]{1,0:T(8,128)(2,1)} %bitcast.45), custom_call_target="tpu_custom_call" | custom-call | flops 800000000 | bytes 1048576 | tf_op jit(solution)/shard_map/transpose_kernel/pallas_call | solution.py:805
  17.5 1.9 pack_cross_kernel.1
  19.5 6.6 %collective-permute-done.chip = bf16[2,80,1536]{2,1,0:T(8,128)(2,1)S(1)} collective-permute-done((bf16[2,80,1536]{2,1,0:T(8,128)(2,1)}, bf16[2,80,1536]{2,1,0:T(8,128)(2,1)S(1)}, u32[]{:S(2)}, u32[]{:S(2)}) %collective-permute-start) | collective-permute-done | bytes 491552 | tf_op jit(solution)/shard_map/ppermute | solution.py:843
  26.2 4.8 %all-to-all-start.1 = ((bf16[8,24,1664]{2,1,0:T(8,128)(2,1)}), bf16[8,24,1664]{2,1,0:T(8,128)(2,1)S(1)}, u32[]{:S(2)}, u32[]{:S(2)}) async-start(bf16[8,24,1664]{2,1,0:T(8,128)(2,1)} %bitcast.54), calls=%async_computation.1 | async-start | bytes 1277952 | tf_op jit(solution)/shard_map/all_to_all | solution.py:847
  31.7 1.5 collective-permute-start.4
  33.3 1.5 collective-permute-start.3
  34.8 1.7 collective-permute-done.1.core
  37.2 2.9 %spread_kernel.1 = (bf16[4,4,24,1536]{3,2,1,0:T(8,128)(2,1)}, bf16[160,768]{1,0:T(8,128)(2,1)}, bf16[160,768]{1,0:T(8,128)(2,1)}) custom-call(s32[1,4]{1,0:T(1,128)} %add_bitcast_fusion.me.refs_0_, s32[1,160]{1,0:T(1,128)} %arr.3, bf16[80,1536]{1,0:T(8,128)(2,1)} %get-tuple-element.153.near, bf16[2,80,1536]{2,1,0:T(8,128)(2,1)} %copy-done.15, ...), custom_call_target="tpu_custom_call" | custom-call | flops 1200000000 | bytes 1048576 | tf_op jit(solution)/shard_map/spread_kernel/pallas_call | solution.py:805
  40.1 7.3 %collective-permute-done.4.refs_1_ = bf16[4,48,1536]{2,1,0:T(8,128)(2,1)S(1)} collective-permute-done((bf16[4,48,1536]{2,1,0:T(8,128)(2,1)S(1)}, bf16[4,48,1536]{2,1,0:T(8,128)(2,1)S(1)}, u32[]{:S(2)}, u32[]{:S(2)}) %collective-permute-start.4) | collective-permute-done | bytes 589856 | tf_op jit(solution)/shard_map/ppermute | solution.py:843
  48.9 1.6 collective-permute-start.8
  50.5 1.5 collective-permute-start.7
  52.5 4.3 %all-to-all-start.2 = ((bf16[4,96,1536]{2,1,0:T(8,128)(2,1)}), bf16[4,96,1536]{2,1,0:T(8,128)(2,1)S(1)}, u32[]{:S(2)}, u32[]{:S(2)}) async-start(bf16[4,96,1536]{2,1,0:T(8,128)(2,1)} %bitcast.47), calls=%async_computation.2 | async-start | bytes 2359296 | tf_op jit(solution)/shard_map/all_to_all | solution.py:847
  56.9 8.8 %collective-permute-done.8.refs_9_.refs_1_.refs_2_ = bf16[4,48,1664]{2,1,0:T(8,128)(2,1)S(1)} collective-permute-done((bf16[4,48,1664]{2,1,0:T(8,128)(2,1)S(1)}, bf16[4,48,1664]{2,1,0:T(8,128)(2,1)S(1)}, u32[]{:S(2)}, u32[]{:S(2)}) %collective-permute-start.8) | collective-permute-done | bytes 639008 | tf_op jit(solution)/shard_map/ppermute | solution.py:843
  65.7 1.3 collective-permute-done.7.refs_10_.refs_2_.refs_3_
  67.5 1.5 collective-permute-start.13
  69.5 14.8 %collective-permute-done.12.refs_3_ = bf16[4,48,1536]{2,1,0:T(8,128)(2,1)} collective-permute-done((bf16[4,48,1536]{2,1,0:T(8,128)(2,1)}, bf16[4,48,1536]{2,1,0:T(8,128)(2,1)}, u32[]{:S(2)}, u32[]{:S(2)}) %collective-permute-start.12) | collective-permute-done | bytes 589856 | tf_op jit(solution)/shard_map/ppermute | solution.py:843
  87.7 14.6 %forward_kernel.1 = (f32[11,768]{1,0:T(8,128)}, bf16[160,2304]{1,0:T(8,128)(2,1)}, bf16[3,640,160]{2,1,0:T(8,128)(2,1)}, bf16[160,3072]{1,0:T(8,128)(2,1)}, f32[...) custom-call(s32[1,4]{1,0:T(1,128)} %lens.3, ...), custom_call_target="tpu_custom_call" | custom-call | flops 13200000000 | bytes 20971520 | tf_op jit(solution)/shard_map/forward_kernel/pallas_call | solution.py:805
  103.4 7.2 %collective-permute-done.19.refs_2_ = bf16[160,768]{1,0:T(8,128)(2,1)S(1)} collective-permute-done((bf16[160,768]{1,0:T(8,128)(2,1)}, bf16[160,768]{1,0:T(8,128)(2,1)S(1)}, u32[]{:S(2)}, u32[]{:S(2)}) %collective-permute-start.19) | collective-permute-done | bytes 245792 | tf_op jit(solution)/shard_map/ppermute | solution.py:843
  114.2 8.8 %mlp_kernel.1 = (f32[160,768]{1,0:T(8,128)}, bf16[160,768]{1,0:T(8,128)(2,1)}, bf16[160,768]{1,0:T(8,128)(2,1)}, bf16[160,768]{1,0:T(8,128)(2,1)}, f32[160,768]{...) custom-call(s32[1,4]{1,0:T(1,128)} %add_bitcast_fusion.me.refs_0_, ...), custom_call_target="tpu_custom_call" | custom-call | flops 3600000000 | bytes 1048576 | tf_op jit(solution)/shard_map/mlp_kernel/pallas_call | solution.py:805
  123.6 1.2 collective-permute-done.25.far
  125.8 1.6 collective-permute-start.26
  127.4 5.7 %hidden_grad_kernel.1 = bf16[768,1536]{1,0:T(8,128)(2,1)} custom-call(bf16[160,768]{1,0:T(8,128)(2,1)} %get-tuple-element.196.refs_0_, bf16[160,768]{1,0:T(8,128)(2,1)} %copy-done.37, bf16[160,768]{1,0:T(8,128)(2,1)} %copy-done.34, bf16[160,768]{1,0:T(8,128)(2,1)} %copy-done.38, bf16[160,768]{1,0:T(8,128)(2,1)} %get-tuple-element.197.refs_4_.grad_slot, ...), custom_call_target="tpu_custom_call" | custom-call | flops 2400000000 | bytes 1048576 | tf_op jit(solution)/shard_map/hidden_grad_kernel/pallas_call | solution.py:805
  134.6 5.3 %all-to-all-start.3 = ((bf16[8,96,1536]{2,1,0:T(8,128)(2,1)}), bf16[8,96,1536]{2,1,0:T(8,128)(2,1)S(1)}, u32[]{:S(2)}, u32[]{:S(2)}) async-start(bf16[8,96,1536]{2,1,0:T(8,128)(2,1)} %bitcast.44), calls=%async_computation.3 | async-start | bytes 4718592 | tf_op jit(solution)/shard_map/all_to_all | solution.py:847
  139.9 11.9 %cross_back_kernel.1 = (f32[160,768]{1,0:T(8,128)}, f32[66,128]{1,0:T(8,128)}, bf16[160,1152]{1,0:T(8,128)(2,1)}, bf16[160,1152]{1,0:T(8,128)(2,1)}, bf16[1024,7...) custom-call(s32[1,4]{1,0:T(1,128)} %lens.3, s32[1,4]{1,0:T(1,128)} %add_bitcast_fusion.me.refs_0_, ...), custom_call_target="tpu_custom_call" | custom-call | flops 4800000000 | bytes 1048576 | tf_op jit(solution)/shard_map/cross_back_kernel/pallas_call | solution.py:805
  153.6 8.2 %self_back_kernel.1 = (bf16[160,768]{1,0:T(8,128)(2,1)}, f32[66,128]{1,0:T(8,128)}, bf16[160,1152]{1,0:T(8,128)(2,1)}, bf16[160,1152]{1,0:T(8,128)(2,1)}) custom-call(s32[1,4]{1,0:T(1,128)} %add_bitcast_fusion.me.refs_0_, f32[160,768]{1,0:T(8,128)} %get-tuple-element.221.grad_state, bf16[3,640,160]{2,1,0:T(8,128)(2,1)} %get-tuple-element.222.probs, ...), custom_call_target="tpu_custom_call" | custom-call | flops 3200000000 | bytes 1048576 | tf_op jit(solution)/shard_map/self_back_kernel/pallas_call | solution.py:805
  163.1 9.8 %cross_grad_kernel.1 = (bf16[2,4,48,1152]{3,2,1,0:T(8,128)(2,1)}, bf16[2,4,48,1152]{3,2,1,0:T(8,128)(2,1)}, bf16[2,4,48,768]{3,2,1,0:T(8,128)(2,1)}, bf16[2,4,48,768]{3,2,1,0:T(8,128)(2,1)}) custom-call(s32[1,4]{1,0:T(1,128)} %add_bitcast_fusion.me.refs_0_, bf16[160,3072]{1,0:T(8,128)(2,1)} %get-tuple-element.205.refs_0_.saved, ...), custom_call_target="tpu_custom_call" | custom-call | flops 4000000000 | bytes 1048576 | tf_op jit(solution)/shard_map/cross_grad_kernel/pallas_call | solution.py:805
  172.9 2.1 collective-permute-start.35
  175.0 4.3 %self_grad_kernel.1 = (bf16[2,4,48,768]{3,2,1,0:T(8,128)(2,1)}, bf16[2,4,48,768]{3,2,1,0:T(8,128)(2,1)}, bf16[2,4,48,512]{3,2,1,0:T(8,128)(2,1)}, bf16[2,4,48,512]{3,2,1,0:T(8,128)(2,1)}) custom-call(s32[1,4]{1,0:T(1,128)} %add_bitcast_fusion.me.refs_0_, bf16[160,3072]{1,0:T(8,128)(2,1)} %get-tuple-element.205.refs_0_.saved, bf16[160,3072]{1,0:T(8,128)(2,1)} %copy-done.21, ...), custom_call_target="tpu_custom_call" | custom-call | flops 1600000000 | bytes 1048576 | tf_op jit(solution)/shard_map/self_grad_kernel/pallas_call | solution.py:805
  182.0 1.7 collective-permute-done.29.out_core
  184.4 2.6 return_kernel.1
  187.0 20.8 %collective-permute-done.38.refs_7_ = bf16[2,4,48,512]{3,2,1,0:T(8,128)(2,1)S(1)} collective-permute-done((bf16[2,4,48,512]{3,2,1,0:T(8,128)(2,1)}, bf16[2,4,48,512]{3,2,1,0:T(8,128)(2,1)S(1)}, u32[]{:S(2)}, u32[]{:S(2)}) %collective-permute-start.38) | collective-permute-done | bytes 393248 | tf_op jit(solution)/shard_map/ppermute | solution.py:843
  209.2 2.7 add_kernel.2
  212.9 2.4 collective-permute-start.40
  216.3 2.9 %add_kernel.3.so_far = bf16[4,48,3200]{2,1,0:T(8,128)(2,1)} custom-call(bf16[2,4,48,1152]{3,2,1,0:T(8,128)(2,1)} %get-tuple-element.254.refs_0_, bf16[2,4,48,1152]{3,2,1,0:T(8,128)(2,1)} %copy-done.2, bf16[2,4,48,768]{3,2,1,0:T(8,128)(2,1)} %get-tuple-element.261.refs_2_, bf16[2,4,48,768]{3,2,1,0:T(8,128)(2,1)} %copy-done.4, ...), custom_call_target="tpu_custom_call" | custom-call | tf_op jit(solution)/shard_map/add_kernel/pallas_call | solution.py:831
  219.2 8.5 %collective-permute-done.42.refs_3_ = bf16[4,48,512]{2,1,0:T(8,128)(2,1)S(1)} collective-permute-done((bf16[4,48,512]{2,1,0:T(8,128)(2,1)}, bf16[4,48,512]{2,1,0:T(8,128)(2,1)S(1)}, u32[]{:S(2)}, u32[]{:S(2)}) %collective-permute-start.42) | collective-permute-done | bytes 196640 | tf_op jit(solution)/shard_map/ppermute | solution.py:843
  229.2 3.8 %last_add_kernel.1 = bf16[4,48,3200]{2,1,0:T(8,128)(2,1)} custom-call(bf16[4,48,3200]{2,1,0:T(8,128)(2,1)} %add_kernel.3.so_far, bf16[4,48,1152]{2,1,0:T(8,128)(2,1)} %copy-done.11, bf16[4,48,768]{2,1,0:T(8,128)(2,1)} %copy-done.12, bf16[4,48,768]{2,1,0:T(8,128)(2,1)} %copy-done.13, bf16[4,48,512]{2,1,0:T(8,128)(2,1)} %copy-done.14), custom_call_target="tpu_custom_call" | custom-call | flops 800000000 | bytes 1048576 | tf_op jit(solution)/shard_map/last_add_kernel/pallas_call | solution.py:805
  233.0 6.0 %all-to-all-start.4 = ((bf16[8,24,3200]{2,1,0:T(8,128)(2,1)}), bf16[8,24,3200]{2,1,0:T(8,128)(2,1)S(1)}, u32[]{:S(2)}, u32[]{:S(2)}) async-start(bf16[8,24,3200]{2,1,0:T(8,128)(2,1)} %bitcast.43), calls=%async_computation.4 | async-start | bytes 2457600 | tf_op jit(solution)/shard_map/all_to_all | solution.py:847
  239.1 2.9 %depth_sum_kernel.1 = (bf16[24,1536]{1,0:T(8,128)(2,1)}, bf16[24,1536]{1,0:T(8,128)(2,1)}, bf16[2,24,1536]{2,1,0:T(8,128)(2,1)}) custom-call(s32[1,4]{1,0:T(1,128)} %add_bitcast_fusion.me.refs_0_, bf16[8,96,1536]{2,1,0:T(8,128)(2,1)} %copy-done.5), custom_call_target="tpu_custom_call" | custom-call | flops 800000000 | bytes 1048576 | tf_op jit(solution)/shard_map/depth_sum_kernel/pallas_call | solution.py:805
  244.3 4.6 %collective-permute-done.46.chip = bf16[2,24,1536]{2,1,0:T(8,128)(2,1)S(1)} collective-permute-done((bf16[2,24,1536]{2,1,0:T(8,128)(2,1)}, bf16[2,24,1536]{2,1,0:T(8,128)(2,1)S(1)}, u32[]{:S(2)}, u32[]{:S(2)}) %collective-permute-start.46) | collective-permute-done | bytes 147488 | tf_op jit(solution)/shard_map/ppermute | solution.py:843
  248.9 4.8 %collective-permute-done.43.chip = bf16[2,40,1536]{2,1,0:T(8,128)(2,1)S(1)} collective-permute-done((bf16[2,40,1536]{2,1,0:T(8,128)(2,1)S(1)}, bf16[2,40,1536]{2,1,0:T(8,128)(2,1)S(1)}, u32[]{:S(2)}, u32[]{:S(2)}) %collective-permute-start.43) | collective-permute-done | bytes 245792 | tf_op jit(solution)/shard_map/ppermute | solution.py:843
  253.8 7.4 %image_grad_kernel.1 = bf16[1024,768]{1,0:T(8,128)(2,1)} custom-call(bf16[1024,768]{1,0:T(8,128)(2,1)} %get-tuple-element.237.refs_6_.kv_keep, bf16[1024,768]{1,0:T(8,128)(2,1)} %get-tuple-element.277.kv_send, s32[1,4]{1,0:T(1,128)} %add_bitcast_fusion.me.refs_0_, bf16[4,48,1664]{2,1,0:T(8,128)(2,1)} %bitcast.53, bf16[4,48,1664]{2,1,0:T(8,128)(2,1)} %copy-done.23, ...), custom_call_target="tpu_custom_call" | custom-call | flops 2800000000 | bytes 1048576 | tf_op jit(solution)/shard_map/image_grad_kernel/pallas_call | solution.py:805
  261.9 2.5 unpack_hidden_kernel.1
  265.0 2.0 collect_kernel.1
  267.0 2.5 all-to-all-done.4
  (187 shorter events, 33.2 us)
Async XLA Ops:
  2.5 23.7 %all-to-all-start = ((bf16[8,24,1536]{2,1,0:T(8,128)(2,1)}), bf16[8,24,1536]{2,1,0:T(8,128)(2,1)S(1)}, u32[]{:S(2)}, u32[]{:S(2)}) async-start(bf16[8,24,1536]{2,1,0:T(8,128)(2,1)} %bitcast.60), calls=%async_computation | async-start | bytes 1179648 | tf_op jit(solution)/shard_map/all_to_all | solution.py:847
  12.3 13.8 %collective-permute-start = (bf16[2,80,1536]{2,1,0:T(8,128)(2,1)}, bf16[2,80,1536]{2,1,0:T(8,128)(2,1)S(1)}, u32[]{:S(2)}, u32[]{:S(2)}) collective-permute-start(bf16[2,80,1536]{2,1,0:T(8,128)(2,1)} %get-tuple-element.154), channel_id=1, source_target_pairs={{0,2},{2,0},{1,3},{3,1},{4,6},{6,4},{5,7},{7,5},{8,10},{10,8},{9,1... | collective-permute-start | bytes 1474568 | tf_op jit(solution)/shard_map/ppermute | solution.py:843
  26.1 22.7 %collective-permute-start.5 = (bf16[768,1024]{1,0:T(8,128)(2,1)S(1)}, bf16[768,1024]{1,0:T(8,128)(2,1)}, u32[]{:S(2)}, u32[]{:S(2)}) collective-permute-start(bf16[768,1024]{1,0:T(8,128)(2,1)S(1)} %copy-done.7), channel_id=1, source_target_pairs={{0,1},{1,0},{2,3},{3,2},{4,5},{5,4},{6,7},{7,6},{8,9},{9,8},{10,11... | collective-permute-start | bytes 4718600 | tf_op jit(solution)/shard_map/ppermute | solution.py:843
  26.2 22.7 %all-to-all-start.1 = ((bf16[8,24,1664]{2,1,0:T(8,128)(2,1)}), bf16[8,24,1664]{2,1,0:T(8,128)(2,1)S(1)}, u32[]{:S(2)}, u32[]{:S(2)}) async-start(bf16[8,24,1664]{2,1,0:T(8,128)(2,1)} %bitcast.54), calls=%async_computation.1 | async-start | bytes 1277952 | tf_op jit(solution)/shard_map/all_to_all | solution.py:847
  31.1 3.7 %collective-permute-start.2 = (bf16[80,1536]{1,0:T(8,128)(2,1)S(1)}, bf16[80,1536]{1,0:T(8,128)(2,1)S(1)}, u32[]{:S(2)}, u32[]{:S(2)}) collective-permute-start(bf16[80,1536]{1,0:T(8,128)(2,1)S(1)} %slice_bitcast_fusion), channel_id=1, source_target_pairs={{0,1},{1,0},{2,3},{3,2},{4,5},{5,4},{6,7},{7,6},{8,9},{9,8},{10,11... | collective-permute-start | bytes 737288 | tf_op jit(solution)/shard_map/ppermute | solution.py:843
  31.7 8.4 %collective-permute-start.6 = (bf16[4,48,1536]{2,1,0:T(8,128)(2,1)S(1)}, bf16[4,48,1536]{2,1,0:T(8,128)(2,1)S(1)}, u32[]{:S(2)}, u32[]{:S(2)}) collective-permute-start(bf16[4,48,1536]{2,1,0:T(8,128)(2,1)S(1)} %bitcast.55), channel_id=1, source_target_pairs={{0,1},{1,0},{2,3},{3,2},{4,5},{5,4},{6,7},{7,6},{8,9},{9,8},{10,11... | collective-permute-start | bytes 1769480 | tf_op jit(solution)/shard_map/ppermute | solution.py:843
  31.7 15.7 %collective-permute-start.4 = (bf16[4,48,1536]{2,1,0:T(8,128)(2,1)S(1)}, bf16[4,48,1536]{2,1,0:T(8,128)(2,1)S(1)}, u32[]{:S(2)}, u32[]{:S(2)}) collective-permute-start(bf16[4,48,1536]{2,1,0:T(8,128)(2,1)S(1)} %bitcast.56), channel_id=1, source_target_pairs={{0,2},{2,0},{1,3},{3,1},{4,6},{6,4},{5,7},{7,5},{8,10},{10,8},{9,1... | collective-permute-start | bytes 1769480 | tf_op jit(solution)/shard_map/ppermute | solution.py:843
  33.3 15.5 %collective-permute-start.3 = (bf16[4,48,1536]{2,1,0:T(8,128)(2,1)S(1)}, bf16[4,48,1536]{2,1,0:T(8,128)(2,1)}, u32[]{:S(2)}, u32[]{:S(2)}) collective-permute-start(bf16[4,48,1536]{2,1,0:T(8,128)(2,1)S(1)} %bitcast.57), channel_id=1, source_target_pairs={{0,4},{4,0},{1,5},{5,1},{2,6},{6,2},{3,7},{7,3},{8,12},{12,8},{9,1... | collective-permute-start | bytes 1769480 | tf_op jit(solution)/shard_map/ppermute | solution.py:843
  48.9 8.0 %collective-permute-start.11 = (bf16[4,48,1664]{2,1,0:T(8,128)(2,1)S(1)}, bf16[4,48,1664]{2,1,0:T(8,128)(2,1)S(1)}, u32[]{:S(2)}, u32[]{:S(2)}) collective-permute-start(bf16[4,48,1664]{2,1,0:T(8,128)(2,1)S(1)} %bitcast.48), channel_id=1, source_target_pairs={{0,1},{1,0},{2,3},{3,2},{4,5},{5,4},{6,7},{7,6},{8,9},{9,8},{10,11... | collective-permute-start | bytes 1916936 | tf_op jit(solution)/shard_map/ppermute | solution.py:843
  48.9 16.8 %collective-permute-start.8 = (bf16[4,48,1664]{2,1,0:T(8,128)(2,1)S(1)}, bf16[4,48,1664]{2,1,0:T(8,128)(2,1)S(1)}, u32[]{:S(2)}, u32[]{:S(2)}) collective-permute-start(bf16[4,48,1664]{2,1,0:T(8,128)(2,1)S(1)} %bitcast.49), channel_id=1, source_target_pairs={{0,2},{2,0},{1,3},{3,1},{4,6},{6,4},{5,7},{7,5},{8,10},{10,8},{9,1... | collective-permute-start | bytes 1916936 | tf_op jit(solution)/shard_map/ppermute | solution.py:843
  50.5 16.6 %collective-permute-start.7 = (bf16[4,48,1664]{2,1,0:T(8,128)(2,1)S(1)}, bf16[4,48,1664]{2,1,0:T(8,128)(2,1)}, u32[]{:S(2)}, u32[]{:S(2)}) collective-permute-start(bf16[4,48,1664]{2,1,0:T(8,128)(2,1)S(1)} %bitcast.50), channel_id=1, source_target_pairs={{0,4},{4,0},{1,5},{5,1},{2,6},{6,2},{3,7},{7,3},{8,12},{12,8},{9,1... | collective-permute-start | bytes 1916936 | tf_op jit(solution)/shard_map/ppermute | solution.py:843
  52.0 4.8 %collective-permute-start.10 = (bf16[4,48,1536]{2,1,0:T(8,128)(2,1)}, bf16[4,48,1536]{2,1,0:T(8,128)(2,1)}, u32[]{:S(2)}, u32[]{:S(2)}) collective-permute-start(bf16[4,48,1536]{2,1,0:T(8,128)(2,1)} %copy-done.27), channel_id=1, source_target_pairs={{0,1},{1,0},{2,3},{3,2},{4,5},{5,4},{6,7},{7,6},{8,9},{9,8},{10,11... | collective-permute-start | bytes 1769480 | tf_op jit(solution)/shard_map/ppermute | solution.py:843
  52.0 4.9 %collective-permute-start.9 = (bf16[4,48,1536]{2,1,0:T(8,128)(2,1)}, bf16[4,48,1536]{2,1,0:T(8,128)(2,1)}, u32[]{:S(2)}, u32[]{:S(2)}) collective-permute-start(bf16[4,48,1536]{2,1,0:T(8,128)(2,1)} %collective-permute-done.3.refs_2_), channel_id=1, source_target_pairs={{0,1},{1,0},{2,3},{3,2},{4,5},{5,4},{6,7},{7,6},{8,9},{9,8},{10,11... | collective-permute-start | bytes 1769480 | tf_op jit(solution)/shard_map/ppermute | solution.py:843
  52.5 33.4 %all-to-all-start.2 = ((bf16[4,96,1536]{2,1,0:T(8,128)(2,1)}), bf16[4,96,1536]{2,1,0:T(8,128)(2,1)S(1)}, u32[]{:S(2)}, u32[]{:S(2)}) async-start(bf16[4,96,1536]{2,1,0:T(8,128)(2,1)} %bitcast.47), calls=%async_computation.2 | async-start | bytes 2359296 | tf_op jit(solution)/shard_map/all_to_all | solution.py:847
  67.0 17.3 %collective-permute-start.15 = (bf16[4,48,1664]{2,1,0:T(8,128)(2,1)}, bf16[4,48,1664]{2,1,0:T(8,128)(2,1)S(1)}, u32[]{:S(2)}, u32[]{:S(2)}) collective-permute-start(bf16[4,48,1664]{2,1,0:T(8,128)(2,1)} %collective-permute-done.7.refs_10_.refs_2_.refs_3_), channel_id=1, source_target_pairs={{0,1},{1,0},{2,3},{3,2},{4,5},{5,4},{6,7},{7,6},{8,9},{9,8},{10,11... | collective-permute-start | bytes 1916936 | tf_op jit(solution)/shard_map/ppermute | solution.py:843
  67.0 17.3 %collective-permute-start.14 = (bf16[4,48,1664]{2,1,0:T(8,128)(2,1)S(1)}, bf16[4,48,1664]{2,1,0:T(8,128)(2,1)S(1)}, u32[]{:S(2)}, u32[]{:S(2)}) collective-permute-start(bf16[4,48,1664]{2,1,0:T(8,128)(2,1)S(1)} %collective-permute-done.8.refs_9_.refs_1_.refs_2_), channel_id=1, source_target_pairs={{0,1},{1,0},{2,3},{3,2},{4,5},{5,4},{6,7},{7,6},{8,9},{9,8},{10,11... | collective-permute-start | bytes 1916936 | tf_op jit(solution)/shard_map/ppermute | solution.py:843
  67.5 16.8 %collective-permute-start.13 = (bf16[4,48,1664]{2,1,0:T(8,128)(2,1)S(1)}, bf16[4,48,1664]{2,1,0:T(8,128)(2,1)}, u32[]{:S(2)}, u32[]{:S(2)}) collective-permute-start(bf16[4,48,1664]{2,1,0:T(8,128)(2,1)S(1)} %collective-permute-done.8.refs_9_.refs_1_.refs_2_), channel_id=1, source_target_pairs={{0,4},{4,0},{1,5},{5,1},{2,6},{6,2},{3,7},{7,3},{8,12},{12,8},{9,1... | collective-permute-start | bytes 1916936 | tf_op jit(solution)/shard_map/ppermute | solution.py:843
  69.0 15.3 %collective-permute-start.12 = (bf16[4,48,1536]{2,1,0:T(8,128)(2,1)}, bf16[4,48,1536]{2,1,0:T(8,128)(2,1)}, u32[]{:S(2)}, u32[]{:S(2)}) collective-permute-start(bf16[4,48,1536]{2,1,0:T(8,128)(2,1)} %collective-permute-done.3.refs_2_), channel_id=1, source_target_pairs={{0,2},{2,0},{1,3},{3,1},{4,6},{6,4},{5,7},{7,5},{8,10},{10,8},{9,1... | collective-permute-start | bytes 1769480 | tf_op jit(solution)/shard_map/ppermute | solution.py:843
  85.4 17.5 %collective-permute-start.22 = (bf16[160,768]{1,0:T(8,128)(2,1)S(1)}, bf16[160,768]{1,0:T(8,128)(2,1)}, u32[]{:S(2)}, u32[]{:S(2)}) collective-permute-start(bf16[160,768]{1,0:T(8,128)(2,1)S(1)} %copy-done.31), channel_id=1, source_target_pairs={{0,2},{2,0},{1,3},{3,1},{4,6},{6,4},{5,7},{7,5},{8,10},{10,8},{9,1... | collective-permute-start | bytes 737288 | tf_op jit(solution)/shard_map/ppermute | solution.py:843
  85.9 27.3 %collective-permute-start.24 = (bf16[4,96,1536]{2,1,0:T(8,128)(2,1)S(1)}, bf16[4,96,1536]{2,1,0:T(8,128)(2,1)S(1)}, u32[]{:S(2)}, u32[]{:S(2)}) collective-permute-start(bf16[4,96,1536]{2,1,0:T(8,128)(2,1)S(1)} %all-to-all-done.2.refs_8_), channel_id=1, source_target_pairs={{0,4},{4,0},{1,5},{5,1},{2,6},{6,2},{3,7},{7,3},{8,12},{12,8},{9,1... | collective-permute-start | bytes 3538952 | tf_op jit(solution)/shard_map/ppermute | solution.py:843
  102.4 8.2 %collective-permute-start.19 = (bf16[160,768]{1,0:T(8,128)(2,1)}, bf16[160,768]{1,0:T(8,128)(2,1)S(1)}, u32[]{:S(2)}, u32[]{:S(2)}) collective-permute-start(bf16[160,768]{1,0:T(8,128)(2,1)} %get-tuple-element.196.refs_0_), channel_id=1, source_target_pairs={{0,2},{2,0},{1,3},{3,1},{4,6},{6,4},{5,7},{7,5},{8,10},{10,8},{9,1... | collective-permute-start | bytes 737288 | tf_op jit(solution)/shard_map/ppermute | solution.py:843
  102.9 7.7 %collective-permute-start.21 = (bf16[160,768]{1,0:T(8,128)(2,1)S(1)}, bf16[160,768]{1,0:T(8,128)(2,1)S(1)}, u32[]{:S(2)}, u32[]{:S(2)}) collective-permute-start(bf16[160,768]{1,0:T(8,128)(2,1)S(1)} %copy-done.31), channel_id=1, source_target_pairs={{0,1},{1,0},{2,3},{3,2},{4,5},{5,4},{6,7},{7,6},{8,9},{9,8},{10,11... | collective-permute-start | bytes 737288 | tf_op jit(solution)/shard_map/ppermute | solution.py:843
  102.9 8.2 %collective-permute-start.23 = (bf16[160,768]{1,0:T(8,128)(2,1)}, bf16[160,768]{1,0:T(8,128)(2,1)S(1)}, u32[]{:S(2)}, u32[]{:S(2)}) collective-permute-start(bf16[160,768]{1,0:T(8,128)(2,1)} %collective-permute-done.22.refs_6_), channel_id=1, source_target_pairs={{0,1},{1,0},{2,3},{3,2},{4,5},{5,4},{6,7},{7,6},{8,9},{9,8},{10,11... | collective-permute-start | bytes 737288 | tf_op jit(solution)/shard_map/ppermute | solution.py:843
  103.4 7.7 %collective-permute-start.18 = (bf16[160,768]{1,0:T(8,128)(2,1)}, bf16[160,768]{1,0:T(8,128)(2,1)S(1)}, u32[]{:S(2)}, u32[]{:S(2)}) collective-permute-start(bf16[160,768]{1,0:T(8,128)(2,1)} %get-tuple-element.196.refs_0_), channel_id=1, source_target_pairs={{0,1},{1,0},{2,3},{3,2},{4,5},{5,4},{6,7},{7,6},{8,9},{9,8},{10,11... | collective-permute-start | bytes 737288 | tf_op jit(solution)/shard_map/ppermute | solution.py:843
  110.6 22.4 %collective-permute-start.28 = (bf16[160,3072]{1,0:T(8,128)(2,1)}, bf16[160,3072]{1,0:T(8,128)(2,1)S(1)}, u32[]{:S(2)}, u32[]{:S(2)}) collective-permute-start(bf16[160,3072]{1,0:T(8,128)(2,1)} %get-tuple-element.205.refs_0_.saved), channel_id=1, source_target_pairs={{0,1},{1,0},{2,3},{3,2},{4,5},{5,4},{6,7},{7,6},{8,9},{9,8},{10,11... | collective-permute-start | bytes 2949128 | tf_op jit(solution)/shard_map/ppermute | solution.py:843
  123.1 10.0 %collective-permute-start.27 = (bf16[160,768]{1,0:T(8,128)(2,1)}, bf16[160,768]{1,0:T(8,128)(2,1)S(1)}, u32[]{:S(2)}, u32[]{:S(2)}) collective-permute-start(bf16[160,768]{1,0:T(8,128)(2,1)} %get-tuple-element.202), channel_id=1, source_target_pairs={{0,1},{1,0},{2,3},{3,2},{4,5},{5,4},{6,7},{7,6},{8,9},{9,8},{10,11... | collective-permute-start | bytes 737288 | tf_op jit(solution)/shard_map/ppermute | solution.py:843
  125.8 8.1 %collective-permute-start.26 = (bf16[160,768]{1,0:T(8,128)(2,1)S(1)}, bf16[160,768]{1,0:T(8,128)(2,1)S(1)}, u32[]{:S(2)}, u32[]{:S(2)}) collective-permute-start(bf16[160,768]{1,0:T(8,128)(2,1)S(1)} %combine_kernel.2), channel_id=1, source_target_pairs={{0,2},{2,0},{1,3},{3,1},{4,6},{6,4},{5,7},{7,5},{8,10},{10,8},{9,1... | collective-permute-start | bytes 737288 | tf_op jit(solution)/shard_map/ppermute | solution.py:843
  134.6 93.8 %all-to-all-start.3 = ((bf16[8,96,1536]{2,1,0:T(8,128)(2,1)}), bf16[8,96,1536]{2,1,0:T(8,128)(2,1)S(1)}, u32[]{:S(2)}, u32[]{:S(2)}) async-start(bf16[8,96,1536]{2,1,0:T(8,128)(2,1)} %bitcast.44), calls=%async_computation.3 | async-start | bytes 4718592 | tf_op jit(solution)/shard_map/all_to_all | solution.py:847
  139.8 12.0 %collective-permute-start.30 = (bf16[160,768]{1,0:T(8,128)(2,1)}, bf16[160,768]{1,0:T(8,128)(2,1)S(1)}, u32[]{:S(2)}, u32[]{:S(2)}) collective-permute-start(bf16[160,768]{1,0:T(8,128)(2,1)} %get-tuple-element.220), channel_id=1, source_target_pairs={{0,1},{1,0},{2,3},{3,2},{4,5},{5,4},{6,7},{7,6},{8,9},{9,8},{10,11... | collective-permute-start | bytes 737288 | tf_op jit(solution)/shard_map/ppermute | solution.py:843
  151.8 10.0 %collective-permute-start.32 = (bf16[1024,768]{1,0:T(8,128)(2,1)}, bf16[1024,768]{1,0:T(8,128)(2,1)S(1)}, u32[]{:S(2)}, u32[]{:S(2)}) collective-permute-start(bf16[1024,768]{1,0:T(8,128)(2,1)} %get-tuple-element.277.kv_send), channel_id=1, source_target_pairs={{0,1},{1,0},{2,3},{3,2},{4,5},{5,4},{6,7},{7,6},{8,9},{9,8},{10,11... | collective-permute-start | bytes 4718600 | tf_op jit(solution)/shard_map/ppermute | solution.py:843
  152.4 9.4 %collective-permute-start.31 = (bf16[160,1152]{1,0:T(8,128)(2,1)}, bf16[160,1152]{1,0:T(8,128)(2,1)S(1)}, u32[]{:S(2)}, u32[]{:S(2)}) collective-permute-start(bf16[160,1152]{1,0:T(8,128)(2,1)} %get-tuple-element.227), channel_id=1, source_target_pairs={{0,1},{1,0},{2,3},{3,2},{4,5},{5,4},{6,7},{7,6},{8,9},{9,8},{10,11... | collective-permute-start | bytes 1105928 | tf_op jit(solution)/shard_map/ppermute | solution.py:843
  152.5 9.3 %collective-permute-start.33 = (bf16[160,768]{1,0:T(8,128)(2,1)S(1)}, bf16[160,768]{1,0:T(8,128)(2,1)S(1)}, u32[]{:S(2)}, u32[]{:S(2)}) collective-permute-start(bf16[160,768]{1,0:T(8,128)(2,1)S(1)} %combine_kernel.3), channel_id=1, source_target_pairs={{0,2},{2,0},{1,3},{3,1},{4,6},{6,4},{5,7},{7,5},{8,10},{10,8},{9,1... | collective-permute-start | bytes 737288 | tf_op jit(solution)/shard_map/ppermute | solution.py:843
  161.8 11.0 %collective-permute-start.34 = (bf16[160,1152]{1,0:T(8,128)(2,1)}, bf16[160,1152]{1,0:T(8,128)(2,1)S(1)}, u32[]{:S(2)}, u32[]{:S(2)}) collective-permute-start(bf16[160,1152]{1,0:T(8,128)(2,1)} %get-tuple-element.243), channel_id=1, source_target_pairs={{0,1},{1,0},{2,3},{3,2},{4,5},{5,4},{6,7},{7,6},{8,9},{9,8},{10,11... | collective-permute-start | bytes 1105928 | tf_op jit(solution)/shard_map/ppermute | solution.py:843
  172.9 34.9 %collective-permute-start.35 = (bf16[2,4,48,1152]{3,2,1,0:T(8,128)(2,1)}, bf16[2,4,48,1152]{3,2,1,0:T(8,128)(2,1)S(1)}, u32[]{:S(2)}, u32[]{:S(2)}) collective-permute-start(bf16[2,4,48,1152]{3,2,1,0:T(8,128)(2,1)} %get-tuple-element.255), channel_id=1, source_target_pairs={{0,4},{4,0},{1,5},{5,1},{2,6},{6,2},{3,7},{7,3},{8,12},{12,8},{9,1... | collective-permute-start | bytes 2654216 | tf_op jit(solution)/shard_map/ppermute | solution.py:843
  179.3 28.5 %collective-permute-start.37 = (bf16[2,4,48,768]{3,2,1,0:T(8,128)(2,1)}, bf16[2,4,48,768]{3,2,1,0:T(8,128)(2,1)S(1)}, u32[]{:S(2)}, u32[]{:S(2)}) collective-permute-start(bf16[2,4,48,768]{3,2,1,0:T(8,128)(2,1)} %get-tuple-element.257), channel_id=1, source_target_pairs={{0,2},{2,0},{1,3},{3,1},{4,6},{6,4},{5,7},{7,5},{8,10},{10,8},{9,1... | collective-permute-start | bytes 1769480 | tf_op jit(solution)/shard_map/ppermute | solution.py:843
  180.3 27.5 %collective-permute-start.36 = (bf16[2,4,48,768]{3,2,1,0:T(8,128)(2,1)S(1)}, bf16[2,4,48,768]{3,2,1,0:T(8,128)(2,1)S(1)}, u32[]{:S(2)}, u32[]{:S(2)}) collective-permute-start(bf16[2,4,48,768]{3,2,1,0:T(8,128)(2,1)S(1)} %copy-done.28), channel_id=1, source_target_pairs={{0,2},{2,0},{1,3},{3,1},{4,6},{6,4},{5,7},{7,5},{8,10},{10,8},{9,1... | collective-permute-start | bytes 1769480 | tf_op jit(solution)/shard_map/ppermute | solution.py:843
  181.3 26.4 %collective-permute-start.38 = (bf16[2,4,48,512]{3,2,1,0:T(8,128)(2,1)}, bf16[2,4,48,512]{3,2,1,0:T(8,128)(2,1)S(1)}, u32[]{:S(2)}, u32[]{:S(2)}) collective-permute-start(bf16[2,4,48,512]{3,2,1,0:T(8,128)(2,1)} %get-tuple-element.258), channel_id=1, source_target_pairs={{0,4},{4,0},{1,5},{5,1},{2,6},{6,2},{3,7},{7,3},{8,12},{12,8},{9,1... | collective-permute-start | bytes 1179656 | tf_op jit(solution)/shard_map/ppermute | solution.py:843
  211.9 16.5 %collective-permute-start.39 = (bf16[4,48,1152]{2,1,0:T(8,128)(2,1)}, bf16[4,48,1152]{2,1,0:T(8,128)(2,1)S(1)}, u32[]{:S(2)}, u32[]{:S(2)}) collective-permute-start(bf16[4,48,1152]{2,1,0:T(8,128)(2,1)} %get-tuple-element.267), channel_id=1, source_target_pairs={{0,2},{2,0},{1,3},{3,1},{4,6},{6,4},{5,7},{7,5},{8,10},{10,8},{9,1... | collective-permute-start | bytes 1327112 | tf_op jit(solution)/shard_map/ppermute | solution.py:843
  212.9 14.8 %collective-permute-start.40 = (bf16[4,48,768]{2,1,0:T(8,128)(2,1)}, bf16[4,48,768]{2,1,0:T(8,128)(2,1)S(1)}, u32[]{:S(2)}, u32[]{:S(2)}) collective-permute-start(bf16[4,48,768]{2,1,0:T(8,128)(2,1)} %get-tuple-element.268), channel_id=1, source_target_pairs={{0,4},{4,0},{1,5},{5,1},{2,6},{6,2},{3,7},{7,3},{8,12},{12,8},{9,1... | collective-permute-start | bytes 884744 | tf_op jit(solution)/shard_map/ppermute | solution.py:843
  215.3 12.8 %collective-permute-start.41 = (bf16[4,48,768]{2,1,0:T(8,128)(2,1)}, bf16[4,48,768]{2,1,0:T(8,128)(2,1)S(1)}, u32[]{:S(2)}, u32[]{:S(2)}) collective-permute-start(bf16[4,48,768]{2,1,0:T(8,128)(2,1)} %get-tuple-element.269), channel_id=1, source_target_pairs={{0,4},{4,0},{1,5},{5,1},{2,6},{6,2},{3,7},{7,3},{8,12},{12,8},{9,1... | collective-permute-start | bytes 884744 | tf_op jit(solution)/shard_map/ppermute | solution.py:843
  215.3 12.4 %collective-permute-start.42 = (bf16[4,48,512]{2,1,0:T(8,128)(2,1)}, bf16[4,48,512]{2,1,0:T(8,128)(2,1)S(1)}, u32[]{:S(2)}, u32[]{:S(2)}) collective-permute-start(bf16[4,48,512]{2,1,0:T(8,128)(2,1)} %get-tuple-element.270), channel_id=1, source_target_pairs={{0,2},{2,0},{1,3},{3,1},{4,6},{6,4},{5,7},{7,5},{8,10},{10,8},{9,1... | collective-permute-start | bytes 589832 | tf_op jit(solution)/shard_map/ppermute | solution.py:843
  233.0 36.5 %all-to-all-start.4 = ((bf16[8,24,3200]{2,1,0:T(8,128)(2,1)}), bf16[8,24,3200]{2,1,0:T(8,128)(2,1)S(1)}, u32[]{:S(2)}, u32[]{:S(2)}) async-start(bf16[8,24,3200]{2,1,0:T(8,128)(2,1)} %bitcast.43), calls=%async_computation.4 | async-start | bytes 2457600 | tf_op jit(solution)/shard_map/all_to_all | solution.py:847
  242.0 6.9 %collective-permute-start.46 = (bf16[2,24,1536]{2,1,0:T(8,128)(2,1)}, bf16[2,24,1536]{2,1,0:T(8,128)(2,1)S(1)}, u32[]{:S(2)}, u32[]{:S(2)}) collective-permute-start(bf16[2,24,1536]{2,1,0:T(8,128)(2,1)} %get-tuple-element.290), channel_id=1, source_target_pairs={{0,2},{2,0},{1,3},{3,1},{4,6},{6,4},{5,7},{7,5},{8,10},{10,8},{9,1... | collective-permute-start | bytes 442376 | tf_op jit(solution)/shard_map/ppermute | solution.py:843
  243.0 21.3 %collective-permute-start.44 = (bf16[40,1536]{1,0:T(8,128)(2,1)S(1)}, bf16[40,1536]{1,0:T(8,128)(2,1)S(1)}, u32[]{:S(2)}, u32[]{:S(2)}) collective-permute-start(bf16[40,1536]{1,0:T(8,128)(2,1)S(1)} %copy-done.44), channel_id=1, source_target_pairs={{0,1},{1,0},{2,3},{3,2},{4,5},{5,4},{6,7},{7,6},{8,9},{9,8},{10,11... | collective-permute-start | bytes 368648 | tf_op jit(solution)/shard_map/ppermute | solution.py:843
  243.2 10.5 %collective-permute-start.43 = (bf16[2,40,1536]{2,1,0:T(8,128)(2,1)S(1)}, bf16[2,40,1536]{2,1,0:T(8,128)(2,1)S(1)}, u32[]{:S(2)}, u32[]{:S(2)}) collective-permute-start(bf16[2,40,1536]{2,1,0:T(8,128)(2,1)S(1)} %copy-done.32), channel_id=1, source_target_pairs={{0,2},{2,0},{1,3},{3,1},{4,6},{6,4},{5,7},{7,5},{8,10},{10,8},{9,1... | collective-permute-start | bytes 737288 | tf_op jit(solution)/shard_map/ppermute | solution.py:843
  244.2 17.0 %collective-permute-start.47 = (bf16[24,1536]{1,0:T(8,128)(2,1)}, bf16[24,1536]{1,0:T(8,128)(2,1)S(1)}, u32[]{:S(2)}, u32[]{:S(2)}) collective-permute-start(bf16[24,1536]{1,0:T(8,128)(2,1)} %get-tuple-element.291), channel_id=1, source_target_pairs={{0,1},{1,0},{2,3},{3,2},{4,5},{5,4},{6,7},{7,6},{8,9},{9,8},{10,11... | collective-permute-start | bytes 221192 | tf_op jit(solution)/shard_map/ppermute | solution.py:843
  248.9 12.4 %collective-permute-start.48 = (bf16[24,1536]{1,0:T(8,128)(2,1)S(1)}, bf16[24,1536]{1,0:T(8,128)(2,1)S(1)}, u32[]{:S(2)}, u32[]{:S(2)}) collective-permute-start(bf16[24,1536]{1,0:T(8,128)(2,1)S(1)} %slice_bitcast_fusion.2), channel_id=1, source_target_pairs={{0,1},{1,0},{2,3},{3,2},{4,5},{5,4},{6,7},{7,6},{8,9},{9,8},{10,11... | collective-permute-start | bytes 221192 | tf_op jit(solution)/shard_map/ppermute | solution.py:843
  253.7 10.6 %collective-permute-start.45 = (bf16[40,1536]{1,0:T(8,128)(2,1)S(1)}, bf16[40,1536]{1,0:T(8,128)(2,1)S(1)}, u32[]{:S(2)}, u32[]{:S(2)}) collective-permute-start(bf16[40,1536]{1,0:T(8,128)(2,1)S(1)} %slice_bitcast_fusion.1), channel_id=1, source_target_pairs={{0,1},{1,0},{2,3},{3,2},{4,5},{5,4},{6,7},{7,6},{8,9},{9,8},{10,11... | collective-permute-start | bytes 368648 | tf_op jit(solution)/shard_map/ppermute | solution.py:843
  (55 other events, 307.7 us)
